TPU v7x, 128 devices: a whole 4x4x4 slice. The times are simulated.
128 devices in a mesh: dp: 16 (over z_hi, x, core), vocab: 8 (over z_lo, y).
Axes of the slice: x: 4, y: 4, z: 4 (z_hi: 2, z_lo: 2; z = z_hi * 2 + z_lo), core: 2. Of those that a mesh axis runs over, the one named last changes fastest.
Arguments:
- hidden: bfloat16 [512, 4608], P('dp'), may hold values from -6 to 6
- head: bfloat16 [4608, 131072], P(None, ('dp', 'vocab')), may hold values from -0.1875 to 0.1875
- verdict_ids: int32 [512], replicated, may hold values from 0 to 131071
- row_weight: float32 [512], replicated, may hold values from 0.5 to 2
Outputs:
- logprob: float32 [512], P('dp')
- head_grad: bfloat16 [4608, 131072], P(None, ('dp', 'vocab'))
- hidden_grad: bfloat16 [512, 4608], P('dp', 'vocab')
Inputs may be any that keep to these rules, and one draw needn't show every extreme that they name: `verdict_ids`: each row's verdict token is a column of the whole vocabulary of 131072.
All inputs are finite; a program needn't handle non-finite values.
Results may differ from a plain program's by a relative error of at most 0.02.
Values may be sent and summed in bfloat16 or wider, within the bound.
No kernel may reach another device: no remote copies, remote signals or barrier semaphores. Data moves between devices by JAX's collectives and lax.ppermute only.
A program may use at most 128 MiB of HBM per device.

v0:
```python
import jax
import jax.numpy as jnp
from jax import lax
from jax.experimental import pallas as pl
from jax.experimental.pallas import tpu as pltpu
from jax.sharding import PartitionSpec as P

softcap = 30.0
AXES = ("dp", "vocab")
bf16 = jnp.bfloat16
f32 = jnp.float32
D = 4608
WIDTH = 1024
FEATURES = 576
COLUMN = (512, 128)


def flips(core0, core1):
    return [(i, i ^ (core1 if i & 8 else core0)) for i in range(128)]


CORE = flips(8, 8)
X1, X2 = flips(16, 48), flips(48, 16)
Y1, Y2 = flips(1, 3), flips(3, 1)
ZL, ZH = flips(4, 4), flips(68, 68)


def send(array, partner):
    return lax.ppermute(array, AXES, partner)


def slot_flip(slot, core):
    return (0, 1 + 2 * core, 3 - 2 * core, 2)[slot]


def whole_block(me, i):
    core = ((me >> 3) & 1) ^ ((i >> 2) & 1)
    x = ((me >> 4) & 3) ^ slot_flip(i & 3, core)
    return ((me >> 6) ^ (i >> 3)) * 8 + x * 2 + core


def feature_slot(me, i, other):
    core = ((me >> 3) & 1) ^ other
    apart = (me & 3) ^ (i & 3)
    slot = jnp.where(apart == 1 + 2 * core, 1, jnp.where(apart == 3 - 2 * core, 2, jnp.where(apart == 2, 3, 0)))
    return (((me >> 2) & 1) ^ (i >> 2)) * 4 + slot


def call(kernel, ins, outs, scratch=(), flops=0, moved=0, mib=16):
    places = {"v": pltpu.VMEM, "s": pltpu.SMEM, "h": pl.ANY}
    return pl.pallas_call(
        kernel,
        in_specs=[pl.BlockSpec(memory_space=places[i]) for i in ins],
        out_specs=[pl.BlockSpec(memory_space=places[o[0]]) for o in outs],
        out_shape=[jax.ShapeDtypeStruct(o[1], o[2]) for o in outs],
        scratch_shapes=list(scratch),
        compiler_params=pltpu.CompilerParams(vmem_limit_bytes=mib << 20),
        cost_estimate=pl.CostEstimate(flops=flops, bytes_accessed=moved, transcendentals=0),
        name=kernel.__name__,
    )


def rows_of(i):
    return slice(32 * i, 32 * i + 32)


def from_lanes(row):
    return jnp.broadcast_to(row, (128, 128)).T


def local_block(me, i, whole):
    return whole[pl.ds(pl.multiple_of(whole_block(me, i) * 32, 32), 32), :]


def spread(me_ref, ids_ref, weight_ref, ids_out, weight_out, ids_whole, weight_whole):
    me = me_ref[0]
    for j in range(4):
        ids_whole[128 * j : 128 * j + 128, :] = from_lanes(ids_ref[j : j + 1, :])
        weight_whole[128 * j : 128 * j + 128, :] = from_lanes(weight_ref[j : j + 1, :])
    for i in range(16):
        ids_out[rows_of(i), :] = local_block(me, i, ids_whole)
        weight_out[rows_of(i), :] = local_block(me, i, weight_whole)


def run_spread(me, ids, weight):
    column = ("v", COLUMN, f32)
    return call(spread, "svv", [column, column], scratch=[pltpu.VMEM(COLUMN, f32)] * 2, moved=1 << 20)(me, ids, weight)


def hits_of(me, ids, j):
    lane = lax.broadcasted_iota(jnp.int32, (ids.shape[0], 128), 1)
    return ids == (lane + (me * WIDTH + 128 * j)).astype(f32)


def forward(half, me_ref, *refs):
    pieces, (ids_ref, head_ref, rows, capped_ref, term_ref, total_ref, target_ref) = refs[:8], refs[8:]
    me = me_ref[0]
    for i in range(8):
        rows[rows_of(i), :] = pieces[i][...]
    ids = ids_ref[256 * half : 256 * half + 256, :]
    total = jnp.zeros((256, 128), f32)
    target = jnp.zeros((256, 128), f32)
    for n in range(4):
        raw = jnp.dot(rows[...], head_ref[:, 256 * n : 256 * n + 256], preferred_element_type=f32)
        ratio = jnp.tanh(raw / softcap)
        for j in range(2):
            start = 256 * n + 128 * j
            part = ratio[:, 128 * j : 128 * j + 128]
            capped = softcap * part
            expo = jnp.exp(capped)
            hit = hits_of(me, ids, 2 * n + j)
            capped_ref[:, start : start + 128] = capped
            term_ref[:, start : start + 128] = jnp.where(hit, 0.0, expo * (1.0 - part * part)).astype(bf16)
            total = total + expo
            target = target + jnp.where(hit, capped, 0.0)
    total_ref[...] = total
    target_ref[...] = target


def forward_low(*refs):
    forward(0, *refs)


def forward_high(*refs):
    forward(1, *refs)


def run_forward(kernel, me, pieces, ids, head):
    return call(
        kernel,
        "s" + "v" * 10,
        [
            ("v", (256, D), bf16),
            ("v", (256, WIDTH), f32),
            ("v", (256, WIDTH), bf16),
            ("v", (256, 128), f32),
            ("v", (256, 128), f32),
        ],
        flops=2 * 256 * D * WIDTH,
        moved=2 * D * WIDTH,
    )(me, *pieces, ids, head)


def pack(me_ref, total0, total1, target0, target1, out_ref, whole):
    me = me_ref[0]
    sums = []
    for halves in ((total0, total1), (target0, target1)):
        for i in range(16):
            spot = pl.ds(pl.multiple_of(whole_block(me, i) * 32, 32), 32)
            whole[spot, :] = halves[i // 8][rows_of(i % 8), :]
        for j in range(4):
            sums.append(jnp.sum(whole[128 * j : 128 * j + 128, :].T, axis=0, keepdims=True))
    out_ref[...] = jnp.broadcast_to(jnp.concatenate(sums, axis=0)[None], (128, 8, 128))


def run_pack(me, *columns):
    return call(pack, "svvvv", [("v", (128, 8, 128), f32)], scratch=[pltpu.VMEM(COLUMN, f32)], moved=1 << 20)(
        me, *columns
    )[0]


def unpack(me_ref, arrived_ref, weight_ref, log_ref, own_ref, rest_ref, pick_ref, logs, targets):
    me = me_ref[0]
    sums = jnp.sum(arrived_ref[...], axis=0)
    for j in range(4):
        logs[128 * j : 128 * j + 128, :] = from_lanes(jnp.log(sums[j : j + 1, :]))
        targets[128 * j : 128 * j + 128, :] = from_lanes(sums[4 + j : 5 + j, :])
    for i in range(16):
        log_ref[rows_of(i), :] = local_block(me, i, logs)
    log_total = local_block(me, 0, logs)
    target = local_block(me, 0, targets)
    weight = weight_ref[rows_of(0), :]
    ratio = target / softcap
    own_ref[...] = target - log_total
    rest_ref[...] = weight * jnp.exp(-log_total)
    pick_ref[...] = weight * (jnp.exp(target - log_total) - 1.0) * (1.0 - ratio * ratio)


def run_unpack(me, arrived, weight):
    own = ("v", (32, 128), f32)
    return call(
        unpack, "svv", [("v", COLUMN, f32), own, own, own], scratch=[pltpu.VMEM(COLUMN, f32)] * 2, moved=1 << 20
    )(me, arrived, weight)


def back(me_ref, rows_ref, head_ref, mine_ref, mate_ref):
    me = me_ref[0]
    for n in range(4):
        out = lax.dot_general(
            rows_ref[...],
            head_ref[1152 * n : 1152 * n + 1152, :],
            (((1,), (1,)), ((), ())),
            preferred_element_type=f32,
        ).astype(bf16)
        for i in range(2):
            part = out[:, FEATURES * i : FEATURES * i + FEATURES]
            mine_ref[feature_slot(me, 2 * n + i, 0)] = part[:128].reshape(4, 32, FEATURES)
            mate_ref[feature_slot(me, 2 * n + i, 1)] = part[128:].reshape(4, 32, FEATURES)


BLOCKS = ("v", (8, 4, 32, FEATURES), bf16)
BACK_COST = dict(flops=2 * 256 * D * WIDTH, moved=2 * D * WIDTH)


def run_back(me, rows, head):
    return call(back, "svv", [BLOCKS, BLOCKS], **BACK_COST)(me, rows, head)


def pick(half, me_ref, ids_ref, head_ref, mine_ref, mate_ref, rows):
    ids = ids_ref[256 * half : 256 * half + 256, :]
    for j in range(WIDTH // 128):
        rows[:, 128 * j : 128 * j + 128] = jnp.where(hits_of(me_ref[0], ids, j), 1.0, 0.0).astype(bf16)
    back(me_ref, rows, head_ref, mine_ref, mate_ref)


def pick_low(*refs):
    pick(0, *refs)


def pick_high(*refs):
    pick(1, *refs)


def run_pick(kernel, me, ids, head):
    return call(kernel, "svv", [BLOCKS, BLOCKS], scratch=[pltpu.VMEM((256, WIDTH), bf16)], **BACK_COST)(me, ids, head)


def fold(*refs):
    parts, (p_keep, p_send, q_keep, q_send) = refs[:4], refs[4:]
    for zr in range(2):
        mine, got = parts[2 * zr : 2 * zr + 2]
        for zl in range(2):
            for k in range(4):
                for x in range(4):
                    total = mine[4 * zl + k, x] + got[4 * zl + k, x]
                    (p_keep if k < 2 else p_send)[x // 2, k % 2, x % 2, zr, zl] = total[:16]
                    (q_keep if x < 2 else q_send)[k // 2, k % 2, x % 2, zr, zl] = total[16:]


def run_fold(*parts):
    return call(fold, "vvvv", [("v", (2, 2, 2, 2, 2, 16, FEATURES), bf16)] * 4, moved=512 * D * 4)(*parts)


def fold_picks(*refs):
    parts, (keep, out) = refs[:4], refs[4:]
    for zr in range(2):
        mine, got = parts[2 * zr : 2 * zr + 2]
        for zl in range(2):
            for k in range(4):
                for x in range(4):
                    (keep if k < 2 else out)[k % 2, x, zr, zl] = mine[4 * zl + k, x] + got[4 * zl + k, x]


def run_fold_picks(*parts):
    return call(fold_picks, "vvvv", [("v", (2, 4, 2, 2, 32, FEATURES), bf16)] * 2, moved=512 * D * 4)(*parts)


def finish(rest_ref, pick_ref, own_ref, got_ref, out_ref):
    for start in range(0, FEATURES, 128):
        wide = min(128, FEATURES - start)
        spot = slice(start, start + wide)
        total = own_ref[:, spot].astype(f32) + got_ref[:, spot].astype(f32)
        out_ref[:, spot] = (rest_ref[:, :wide] * total[:32] + pick_ref[:, :wide] * total[32:]).astype(bf16)


def run_finish(rest, pick, own, got):
    return call(finish, "vvvv", [("v", (32, FEATURES), bf16)], moved=1 << 17)(rest, pick, own, got)[0]


def dlogits(me_ref, low_ref, high_ref, log_ref, weight_ref, ids_ref, out_ref):
    me = me_ref[0]
    for n in range(4):
        capped_ref = low_ref if n < 2 else high_ref
        rows = slice(128 * (n % 2), 128 * (n % 2) + 128)
        out_rows = slice(128 * n, 128 * n + 128)
        log_total = log_ref[out_rows, :]
        weight = weight_ref[out_rows, :]
        ids = ids_ref[out_rows, :]
        for j in range(WIDTH // 128):
            spot = slice(128 * j, 128 * j + 128)
            capped = capped_ref[rows, spot]
            prob = jnp.exp(capped - log_total)
            onehot = jnp.where(hits_of(me, ids, j), 1.0, 0.0)
            ratio = capped / softcap
            out_ref[out_rows, spot] = (weight * (prob - onehot) * (1.0 - ratio * ratio)).astype(bf16)


def run_dlogits(me, low, high, log_total, weight, ids):
    return call(
        dlogits, "svvvvv", [("v", (512, WIDTH), bf16)], flops=512 * WIDTH * 16, moved=6 * 512 * WIDTH
    )(me, low, high, log_total, weight, ids)[0]


def head_gradient(low_ref, high_ref, dlog_ref, out_ref, rows, buffer, sems):
    def copy(i):
        return pltpu.make_async_copy(buffer.at[i % 2], out_ref.at[pl.ds(512 * i, 512)], sems.at[i % 2])

    for i in range(9):
        spot = slice(512 * i, 512 * i + 512)
        rows[:256, :] = low_ref[:, spot]
        rows[256:, :] = high_ref[:, spot]
        if i >= 2:
            copy(i - 2).wait()
        buffer[i % 2] = lax.dot_general(
            rows[...], dlog_ref[...], (((0,), (0,)), ((), ())), preferred_element_type=f32
        ).astype(bf16)
        copy(i).start()
    copy(7).wait()
    copy(8).wait()


def run_head_gradient(low, high, dlog):
    return call(
        head_gradient,
        "vvv",
        [("h", (D, WIDTH), bf16)],
        scratch=[
            pltpu.VMEM((512, 512), bf16),
            pltpu.VMEM((2, 512, WIDTH), bf16),
            pltpu.SemaphoreType.DMA((2,)),
        ],
        flops=2 * 512 * WIDTH * D,
        moved=2 * D * WIDTH,
    )(low, high, dlog)[0]


def tie(*arrays):
    return lax.optimization_barrier(arrays)


def add(a, b):
    return (a.astype(f32) + b.astype(f32)).astype(bf16)


def halve(keep, got):
    n = keep.shape[0] // 2
    return add(keep[:n], got[:n]), add(keep[n:], got[n:])


def local(hidden, head, verdict_ids, row_weight):
    me = (lax.axis_index("dp") * 8 + lax.axis_index("vocab")).astype(jnp.int32).reshape(1)
    ids, weight = run_spread(me, verdict_ids.astype(f32).reshape(4, 128), row_weight.reshape(4, 128))

    a1, a2 = send(hidden, X1), send(hidden, X2)
    o0 = send(hidden, ZH)

    g0_mine, g0_mate = run_pick(pick_low, me, ids, head)
    a1, g0_mine = tie(a1, g0_mine)
    a3 = send(a1, X2)
    o1, o2, o3 = send(o0, X1), send(o0, X2), send(a3, ZH)
    g1_mine, g1_mate = run_pick(pick_high, me, ids, head)
    g_keep, g_send = run_fold_picks(g0_mine, send(g0_mate, CORE), g1_mine, send(g1_mate, CORE))
    g_got = send(g_send, Y2)

    own_half = [hidden, a1, a2, a3]
    own_half += [send(piece, CORE) for piece in own_half]
    rows0, capped0, term0, total0, target0 = run_forward(forward_low, me, own_half, ids, head)
    a0_mine, a0_mate = run_back(me, term0, head)
    o3, total0, a0_mate = tie(o3, total0, a0_mate)
    other_half = [o0, o1, o2, o3]
    other_half += [send(piece, CORE) for piece in other_half]
    rows1, capped1, term1, total1, target1 = run_forward(forward_high, me, other_half, ids, head)
    a1_mine, a1_mate = run_back(me, term1, head)
    p_keep, p_send, q_keep, q_send = run_fold(a0_mine, send(a0_mate, CORE), a1_mine, send(a1_mate, CORE))

    total0, p_keep = tie(total0, p_keep)
    arrived = lax.all_to_all(run_pack(me, total0, total1, target0, target1), AXES, 0, 0, tiled=True)
    log_total, own, rest, pick = run_unpack(me, arrived, weight)
    dlog = run_dlogits(me, capped0, capped1, log_total, weight, ids)
    head_grad = run_head_gradient(rows0, rows1, dlog)

    p_got, q_got = send(p_send, Y2), send(q_send, X2)
    p_keep, p_send = halve(p_keep, p_got)
    q_keep, q_send = halve(q_keep, q_got)
    g_keep, g_send = halve(g_keep, g_got)
    p_got, q_got, g_got = send(p_send, X2), send(q_send, Y2), send(g_send, Y1)
    both_keep, both_send = (
        jnp.concatenate([add(p_keep[0, i], p_got[0, i]), add(q_keep[0, i], q_got[0, i])], axis=3) for i in (0, 1)
    )
    g_keep, g_send = halve(g_keep[0], g_got[0])
    both_keep, both_send = halve(both_keep, send(both_send, Y1))
    g_keep, g_send = halve(g_keep, send(g_send, X2))
    both = add(both_keep[0], send(both_send[0], X1))
    g = add(g_keep[0], send(g_send[0], X1))
    both = jnp.concatenate([both, g], axis=2)
    got = send(both[1], ZH)
    keep, out = add(both[0, 0], got[1]), add(both[0, 1], got[0])
    hidden_grad = run_finish(rest, pick, keep, send(out, ZL))
    return (own[:, 0], head_grad, hidden_grad)


def solution(mesh):
    in_specs = (P("dp", None), P(None, ("dp", "vocab")), P(), P())
    out_specs = (P("dp"), P(None, ("dp", "vocab")), P("dp", "vocab"))
    return jax.shard_map(local, mesh=mesh, in_specs=in_specs, out_specs=out_specs, check_vma=False)
```

profile of v0, /device:TPU:0, one launch (start us, length us, event | category | flops | bytes accessed | tf_op | source)
XLA Modules:
  0.0 128.3 jit_solution(9305330795683511324)
XLA Ops:
  0.6 2.9 %collective-permute-start.3 = (bf16[32,4608]{1,0:T(8,128)(2,1)}, bf16[32,4608]{1,0:T(8,128)(2,1)S(1)}, u32[]{:S(2)}, u32[]{:S(2)}) collective-permute-start(bf16[32,4608]{1,0:T(8,128)(2,1)} %refs_1_.1), channel_id=1, source_target_pairs={{0,48},{1,49},{2,50},{3,51},{4,52},{5,53},{6,54},{7,55},{8,24},{9,... | collective-permute-start | bytes 884744 | tf_op jit(solution)/shard_map/ppermute | solution.py:29
  5.4 3.7 %copy-done = bf16[4608,1024]{1,0:T(8,128)(2,1)S(1)} copy-done((bf16[4608,1024]{1,0:T(8,128)(2,1)S(1)}, bf16[4608,1024]{1,0:T(8,128)(2,1)}, u32[]{:S(2)}) %copy-start) | copy-done | bytes 9437208
  9.1 3.0 %pick_low.1 = (bf16[8,4,32,576]{3,2,1,0:T(8,128)(2,1)S(1)}, bf16[8,4,32,576]{3,2,1,0:T(8,128)(2,1)S(1)}) custom-call(s32[1]{0:T(128)} %bitcast.me_ref.refs_0_, f32[512,128]{1,0:T(8,128)S(1)} %get-tuple-element.40.refs_1_.refs_9_.ids_ref, bf16[4608,1024]{1,0:T(8,128)(2,1)S(1)} %copy-done), custom_call_target="tpu_custom_call" | custom-call | flops 2415919104 | bytes 9437184 | tf_op jit(solution)/shard_map/pick_low/pallas_call | solution.py:225
  13.3 4.0 %collective-permute-start.9 = (bf16[32,4608]{1,0:T(8,128)(2,1)S(1)}, bf16[32,4608]{1,0:T(8,128)(2,1)S(1)}, u32[]{:S(2)}, u32[]{:S(2)}) collective-permute-start(bf16[32,4608]{1,0:T(8,128)(2,1)S(1)} %copy-done.4), channel_id=1, source_target_pairs={{0,68},{1,69},{2,70},{3,71},{4,64},{5,65},{6,66},{7,67},{8,76},{9,... | collective-permute-start | bytes 884744 | tf_op jit(solution)/shard_map/ppermute | solution.py:29
  17.9 2.2 %collective-permute-done.1.refs_4_ = bf16[32,4608]{1,0:T(8,128)(2,1)S(1)} collective-permute-done((bf16[32,4608]{1,0:T(8,128)(2,1)S(1)}, bf16[32,4608]{1,0:T(8,128)(2,1)S(1)}, u32[]{:S(2)}, u32[]{:S(2)}) %collective-permute-start.1) | collective-permute-done | bytes 294944 | tf_op jit(solution)/shard_map/ppermute | solution.py:29
  20.1 3.5 %collective-permute-done.9.refs_1_ = bf16[32,4608]{1,0:T(8,128)(2,1)S(1)} collective-permute-done((bf16[32,4608]{1,0:T(8,128)(2,1)S(1)}, bf16[32,4608]{1,0:T(8,128)(2,1)S(1)}, u32[]{:S(2)}, u32[]{:S(2)}) %collective-permute-start.9) | collective-permute-done | bytes 294944 | tf_op jit(solution)/shard_map/ppermute | solution.py:29
  23.6 1.6 %collective-permute-start.11 = (bf16[32,4608]{1,0:T(8,128)(2,1)S(1)}, bf16[32,4608]{1,0:T(8,128)(2,1)S(1)}, u32[]{:S(2)}, u32[]{:S(2)}) collective-permute-start(bf16[32,4608]{1,0:T(8,128)(2,1)S(1)} %collective-permute-done.9.refs_1_), channel_id=1, source_target_pairs={{0,48},{1,49},{2,50},{3,51},{4,52},{5,53},{6,54},{7,55},{8,24},{9,... | collective-permute-start | bytes 884744 | tf_op jit(solution)/shard_map/ppermute | solution.py:29
  25.1 3.0 %pick_high.1 = (bf16[8,4,32,576]{3,2,1,0:T(8,128)(2,1)S(1)}, bf16[8,4,32,576]{3,2,1,0:T(8,128)(2,1)S(1)}) custom-call(s32[1]{0:T(128)} %bitcast.me_ref.refs_0_, f32[512,128]{1,0:T(8,128)S(1)} %get-tuple-element.40.refs_1_.refs_9_.ids_ref, bf16[4608,1024]{1,0:T(8,128)(2,1)S(1)} %copy-done), custom_call_target="tpu_custom_call" | custom-call | flops 2415919104 | bytes 9437184 | tf_op jit(solution)/shard_map/pick_high/pallas_call | solution.py:225
  29.8 3.0 %collective-permute-start.2 = (bf16[32,4608]{1,0:T(8,128)(2,1)S(1)}, bf16[32,4608]{1,0:T(8,128)(2,1)S(1)}, u32[]{:S(2)}, u32[]{:S(2)}) collective-permute-start(bf16[32,4608]{1,0:T(8,128)(2,1)S(1)} %collective-permute-done.1.refs_4_), channel_id=1, source_target_pairs={{0,68},{1,69},{2,70},{3,71},{4,64},{5,65},{6,66},{7,67},{8,76},{9,... | collective-permute-start | bytes 884744 | tf_op jit(solution)/shard_map/ppermute | solution.py:29
  32.8 3.0 %forward_low.1 = (bf16[256,4608]{1,0:T(8,128)(2,1)S(1)}, f32[256,1024]{1,0:T(8,128)S(1)}, bf16[256,1024]{1,0:T(8,128)(2,1)S(1)}, f32[256,128]{1,0:T(8,128)S(1)}, f32[256,128]{1,0:T(8,128)S(1)}) custom-call(s32[1]{0:T(128)} %bitcast.me_ref.refs_0_, bf16[32,4608]{1,0:T(8,128)(2,1)S(1)} %copy-done.4, bf16[32,4608]{1,0:T(8,128)(2,1)S(1)} %collective-permute-done.refs_2_, ...), custom_call_target="tpu_custom_call" | custom-call | flops 2415919104 | bytes 9437184 | tf_op jit(solution)/shard_map/forward_low/pallas_call | solution.py:129
  37.3 3.1 %back.2 = (bf16[8,4,32,576]{3,2,1,0:T(8,128)(2,1)S(1)}, bf16[8,4,32,576]{3,2,1,0:T(8,128)(2,1)S(1)}) custom-call(s32[1]{0:T(128)} %bitcast.me_ref.refs_0_, bf16[256,1024]{1,0:T(8,128)(2,1)S(1)} %get-tuple-element.44.rows_ref, bf16[4608,1024]{1,0:T(8,128)(2,1)S(1)} %bitcast.61), custom_call_target="tpu_custom_call" | custom-call | flops 2415919104 | bytes 9437184 | tf_op jit(solution)/shard_map/back/pallas_call | solution.py:206
  42.9 3.0 %forward_high.1 = (bf16[256,4608]{1,0:T(8,128)(2,1)S(1)}, f32[256,1024]{1,0:T(8,128)S(1)}, bf16[256,1024]{1,0:T(8,128)(2,1)S(1)}, f32[256,128]{1,0:T(8,128)S(1)}, f32[256,128]{1,0:T(8,128)S(1)}) custom-call(s32[1]{0:T(128)} %bitcast.me_ref.refs_0_, bf16[32,4608]{1,0:T(8,128)(2,1)S(1)} %collective-permute-done.9.refs_1_, ...), custom_call_target="tpu_custom_call" | custom-call | flops 2415919104 | bytes 9437184 | tf_op jit(solution)/shard_map/forward_high/pallas_call | solution.py:129
  47.3 3.1 %back.3 = (bf16[8,4,32,576]{3,2,1,0:T(8,128)(2,1)S(1)}, bf16[8,4,32,576]{3,2,1,0:T(8,128)(2,1)S(1)}) custom-call(s32[1]{0:T(128)} %bitcast.me_ref.refs_0_, bf16[256,1024]{1,0:T(8,128)(2,1)S(1)} %get-tuple-element.50.rows_ref, bf16[4608,1024]{1,0:T(8,128)(2,1)S(1)} %bitcast.61), custom_call_target="tpu_custom_call" | custom-call | flops 2415919104 | bytes 9437184 | tf_op jit(solution)/shard_map/back/pallas_call | solution.py:206
  51.1 3.1 %collective-permute-start.25 = (bf16[2,4,2,2,32,576]{5,4,3,2,1,0:T(8,128)(2,1)S(1)}, bf16[2,4,2,2,32,576]{5,4,3,2,1,0:T(8,128)(2,1)S(1)}, u32[]{:S(2)}, u32[]{:S(2)}) collective-permute-start(bf16[2,4,2,2,32,576]{5,4,3,2,1,0:T(8,128)(2,1)S(1)} %get-tuple-element.76), channel_id=1, source_target_pairs={{0,3},{1,2},{2,1},{3,0},{4,7},{5,6},{6,5},{7,4},{8,9},{9,8},{10,11... | collective-permute-start | bytes 3538952 | tf_op jit(solution)/shard_map/ppermute | solution.py:29
  54.2 1.4 %fold.1 = (bf16[2,2,2,2,2,16,576]{6,5,4,3,2,1,0:T(8,128)(2,1)S(1)}, bf16[2,2,2,2,2,16,576]{6,5,4,3,2,1,0:T(8,128)(2,1)}, bf16[2,2,2,2,2,16,576]{6,5,4,3,2,1,0:T(...) custom-call(bf16[8,4,32,576]{3,2,1,0:T(8,128)(2,1)S(1)} %get-tuple-element.47.refs_0_, ...), custom_call_target="tpu_custom_call" | custom-call | bytes 9437184 | tf_op jit(solution)/shard_map/fold/pallas_call | solution.py:241
  56.6 2.3 %collective-permute-start.17 = (bf16[2,2,2,2,2,16,576]{6,5,4,3,2,1,0:T(8,128)(2,1)}, bf16[2,2,2,2,2,16,576]{6,5,4,3,2,1,0:T(8,128)(2,1)}, u32[]{:S(2)}, u32[]{:S(2)}) collective-permute-start(bf16[2,2,2,2,2,16,576]{6,5,4,3,2,1,0:T(8,128)(2,1)} %get-tuple-element.68), channel_id=1, source_target_pairs={{0,3},{1,2},{2,1},{3,0},{4,7},{5,6},{6,5},{7,4},{8,9},{9,8},{10,11... | collective-permute-start | bytes 1769480 | tf_op jit(solution)/shard_map/ppermute | solution.py:29
  58.8 1.6 %collective-permute-start.19 = (bf16[2,2,2,2,2,16,576]{6,5,4,3,2,1,0:T(8,128)(2,1)}, bf16[2,2,2,2,2,16,576]{6,5,4,3,2,1,0:T(8,128)(2,1)}, u32[]{:S(2)}, u32[]{:S(2)}) collective-permute-start(bf16[2,2,2,2,2,16,576]{6,5,4,3,2,1,0:T(8,128)(2,1)} %get-tuple-element.70), channel_id=1, source_target_pairs={{0,48},{1,49},{2,50},{3,51},{4,52},{5,53},{6,54},{7,55},{8,24},{9,... | collective-permute-start | bytes 1769480 | tf_op jit(solution)/shard_map/ppermute | solution.py:29
  60.4 9.6 %collective-permute-done.25 = bf16[2,4,2,2,32,576]{5,4,3,2,1,0:T(8,128)(2,1)S(1)} collective-permute-done((bf16[2,4,2,2,32,576]{5,4,3,2,1,0:T(8,128)(2,1)S(1)}, bf16[2,4,2,2,32,576]{5,4,3,2,1,0:T(8,128)(2,1)S(1)}, u32[]{:S(2)}, u32[]{:S(2)}) %collective-permute-start.25) | collective-permute-done | bytes 1179680 | tf_op jit(solution)/shard_map/ppermute | solution.py:29
  70.0 1.4 %add_convert_fusion.1 = (bf16[1,4,2,2,32,576]{5,4,3,2,1,0:T(8,128)(2,1)}, bf16[1,4,2,2,32,576]{5,4,3,2,1,0:T(8,128)(2,1)}) fusion(bf16[2,4,2,2,32,576]{5,4,3,2,1,0:T(8,128)(2,1)S(1)} %collective-permute-done.25, bf16[2,4,2,2,32,576]{5,4,3,2,1,0:T(8,128)(2,1)S(1)} %get-tuple-element.75), kind=kLoop, calls=%fused_computation.1 | loop fusion | flops 2359296 | bytes 3538944 | tf_op jit(solution)/shard_map/convert_element_type | solution.py:332
  72.9 8.9 %all-to-all-start = ((f32[128,8,128]{2,1,0:T(8,128)}), f32[128,8,128]{2,1,0:T(8,128)S(1)}, u32[]{:S(2)}, u32[]{:S(2)}) async-start(f32[128,8,128]{2,1,0:T(8,128)} %pack.1), calls=%async_computation | async-start | bytes 1048576 | tf_op jit(solution)/shard_map/all_to_all | solution.py:367
  81.8 1.5 %add_convert_fusion.7 = (bf16[1,2,2,2,2,16,576]{6,5,4,3,2,1,0:T(8,128)(2,1)S(1)}, bf16[1,2,2,2,2,16,576]{6,5,4,3,2,1,0:T(8,128)(2,1)S(1)}) fusion(bf16[2,2,2,2,2,16,576]{6,5,4,3,2,1,0:T(8,128)(2,1)} %collective-permute-done.17, bf16[2,2,2,2,2,16,576]{6,5,4,3,2,1,0:T(8,128)(2,1)} %copy-done.3), kind=kLoop, calls=%fused_computation.7 | loop fusion | flops 1179648 | bytes 1769472 | tf_op jit(solution)/shard_map/convert_element_type | solution.py:332
  83.3 2.0 %collective-permute-start.18 = (bf16[1,2,2,2,2,16,576]{6,5,4,3,2,1,0:T(8,128)(2,1)S(1)}, bf16[1,2,2,2,2,16,576]{6,5,4,3,2,1,0:T(8,128)(2,1)S(1)}, u32[]{:S(2)}, u32[]{:S(2)}) collective-permute-start(bf16[1,2,2,2,2,16,576]{6,5,4,3,2,1,0:T(8,128)(2,1)S(1)} %get-tuple-element.82), channel_id=1, source_target_pairs={{0,48},{1,49},{2,50},{3,51},{4,52},{5,53},{6,54},{7,55},{8,24},{9,... | collective-permute-start | bytes 884744 | tf_op jit(solution)/shard_map/ppermute | solution.py:29
  86.6 2.9 %collective-permute-start.20 = (bf16[1,2,2,2,2,16,576]{6,5,4,3,2,1,0:T(8,128)(2,1)S(1)}, bf16[1,2,2,2,2,16,576]{6,5,4,3,2,1,0:T(8,128)(2,1)S(1)}, u32[]{:S(2)}, u32[]{:S(2)}) collective-permute-start(bf16[1,2,2,2,2,16,576]{6,5,4,3,2,1,0:T(8,128)(2,1)S(1)} %get-tuple-element.84), channel_id=1, source_target_pairs={{0,3},{1,2},{2,1},{3,0},{4,7},{5,6},{6,5},{7,4},{8,9},{9,8},{10,11... | collective-permute-start | bytes 884744 | tf_op jit(solution)/shard_map/ppermute | solution.py:29
  89.5 2.1 %add_convert_fusion.3 = (bf16[1,2,2,2,32,576]{5,4,3,2,1,0:T(8,128)(2,1)}, bf16[2,2,2,32,576]{4,3,2,1,0:T(8,128)(2,1)}) fusion(bf16[1,4,2,2,32,576]{5,4,3,2,1,0:T(8,128)(2,1)} %collective-permute-done.26, bf16[1,4,2,2,32,576]{5,4,3,2,1,0:T(8,128)(2,1)S(1)} %copy-done.10), kind=kLoop, calls=%fused_computation.3 | loop fusion | flops 1179648 | bytes 1769472 | tf_op jit(solution)/shard_map/convert_element_type | solution.py:332
  93.3 1.9 %collective-permute-done.20 = bf16[1,2,2,2,2,16,576]{6,5,4,3,2,1,0:T(8,128)(2,1)S(1)} collective-permute-done((bf16[1,2,2,2,2,16,576]{6,5,4,3,2,1,0:T(8,128)(2,1)S(1)}, bf16[1,2,2,2,2,16,576]{6,5,4,3,2,1,0:T(8,128)(2,1)S(1)}, u32[]{:S(2)}, u32[]{:S(2)}) %collective-permute-start.20) | collective-permute-done | bytes 294944 | tf_op jit(solution)/shard_map/ppermute | solution.py:29
  97.6 2.6 %collective-permute-done.27 = bf16[2,2,2,32,576]{4,3,2,1,0:T(8,128)(2,1)} collective-permute-done((bf16[2,2,2,32,576]{4,3,2,1,0:T(8,128)(2,1)}, bf16[2,2,2,32,576]{4,3,2,1,0:T(8,128)(2,1)}, u32[]{:S(2)}, u32[]{:S(2)}) %collective-permute-start.27) | collective-permute-done | bytes 294944 | tf_op jit(solution)/shard_map/ppermute | solution.py:29
  101.2 2.2 %collective-permute-done.21 = bf16[2,2,2,32,576]{4,3,2,1,0:T(8,128)(2,1)} collective-permute-done((bf16[2,2,2,32,576]{4,3,2,1,0:T(8,128)(2,1)}, bf16[2,2,2,32,576]{4,3,2,1,0:T(8,128)(2,1)}, u32[]{:S(2)}, u32[]{:S(2)}) %collective-permute-start.21) | collective-permute-done | bytes 294944 | tf_op jit(solution)/shard_map/ppermute | solution.py:29
  105.1 1.5 %collective-permute-done.28 = bf16[2,2,32,576]{3,2,1,0:T(8,128)(2,1)S(1)} collective-permute-done((bf16[2,2,32,576]{3,2,1,0:T(8,128)(2,1)S(1)}, bf16[2,2,32,576]{3,2,1,0:T(8,128)(2,1)S(1)}, u32[]{:S(2)}, u32[]{:S(2)}) %collective-permute-start.28) | collective-permute-done | bytes 147488 | tf_op jit(solution)/shard_map/ppermute | solution.py:29
  107.5 2.5 %collective-permute-done.22 = bf16[2,2,32,576]{3,2,1,0:T(8,128)(2,1)S(1)} collective-permute-done((bf16[2,2,32,576]{3,2,1,0:T(8,128)(2,1)S(1)}, bf16[2,2,32,576]{3,2,1,0:T(8,128)(2,1)S(1)}, u32[]{:S(2)}, u32[]{:S(2)}) %collective-permute-start.22) | collective-permute-done | bytes 147488 | tf_op jit(solution)/shard_map/ppermute | solution.py:29
  111.0 3.5 %collective-permute-start.29 = (bf16[2,64,576]{2,1,0:T(8,128)(2,1)S(1)}, bf16[2,64,576]{2,1,0:T(8,128)(2,1)S(1)}, u32[]{:S(2)}, u32[]{:S(2)}) collective-permute-start(bf16[2,64,576]{2,1,0:T(8,128)(2,1)S(1)} %fusion.14), channel_id=1, source_target_pairs={{0,68},{1,69},{2,70},{3,71},{4,64},{5,65},{6,66},{7,67},{8,76},{9,... | collective-permute-start | bytes 442376 | tf_op jit(solution)/shard_map/ppermute | solution.py:29
  114.4 8.6 %head_gradient.1 = bf16[4608,1024]{1,0:T(8,128)(2,1)} custom-call(bf16[256,4608]{1,0:T(8,128)(2,1)S(1)} %copy-done.7, bf16[256,4608]{1,0:T(8,128)(2,1)S(1)} %copy-done.9, bf16[512,1024]{1,0:T(8,128)(2,1)S(1)} %dlogits.1.dlog_ref), custom_call_target="tpu_custom_call" | custom-call | flops 4831838208 | bytes 9437184 | tf_op jit(solution)/shard_map/head_gradient/pallas_call | solution.py:313
  123.8 3.8 %collective-permute-done.30.got_ref = bf16[64,576]{1,0:T(8,128)(2,1)S(1)} collective-permute-done((bf16[64,576]{1,0:T(8,128)(2,1)S(1)}, bf16[64,576]{1,0:T(8,128)(2,1)S(1)}, u32[]{:S(2)}, u32[]{:S(2)}) %collective-permute-start.30) | collective-permute-done | bytes 73760 | tf_op jit(solution)/shard_map/ppermute | solution.py:29
  (92 shorter events, 25.2 us)
Async XLA Ops:
  0.6 16.7 %collective-permute-start.3 = (bf16[32,4608]{1,0:T(8,128)(2,1)}, bf16[32,4608]{1,0:T(8,128)(2,1)S(1)}, u32[]{:S(2)}, u32[]{:S(2)}) collective-permute-start(bf16[32,4608]{1,0:T(8,128)(2,1)} %refs_1_.1), channel_id=1, source_target_pairs={{0,48},{1,49},{2,50},{3,51},{4,52},{5,53},{6,54},{7,55},{8,24},{9,... | collective-permute-start | bytes 884744 | tf_op jit(solution)/shard_map/ppermute | solution.py:29
  3.6 8.5 %collective-permute-start = (bf16[32,4608]{1,0:T(8,128)(2,1)}, bf16[32,4608]{1,0:T(8,128)(2,1)S(1)}, u32[]{:S(2)}, u32[]{:S(2)}) collective-permute-start(bf16[32,4608]{1,0:T(8,128)(2,1)} %refs_1_.1), channel_id=1, source_target_pairs={{0,16},{1,17},{2,18},{3,19},{4,20},{5,21},{6,22},{7,23},{8,56},{9,... | collective-permute-start | bytes 884744 | tf_op jit(solution)/shard_map/ppermute | solution.py:29
  12.1 8.0 %collective-permute-start.1 = (bf16[32,4608]{1,0:T(8,128)(2,1)S(1)}, bf16[32,4608]{1,0:T(8,128)(2,1)S(1)}, u32[]{:S(2)}, u32[]{:S(2)}) collective-permute-start(bf16[32,4608]{1,0:T(8,128)(2,1)S(1)} %collective-permute-done.refs_2_), channel_id=1, source_target_pairs={{0,48},{1,49},{2,50},{3,51},{4,52},{5,53},{6,54},{7,55},{8,24},{9,... | collective-permute-start | bytes 884744 | tf_op jit(solution)/shard_map/ppermute | solution.py:29
  13.3 10.3 %collective-permute-start.9 = (bf16[32,4608]{1,0:T(8,128)(2,1)S(1)}, bf16[32,4608]{1,0:T(8,128)(2,1)S(1)}, u32[]{:S(2)}, u32[]{:S(2)}) collective-permute-start(bf16[32,4608]{1,0:T(8,128)(2,1)S(1)} %copy-done.4), channel_id=1, source_target_pairs={{0,68},{1,69},{2,70},{3,71},{4,64},{5,65},{6,66},{7,67},{8,76},{9,... | collective-permute-start | bytes 884744 | tf_op jit(solution)/shard_map/ppermute | solution.py:29
  17.3 10.8 %collective-permute-start.4 = (bf16[32,4608]{1,0:T(8,128)(2,1)S(1)}, bf16[32,4608]{1,0:T(8,128)(2,1)S(1)}, u32[]{:S(2)}, u32[]{:S(2)}) collective-permute-start(bf16[32,4608]{1,0:T(8,128)(2,1)S(1)} %copy-done.4), channel_id=1, source_target_pairs={{0,8},{1,9},{2,10},{3,11},{4,12},{5,13},{6,14},{7,15},{8,0},{9,1},... | collective-permute-start | bytes 884744 | tf_op jit(solution)/shard_map/ppermute | solution.py:29
  17.4 10.9 %collective-permute-start.6 = (bf16[32,4608]{1,0:T(8,128)(2,1)S(1)}, bf16[32,4608]{1,0:T(8,128)(2,1)S(1)}, u32[]{:S(2)}, u32[]{:S(2)}) collective-permute-start(bf16[32,4608]{1,0:T(8,128)(2,1)S(1)} %collective-permute-done.3.refs_3_), channel_id=1, source_target_pairs={{0,8},{1,9},{2,10},{3,11},{4,12},{5,13},{6,14},{7,15},{8,0},{9,1},... | collective-permute-start | bytes 884744 | tf_op jit(solution)/shard_map/ppermute | solution.py:29
  17.9 10.9 %collective-permute-start.5 = (bf16[32,4608]{1,0:T(8,128)(2,1)S(1)}, bf16[32,4608]{1,0:T(8,128)(2,1)S(1)}, u32[]{:S(2)}, u32[]{:S(2)}) collective-permute-start(bf16[32,4608]{1,0:T(8,128)(2,1)S(1)} %collective-permute-done.refs_2_), channel_id=1, source_target_pairs={{0,8},{1,9},{2,10},{3,11},{4,12},{5,13},{6,14},{7,15},{8,0},{9,1},... | collective-permute-start | bytes 884744 | tf_op jit(solution)/shard_map/ppermute | solution.py:29
  20.1 9.7 %collective-permute-start.7 = (bf16[32,4608]{1,0:T(8,128)(2,1)S(1)}, bf16[32,4608]{1,0:T(8,128)(2,1)S(1)}, u32[]{:S(2)}, u32[]{:S(2)}) collective-permute-start(bf16[32,4608]{1,0:T(8,128)(2,1)S(1)} %collective-permute-done.1.refs_4_), channel_id=1, source_target_pairs={{0,8},{1,9},{2,10},{3,11},{4,12},{5,13},{6,14},{7,15},{8,0},{9,1},... | collective-permute-start | bytes 884744 | tf_op jit(solution)/shard_map/ppermute | solution.py:29
  23.6 13.6 %collective-permute-start.11 = (bf16[32,4608]{1,0:T(8,128)(2,1)S(1)}, bf16[32,4608]{1,0:T(8,128)(2,1)S(1)}, u32[]{:S(2)}, u32[]{:S(2)}) collective-permute-start(bf16[32,4608]{1,0:T(8,128)(2,1)S(1)} %collective-permute-done.9.refs_1_), channel_id=1, source_target_pairs={{0,48},{1,49},{2,50},{3,51},{4,52},{5,53},{6,54},{7,55},{8,24},{9,... | collective-permute-start | bytes 884744 | tf_op jit(solution)/shard_map/ppermute | solution.py:29
  28.1 22.7 %collective-permute-start.24 = (bf16[8,4,32,576]{3,2,1,0:T(8,128)(2,1)S(1)}, bf16[8,4,32,576]{3,2,1,0:T(8,128)(2,1)S(1)}, u32[]{:S(2)}, u32[]{:S(2)}) collective-permute-start(bf16[8,4,32,576]{3,2,1,0:T(8,128)(2,1)S(1)} %get-tuple-element.74), channel_id=1, source_target_pairs={{0,8},{1,9},{2,10},{3,11},{4,12},{5,13},{6,14},{7,15},{8,0},{9,1},... | collective-permute-start | bytes 3538952 | tf_op jit(solution)/shard_map/ppermute | solution.py:29
  28.2 12.8 %collective-permute-start.12 = (bf16[32,4608]{1,0:T(8,128)(2,1)S(1)}, bf16[32,4608]{1,0:T(8,128)(2,1)S(1)}, u32[]{:S(2)}, u32[]{:S(2)}) collective-permute-start(bf16[32,4608]{1,0:T(8,128)(2,1)S(1)} %collective-permute-done.9.refs_1_), channel_id=1, source_target_pairs={{0,8},{1,9},{2,10},{3,11},{4,12},{5,13},{6,14},{7,15},{8,0},{9,1},... | collective-permute-start | bytes 884744 | tf_op jit(solution)/shard_map/ppermute | solution.py:29
  28.7 11.7 %collective-permute-start.10 = (bf16[32,4608]{1,0:T(8,128)(2,1)S(1)}, bf16[32,4608]{1,0:T(8,128)(2,1)S(1)}, u32[]{:S(2)}, u32[]{:S(2)}) collective-permute-start(bf16[32,4608]{1,0:T(8,128)(2,1)S(1)} %collective-permute-done.9.refs_1_), channel_id=1, source_target_pairs={{0,16},{1,17},{2,18},{3,19},{4,20},{5,21},{6,22},{7,23},{8,56},{9,... | collective-permute-start | bytes 884744 | tf_op jit(solution)/shard_map/ppermute | solution.py:29
  29.8 11.0 %collective-permute-start.2 = (bf16[32,4608]{1,0:T(8,128)(2,1)S(1)}, bf16[32,4608]{1,0:T(8,128)(2,1)S(1)}, u32[]{:S(2)}, u32[]{:S(2)}) collective-permute-start(bf16[32,4608]{1,0:T(8,128)(2,1)S(1)} %collective-permute-done.1.refs_4_), channel_id=1, source_target_pairs={{0,68},{1,69},{2,70},{3,71},{4,64},{5,65},{6,66},{7,67},{8,76},{9,... | collective-permute-start | bytes 884744 | tf_op jit(solution)/shard_map/ppermute | solution.py:29
  37.2 13.7 %collective-permute-start.23 = (bf16[8,4,32,576]{3,2,1,0:T(8,128)(2,1)S(1)}, bf16[8,4,32,576]{3,2,1,0:T(8,128)(2,1)S(1)}, u32[]{:S(2)}, u32[]{:S(2)}) collective-permute-start(bf16[8,4,32,576]{3,2,1,0:T(8,128)(2,1)S(1)} %get-tuple-element.72), channel_id=1, source_target_pairs={{0,8},{1,9},{2,10},{3,11},{4,12},{5,13},{6,14},{7,15},{8,0},{9,1},... | collective-permute-start | bytes 3538952 | tf_op jit(solution)/shard_map/ppermute | solution.py:29
  40.4 1.7 %collective-permute-start.14 = (bf16[32,4608]{1,0:T(8,128)(2,1)S(1)}, bf16[32,4608]{1,0:T(8,128)(2,1)S(1)}, u32[]{:S(2)}, u32[]{:S(2)}) collective-permute-start(bf16[32,4608]{1,0:T(8,128)(2,1)S(1)} %collective-permute-done.11.refs_3_), channel_id=1, source_target_pairs={{0,8},{1,9},{2,10},{3,11},{4,12},{5,13},{6,14},{7,15},{8,0},{9,1},... | collective-permute-start | bytes 884744 | tf_op jit(solution)/shard_map/ppermute | solution.py:29
  40.8 1.7 %collective-permute-start.13 = (bf16[32,4608]{1,0:T(8,128)(2,1)S(1)}, bf16[32,4608]{1,0:T(8,128)(2,1)S(1)}, u32[]{:S(2)}, u32[]{:S(2)}) collective-permute-start(bf16[32,4608]{1,0:T(8,128)(2,1)S(1)} %collective-permute-done.10.refs_2_), channel_id=1, source_target_pairs={{0,8},{1,9},{2,10},{3,11},{4,12},{5,13},{6,14},{7,15},{8,0},{9,1},... | collective-permute-start | bytes 884744 | tf_op jit(solution)/shard_map/ppermute | solution.py:29
  41.0 1.9 %collective-permute-start.15 = (bf16[32,4608]{1,0:T(8,128)(2,1)S(1)}, bf16[32,4608]{1,0:T(8,128)(2,1)S(1)}, u32[]{:S(2)}, u32[]{:S(2)}) collective-permute-start(bf16[32,4608]{1,0:T(8,128)(2,1)S(1)} %collective-permute-done.2.refs_4_), channel_id=1, source_target_pairs={{0,8},{1,9},{2,10},{3,11},{4,12},{5,13},{6,14},{7,15},{8,0},{9,1},... | collective-permute-start | bytes 884744 | tf_op jit(solution)/shard_map/ppermute | solution.py:29
  42.1 12.2 %collective-permute-start.8 = (bf16[8,4,32,576]{3,2,1,0:T(8,128)(2,1)S(1)}, bf16[8,4,32,576]{3,2,1,0:T(8,128)(2,1)S(1)}, u32[]{:S(2)}, u32[]{:S(2)}) collective-permute-start(bf16[8,4,32,576]{3,2,1,0:T(8,128)(2,1)S(1)} %get-tuple-element.48), channel_id=1, source_target_pairs={{0,8},{1,9},{2,10},{3,11},{4,12},{5,13},{6,14},{7,15},{8,0},{9,1},... | collective-permute-start | bytes 3538952 | tf_op jit(solution)/shard_map/ppermute | solution.py:29
  50.4 3.9 %collective-permute-start.16 = (bf16[8,4,32,576]{3,2,1,0:T(8,128)(2,1)S(1)}, bf16[8,4,32,576]{3,2,1,0:T(8,128)(2,1)S(1)}, u32[]{:S(2)}, u32[]{:S(2)}) collective-permute-start(bf16[8,4,32,576]{3,2,1,0:T(8,128)(2,1)S(1)} %get-tuple-element.52), channel_id=1, source_target_pairs={{0,8},{1,9},{2,10},{3,11},{4,12},{5,13},{6,14},{7,15},{8,0},{9,1},... | collective-permute-start | bytes 3538952 | tf_op jit(solution)/shard_map/ppermute | solution.py:29
  51.1 18.9 %collective-permute-start.25 = (bf16[2,4,2,2,32,576]{5,4,3,2,1,0:T(8,128)(2,1)S(1)}, bf16[2,4,2,2,32,576]{5,4,3,2,1,0:T(8,128)(2,1)S(1)}, u32[]{:S(2)}, u32[]{:S(2)}) collective-permute-start(bf16[2,4,2,2,32,576]{5,4,3,2,1,0:T(8,128)(2,1)S(1)} %get-tuple-element.76), channel_id=1, source_target_pairs={{0,3},{1,2},{2,1},{3,0},{4,7},{5,6},{6,5},{7,4},{8,9},{9,8},{10,11... | collective-permute-start | bytes 3538952 | tf_op jit(solution)/shard_map/ppermute | solution.py:29
  56.6 25.3 %collective-permute-start.17 = (bf16[2,2,2,2,2,16,576]{6,5,4,3,2,1,0:T(8,128)(2,1)}, bf16[2,2,2,2,2,16,576]{6,5,4,3,2,1,0:T(8,128)(2,1)}, u32[]{:S(2)}, u32[]{:S(2)}) collective-permute-start(bf16[2,2,2,2,2,16,576]{6,5,4,3,2,1,0:T(8,128)(2,1)} %get-tuple-element.68), channel_id=1, source_target_pairs={{0,3},{1,2},{2,1},{3,0},{4,7},{5,6},{6,5},{7,4},{8,9},{9,8},{10,11... | collective-permute-start | bytes 1769480 | tf_op jit(solution)/shard_map/ppermute | solution.py:29
  58.8 26.5 %collective-permute-start.19 = (bf16[2,2,2,2,2,16,576]{6,5,4,3,2,1,0:T(8,128)(2,1)}, bf16[2,2,2,2,2,16,576]{6,5,4,3,2,1,0:T(8,128)(2,1)}, u32[]{:S(2)}, u32[]{:S(2)}) collective-permute-start(bf16[2,2,2,2,2,16,576]{6,5,4,3,2,1,0:T(8,128)(2,1)} %get-tuple-element.70), channel_id=1, source_target_pairs={{0,48},{1,49},{2,50},{3,51},{4,52},{5,53},{6,54},{7,55},{8,24},{9,... | collective-permute-start | bytes 1769480 | tf_op jit(solution)/shard_map/ppermute | solution.py:29
  71.5 18.0 %collective-permute-start.26 = (bf16[1,4,2,2,32,576]{5,4,3,2,1,0:T(8,128)(2,1)}, bf16[1,4,2,2,32,576]{5,4,3,2,1,0:T(8,128)(2,1)}, u32[]{:S(2)}, u32[]{:S(2)}) collective-permute-start(bf16[1,4,2,2,32,576]{5,4,3,2,1,0:T(8,128)(2,1)} %get-tuple-element.78), channel_id=1, source_target_pairs={{0,1},{1,0},{2,3},{3,2},{4,5},{5,4},{6,7},{7,6},{8,11},{9,10},{10,... | collective-permute-start | bytes 1769480 | tf_op jit(solution)/shard_map/ppermute | solution.py:29
  72.9 23.4 %all-to-all-start = ((f32[128,8,128]{2,1,0:T(8,128)}), f32[128,8,128]{2,1,0:T(8,128)S(1)}, u32[]{:S(2)}, u32[]{:S(2)}) async-start(f32[128,8,128]{2,1,0:T(8,128)} %pack.1), calls=%async_computation | async-start | bytes 1048576 | tf_op jit(solution)/shard_map/all_to_all | solution.py:367
  83.3 9.9 %collective-permute-start.18 = (bf16[1,2,2,2,2,16,576]{6,5,4,3,2,1,0:T(8,128)(2,1)S(1)}, bf16[1,2,2,2,2,16,576]{6,5,4,3,2,1,0:T(8,128)(2,1)S(1)}, u32[]{:S(2)}, u32[]{:S(2)}) collective-permute-start(bf16[1,2,2,2,2,16,576]{6,5,4,3,2,1,0:T(8,128)(2,1)S(1)} %get-tuple-element.82), channel_id=1, source_target_pairs={{0,48},{1,49},{2,50},{3,51},{4,52},{5,53},{6,54},{7,55},{8,24},{9,... | collective-permute-start | bytes 884744 | tf_op jit(solution)/shard_map/ppermute | solution.py:29
  86.6 8.6 %collective-permute-start.20 = (bf16[1,2,2,2,2,16,576]{6,5,4,3,2,1,0:T(8,128)(2,1)S(1)}, bf16[1,2,2,2,2,16,576]{6,5,4,3,2,1,0:T(8,128)(2,1)S(1)}, u32[]{:S(2)}, u32[]{:S(2)}) collective-permute-start(bf16[1,2,2,2,2,16,576]{6,5,4,3,2,1,0:T(8,128)(2,1)S(1)} %get-tuple-element.84), channel_id=1, source_target_pairs={{0,3},{1,2},{2,1},{3,0},{4,7},{5,6},{6,5},{7,4},{8,9},{9,8},{10,11... | collective-permute-start | bytes 884744 | tf_op jit(solution)/shard_map/ppermute | solution.py:29
  91.6 8.6 %collective-permute-start.27 = (bf16[2,2,2,32,576]{4,3,2,1,0:T(8,128)(2,1)}, bf16[2,2,2,32,576]{4,3,2,1,0:T(8,128)(2,1)}, u32[]{:S(2)}, u32[]{:S(2)}) collective-permute-start(bf16[2,2,2,32,576]{4,3,2,1,0:T(8,128)(2,1)} %get-tuple-element.80), channel_id=1, source_target_pairs={{0,48},{1,49},{2,50},{3,51},{4,52},{5,53},{6,54},{7,55},{8,24},{9,... | collective-permute-start | bytes 884744 | tf_op jit(solution)/shard_map/ppermute | solution.py:29
  96.1 7.4 %collective-permute-start.21 = (bf16[2,2,2,32,576]{4,3,2,1,0:T(8,128)(2,1)}, bf16[2,2,2,32,576]{4,3,2,1,0:T(8,128)(2,1)}, u32[]{:S(2)}, u32[]{:S(2)}) collective-permute-start(bf16[2,2,2,32,576]{4,3,2,1,0:T(8,128)(2,1)} %pad_maximum_fusion), channel_id=1, source_target_pairs={{0,1},{1,0},{2,3},{3,2},{4,5},{5,4},{6,7},{7,6},{8,11},{9,10},{10,... | collective-permute-start | bytes 884744 | tf_op jit(solution)/shard_map/ppermute | solution.py:29
  101.1 5.4 %collective-permute-start.28 = (bf16[2,2,32,576]{3,2,1,0:T(8,128)(2,1)S(1)}, bf16[2,2,32,576]{3,2,1,0:T(8,128)(2,1)S(1)}, u32[]{:S(2)}, u32[]{:S(2)}) collective-permute-start(bf16[2,2,32,576]{3,2,1,0:T(8,128)(2,1)S(1)} %fusion.12), channel_id=1, source_target_pairs={{0,16},{1,17},{2,18},{3,19},{4,20},{5,21},{6,22},{7,23},{8,56},{9,... | collective-permute-start | bytes 442376 | tf_op jit(solution)/shard_map/ppermute | solution.py:29
  104.6 5.4 %collective-permute-start.22 = (bf16[2,2,32,576]{3,2,1,0:T(8,128)(2,1)S(1)}, bf16[2,2,32,576]{3,2,1,0:T(8,128)(2,1)S(1)}, u32[]{:S(2)}, u32[]{:S(2)}) collective-permute-start(bf16[2,2,32,576]{3,2,1,0:T(8,128)(2,1)S(1)} %fusion.10), channel_id=1, source_target_pairs={{0,16},{1,17},{2,18},{3,19},{4,20},{5,21},{6,22},{7,23},{8,56},{9,... | collective-permute-start | bytes 442376 | tf_op jit(solution)/shard_map/ppermute | solution.py:29
  111.0 12.1 %collective-permute-start.29 = (bf16[2,64,576]{2,1,0:T(8,128)(2,1)S(1)}, bf16[2,64,576]{2,1,0:T(8,128)(2,1)S(1)}, u32[]{:S(2)}, u32[]{:S(2)}) collective-permute-start(bf16[2,64,576]{2,1,0:T(8,128)(2,1)S(1)} %fusion.14), channel_id=1, source_target_pairs={{0,68},{1,69},{2,70},{3,71},{4,64},{5,65},{6,66},{7,67},{8,76},{9,... | collective-permute-start | bytes 442376 | tf_op jit(solution)/shard_map/ppermute | solution.py:29
  123.1 4.5 %collective-permute-start.30 = (bf16[64,576]{1,0:T(8,128)(2,1)S(1)}, bf16[64,576]{1,0:T(8,128)(2,1)S(1)}, u32[]{:S(2)}, u32[]{:S(2)}) collective-permute-start(bf16[64,576]{1,0:T(8,128)(2,1)S(1)} %get-tuple-element.89), channel_id=1, source_target_pairs={{0,4},{1,5},{2,6},{3,7},{4,0},{5,1},{6,2},{7,3},{8,12},{9,13},{10,... | collective-permute-start | bytes 221192 | tf_op jit(solution)/shard_map/ppermute | solution.py:29
  (15 other events, 137.1 us)
where the time goes:
time: 129 us; the launch traced here: 128 us
  starting transfers between devices  42.9 us (33%)
  waiting for transfers between devices  32.2 us (25%)
  Pallas kernels  31.5 us (24%)
  other arithmetic  12 us (9%)
  local copies, waits for them, and re-layouts  8.74 us (7%)
    ppermute x31, starting transfers between devices, send(): return lax.ppermute(array, AXES, partner)  34.1 us
    ppermute x31, waiting for transfers between devices, send(): return lax.ppermute(array, AXES, partner)  32.2 us
    all_to_all x1, starting transfers between devices, local(): lax.all_to_all(run_pack(me, total0, total1, target0, target1), AXES, 0, 0...  8.88 us
    pallas_call x1, Pallas kernels, run_head_gradient(): call(head_gradient, 'vvv', [('h', (D, WIDTH), bf16)], scratch=[pltpu.VMEM...  8.6 us
    convert_element_type x9, other arithmetic, add(): return (a.astype(f32) + b.astype(f32)).astype(bf16)  8.42 us
    unnamed x30, local copies, waits for them, and re-layouts  8.11 us
    pallas_call x2, Pallas kernels, run_back(): return call(back, 'svv', [BLOCKS, BLOCKS], **BACK_COST)(me, rows, head)  6.13 us
    pallas_call x2, Pallas kernels, run_pick(): call(kernel, 'svv', [BLOCKS, BLOCKS], scratch=[pltpu.VMEM((256, WIDTH), b...  5.96 us
  transfers between devices with their start and end apart: 32, of which 13 were waited for; matrix products, arithmetic and copies ran while one was open for 9% of the time, Pallas kernels for 24%

commit v1 on v0

v1 whole, which is shorter than its diff:
```python
import jax
import jax.numpy as jnp
from jax import lax
from jax.experimental import pallas as pl
from jax.experimental.pallas import tpu as pltpu
from jax.sharding import PartitionSpec as P

softcap = 30.0
AXES = ("dp", "vocab")
bf16 = jnp.bfloat16
f32 = jnp.float32
D = 4608
WIDTH = 1024
FEATURES = 576
COLUMN = (512, 128)


def flips(core0, core1):
    return [(i, i ^ (core1 if i & 8 else core0)) for i in range(128)]


CORE = flips(8, 8)
X1, X2 = flips(16, 48), flips(48, 16)
Y1, Y2 = flips(1, 3), flips(3, 1)
X3, Y3 = flips(32, 32), flips(2, 2)
ZL, Z2, ZH = flips(4, 4), flips(64, 64), flips(68, 68)


def send(array, partner):
    return lax.ppermute(array, AXES, partner)


def slot_flip(slot, core):
    return (0, 1 + 2 * core, 3 - 2 * core, 2)[slot]


def whole_block(me, i):
    core = ((me >> 3) & 1) ^ ((i >> 2) & 1)
    x = ((me >> 4) & 3) ^ slot_flip(i & 3, core)
    return ((me >> 6) ^ (i >> 3)) * 8 + x * 2 + core


def feature_slot(me, i, other):
    core = ((me >> 3) & 1) ^ other
    apart = (me & 3) ^ (i & 3)
    slot = jnp.where(apart == 1 + 2 * core, 1, jnp.where(apart == 3 - 2 * core, 2, jnp.where(apart == 2, 3, 0)))
    return (((me >> 2) & 1) ^ (i >> 2)) * 4 + slot


def call(kernel, ins, outs, scratch=(), flops=0, moved=0, mib=16, aliases={}):
    places = {"v": pltpu.VMEM, "s": pltpu.SMEM, "h": pl.ANY}
    return pl.pallas_call(
        kernel,
        in_specs=[pl.BlockSpec(memory_space=places[i]) for i in ins],
        out_specs=[pl.BlockSpec(memory_space=places[o[0]]) for o in outs],
        out_shape=[jax.ShapeDtypeStruct(o[1], o[2]) for o in outs],
        scratch_shapes=list(scratch),
        input_output_aliases=aliases,
        compiler_params=pltpu.CompilerParams(vmem_limit_bytes=mib << 20),
        cost_estimate=pl.CostEstimate(flops=flops, bytes_accessed=moved, transcendentals=0),
        name=kernel.__name__,
    )


def rows_of(i):
    return slice(32 * i, 32 * i + 32)


def from_lanes(row):
    return jnp.broadcast_to(row, (128, 128)).T


def local_block(me, i, whole):
    return whole[pl.ds(pl.multiple_of(whole_block(me, i) * 32, 32), 32), :]


def hits_of(me, ids, j):
    lane = lax.broadcasted_iota(jnp.int32, (ids.shape[0], 128), 1)
    return ids == (lane + (me * WIDTH + 128 * j)).astype(f32)


def forward(half, me_ref, *refs):
    pieces, (ids_ref, head_ref, rows, capped_ref, term_ref, total_ref, target_ref) = refs[:8], refs[8:]
    me = me_ref[0]
    for i in range(8):
        rows[rows_of(i), :] = pieces[i][...]
    ids = ids_ref[256 * half : 256 * half + 256, :]
    total = jnp.zeros((256, 128), f32)
    target = jnp.zeros((256, 128), f32)
    for n in range(4):
        raw = jnp.dot(rows[...], head_ref[:, 256 * n : 256 * n + 256], preferred_element_type=f32)
        ratio = jnp.tanh(raw / softcap)
        for j in range(2):
            start = 256 * n + 128 * j
            part = ratio[:, 128 * j : 128 * j + 128]
            capped = softcap * part
            expo = jnp.exp(capped)
            hit = hits_of(me, ids, 2 * n + j)
            capped_ref[:, start : start + 128] = capped
            term_ref[:, start : start + 128] = jnp.where(hit, 0.0, expo * (1.0 - part * part)).astype(bf16)
            total = total + expo
            target = target + jnp.where(hit, capped, 0.0)
    total_ref[...] = total
    target_ref[...] = target


def forward_low(*refs):
    forward(0, *refs)


def forward_high(*refs):
    forward(1, *refs)


def run_forward(kernel, me, pieces, ids, head):
    return call(
        kernel,
        "s" + "v" * 10,
        [
            ("v", (256, D), bf16),
            ("v", (256, WIDTH), f32),
            ("v", (256, WIDTH), bf16),
            ("v", (256, 128), f32),
            ("v", (256, 128), f32),
        ],
        flops=2 * 256 * D * WIDTH,
        moved=2 * D * WIDTH,
    )(me, *pieces, ids, head)


def pack(me_ref, total0, total1, target0, target1, out_ref, whole):
    me = me_ref[0]
    sums = []
    for halves in ((total0, total1), (target0, target1)):
        for i in range(16):
            spot = pl.ds(pl.multiple_of(whole_block(me, i) * 32, 32), 32)
            whole[spot, :] = halves[i // 8][rows_of(i % 8), :]
        for j in range(4):
            sums.append(jnp.sum(whole[128 * j : 128 * j + 128, :].T, axis=0, keepdims=True))
    out_ref[...] = jnp.concatenate(sums, axis=0)


def run_pack(me, *columns):
    return call(pack, "svvvv", [("v", (8, 128), f32)], scratch=[pltpu.VMEM(COLUMN, f32)], moved=1 << 20)(
        me, *columns
    )[0]


def unpack(me_ref, sums_ref, weight_ref, log_ref, own_ref, rest_ref, pick_ref, logs, targets):
    me = me_ref[0]
    sums = sums_ref[...]
    for j in range(4):
        logs[128 * j : 128 * j + 128, :] = from_lanes(jnp.log(sums[j : j + 1, :]))
        targets[128 * j : 128 * j + 128, :] = from_lanes(sums[4 + j : 5 + j, :])
    for i in range(16):
        log_ref[rows_of(i), :] = local_block(me, i, logs)
    own_ref[...] = local_block(me, 0, targets) - local_block(me, 0, logs)
    for zr in range(2):
        for x in range(4):
            i = 8 * zr + x
            log_total = log_ref[rows_of(i), :]
            target = local_block(me, i, targets)
            weight = weight_ref[rows_of(i), :]
            ratio = target / softcap
            rest_ref[rows_of(4 * zr + x), :] = weight * jnp.exp(-log_total)
            pick_ref[rows_of(4 * zr + x), :] = weight * (jnp.exp(target - log_total) - 1.0) * (1.0 - ratio * ratio)


def run_unpack(me, sums, weight):
    outs = [("v", COLUMN, f32), ("v", (32, 128), f32), ("v", (256, 128), f32), ("v", (256, 128), f32)]
    return call(unpack, "svv", outs, scratch=[pltpu.VMEM(COLUMN, f32)] * 2, moved=1 << 20)(me, sums, weight)


def back_part(me, n, rows, head_ref, mine_ref, mate_ref):
    out = lax.dot_general(
        rows, head_ref[1152 * n : 1152 * n + 1152, :], (((1,), (1,)), ((), ())), preferred_element_type=f32
    ).astype(bf16)
    for i in range(2):
        part = out[:, FEATURES * i : FEATURES * i + FEATURES]
        mine_ref[feature_slot(me, 2 * n + i, 0)] = part[:128].reshape(4, 32, FEATURES)
        mate_ref[feature_slot(me, 2 * n + i, 1)] = part[128:].reshape(4, 32, FEATURES)


def back(me_ref, rows_ref, head_ref, mine_ref, mate_ref):
    for n in range(4):
        back_part(me_ref[0], n, rows_ref[...], head_ref, mine_ref, mate_ref)


BLOCKS = ("v", (8, 4, 32, FEATURES), bf16)
BACK_COST = dict(flops=2 * 256 * D * WIDTH, moved=2 * D * WIDTH)


def run_back(me, rows, head):
    return call(back, "svv", [BLOCKS, BLOCKS], **BACK_COST)(me, rows, head)


def begin(me_ref, ids_ref, weight_ref, head_ref, mine0, mate0, mine1, mate1, held_ref, ids_out, weight_out, *scratch):
    ids_near, weight_near, ids_whole, weight_whole, rows, sems = scratch
    me = me_ref[0]
    small = [
        pltpu.make_async_copy(ids_ref, ids_near, sems.at[4]),
        pltpu.make_async_copy(weight_ref, weight_near, sems.at[5]),
    ]
    loads = []
    for n in range(4):
        spot = pl.ds(1152 * n, 1152)
        loads.append(pltpu.make_async_copy(head_ref.at[spot], held_ref.at[spot], sems.at[n]))
    for copy in small + loads:
        copy.start()
    for copy in small:
        copy.wait()
    for j in range(4):
        ids_whole[128 * j : 128 * j + 128, :] = from_lanes(ids_near[j : j + 1, :].astype(f32))
        weight_whole[128 * j : 128 * j + 128, :] = from_lanes(weight_near[j : j + 1, :])
    for i in range(16):
        ids_out[rows_of(i), :] = local_block(me, i, ids_whole)
        weight_out[rows_of(i), :] = local_block(me, i, weight_whole)
    ids = ids_out[...]
    for j in range(WIDTH // 128):
        rows[:, 128 * j : 128 * j + 128] = jnp.where(hits_of(me, ids, j), 1.0, 0.0).astype(bf16)
    for n in range(4):
        loads[n].wait()
        for half, (mine, mate) in enumerate(((mine0, mate0), (mine1, mate1))):
            back_part(me, n, rows[256 * half : 256 * half + 256, :], held_ref, mine, mate)


def run_begin(me, ids, weight, head):
    column = ("v", COLUMN, f32)
    return call(
        begin,
        "shhh",
        [BLOCKS] * 4 + [("v", (D, WIDTH), bf16), column, column],
        scratch=[
            pltpu.VMEM((4, 128), jnp.int32),
            pltpu.VMEM((4, 128), f32),
            pltpu.VMEM(COLUMN, f32),
            pltpu.VMEM(COLUMN, f32),
            pltpu.VMEM((512, WIDTH), bf16),
            pltpu.SemaphoreType.DMA((6,)),
        ],
        flops=4 * 256 * D * WIDTH,
        moved=2 * D * WIDTH,
    )(me, *(pltpu.with_memory_space_constraint(array, pltpu.HBM) for array in (ids, weight, head)))


def fold(*refs):
    parts, (p_keep, p_send, q_keep, q_send) = refs[:4], refs[4:]
    for zr in range(2):
        mine, got = parts[2 * zr : 2 * zr + 2]
        for zl in range(2):
            for k in range(4):
                for x in range(4):
                    total = mine[4 * zl + k, x] + got[4 * zl + k, x]
                    (p_keep if k < 2 else p_send)[x // 2, k % 2, x % 2, zr, zl] = total[:16]
                    (q_keep if x < 2 else q_send)[k // 2, k % 2, x % 2, zr, zl] = total[16:]


def run_fold(*parts):
    return call(fold, "vvvv", [("v", (2, 2, 2, 2, 2, 16, FEATURES), bf16)] * 4, moved=512 * D * 4)(*parts)


def combine(first_row, slots, rest_ref, pick_ref, a_ref, a_got, g_ref, g_got, keep, out):
    for h in range(2):
        for i in range(2):
            for j in range(2):
                x = slots(h, j)
                for zr in range(2):
                    start_row = 128 * zr + 32 * x + first_row
                    rest = rest_ref[start_row : start_row + 16, :]
                    pick = pick_ref[start_row : start_row + 16, :]
                    for zl in range(2):
                        for start in range(0, FEATURES, 128):
                            wide = min(128, FEATURES - start)
                            at = (h, i, j, zr, zl, slice(None), slice(start, start + wide))
                            terms = (a_ref[at] + a_got[at]).astype(f32)
                            columns = (g_ref[at] + g_got[at]).astype(f32)
                            total = rest[:, :wide] * terms + pick[:, :wide] * columns
                            (out if h else keep)[at[1:]] = total.astype(bf16)


def combine_p(*refs):
    combine(0, lambda h, j: 2 * h + j, *refs)


def combine_q(*refs):
    combine(16, lambda h, j: j, *refs)


def run_combine(kernel, rest, pick, *parts):
    half = ("v", (2, 2, 2, 2, 16, FEATURES), bf16)
    return call(kernel, "v" * 6, [half, half], moved=1 << 22)(rest, pick, *parts)


def finish(*refs):
    terms, out_ref = refs[:4], refs[4]
    out_ref[...] = sum(term[...].astype(f32) for term in terms).astype(bf16)


def run_finish(*terms):
    return call(finish, "v" * 4, [("v", (32, FEATURES), bf16)], moved=1 << 17)(*terms)[0]


def dlogits(me_ref, low_ref, high_ref, log_ref, weight_ref, ids_ref, out_ref):
    me = me_ref[0]
    for n in range(4):
        capped_ref = low_ref if n < 2 else high_ref
        rows = slice(128 * (n % 2), 128 * (n % 2) + 128)
        out_rows = slice(128 * n, 128 * n + 128)
        log_total = log_ref[out_rows, :]
        weight = weight_ref[out_rows, :]
        ids = ids_ref[out_rows, :]
        for j in range(WIDTH // 128):
            spot = slice(128 * j, 128 * j + 128)
            capped = capped_ref[rows, spot]
            prob = jnp.exp(capped - log_total)
            onehot = jnp.where(hits_of(me, ids, j), 1.0, 0.0)
            ratio = capped / softcap
            out_ref[out_rows, spot] = (weight * (prob - onehot) * (1.0 - ratio * ratio)).astype(bf16)


def run_dlogits(me, low, high, log_total, weight, ids):
    return call(
        dlogits, "svvvvv", [("v", (512, WIDTH), bf16)], flops=512 * WIDTH * 16, moved=6 * 512 * WIDTH
    )(me, low, high, log_total, weight, ids)[0]


def head_rows(first, last, low_ref, high_ref, dlog_ref, out_ref, rows, buffer, sems):
    def copy(i):
        return pltpu.make_async_copy(buffer.at[i % 2], out_ref.at[pl.ds(512 * i, 512)], sems.at[i % 2])

    for i in range(first, last):
        spot = slice(512 * i, 512 * i + 512)
        rows[:256, :] = low_ref[:, spot]
        rows[256:, :] = high_ref[:, spot]
        if i >= first + 2:
            copy(i - 2).wait()
        buffer[i % 2] = lax.dot_general(
            rows[...], dlog_ref[...], (((0,), (0,)), ((), ())), preferred_element_type=f32
        ).astype(bf16)
        copy(i).start()
    copy(last - 2).wait()
    copy(last - 1).wait()


def head_gradient_low(low_ref, high_ref, dlog_ref, out_ref, *scratch):
    head_rows(0, 5, low_ref, high_ref, dlog_ref, out_ref, *scratch)


def head_gradient_high(low_ref, high_ref, dlog_ref, started_ref, out_ref, *scratch):
    head_rows(5, 9, low_ref, high_ref, dlog_ref, out_ref, *scratch)


def run_head_gradient(kernel, low, high, dlog, started=()):
    return call(
        kernel,
        "vvv" + "h" * len(started),
        [("h", (D, WIDTH), bf16)],
        scratch=[
            pltpu.VMEM((512, 512), bf16),
            pltpu.VMEM((2, 512, WIDTH), bf16),
            pltpu.SemaphoreType.DMA((2,)),
        ],
        flops=512 * WIDTH * D,
        moved=D * WIDTH,
        aliases={3: 0} if started else {},
    )(low, high, dlog, *started)[0]


def tie(*arrays):
    return lax.optimization_barrier(arrays)


def halve(keep_ref, got_ref, keep, out):
    n = keep.shape[0]
    keep[...] = keep_ref[:n] + got_ref[:n]
    out[...] = keep_ref[n:] + got_ref[n:]


def run_halve(held, got):
    n = held.shape[0] // 2
    half = ("v", (n,) + held.shape[1:], bf16)
    return call(halve, "vv", [half, half], moved=held.size * 6)(held, got)


def join(p_keep, p_got, q_keep, q_got, keep, out):
    for k, target in enumerate((keep, out)):
        target[:, :, :, :16] = p_keep[k] + p_got[k]
        target[:, :, :, 16:] = q_keep[k] + q_got[k]


def run_join(*parts):
    half = ("v", (2, 2, 2, 32, FEATURES), bf16)
    return call(join, "v" * 4, [half, half], moved=1 << 22)(*parts)


def split(keep, got, *outs):
    for z, out in enumerate(outs):
        out[...] = keep[0, z // 2, z % 2] + got[0, z // 2, z % 2]


def run_split(*parts):
    return call(split, "vv", [("v", (32, FEATURES), bf16)] * 4, moved=1 << 20)(*parts)


def local(hidden, head, verdict_ids, row_weight):
    me = (lax.axis_index("dp") * 8 + lax.axis_index("vocab")).astype(jnp.int32).reshape(1)
    a1, a2, a3 = send(hidden, X1), send(hidden, X2), send(hidden, X3)
    o0 = send(hidden, ZH)
    g0_mine, g0_mate, g1_mine, g1_mate, head, ids, weight = run_begin(
        me, verdict_ids.reshape(4, 128), row_weight.reshape(4, 128), head
    )
    a1, a2, a3, o0, g0_mine, g0_mate, g1_mine, g1_mate = tie(a1, a2, a3, o0, g0_mine, g0_mate, g1_mine, g1_mate)
    o1, o2, o3 = send(o0, X1), send(o0, X2), send(a3, ZH)
    g0_got, g1_got = send(g0_mate, CORE), send(g1_mate, CORE)
    gp_keep, gp_send, gq_keep, gq_send = run_fold(g0_mine, g0_got, g1_mine, g1_got)
    o1, gp_send, gq_send, a1 = tie(o1, gp_send, gq_send, a1)
    gp_got, gq_got = send(gp_send, Y2), send(gq_send, X2)
    own_half = [hidden, a1, a2, a3]
    own_half += [send(piece, CORE) for piece in own_half]
    rows0, capped0, term0, total0, target0 = run_forward(forward_low, me, own_half, ids, head)
    a0_mine, a0_mate = run_back(me, term0, head)
    o1, o2, o3, gp_got, gq_got, a0_mate = tie(o1, o2, o3, gp_got, gq_got, a0_mate)
    other_half = [o0, o1, o2, o3]
    other_half += [send(piece, CORE) for piece in other_half]
    rows1, capped1, term1, total1, target1 = run_forward(forward_high, me, other_half, ids, head)

    def step(sums, *partners):
        got = tie(*(send(sums, partner) for partner in partners))
        return sums + sum(got)

    sums = step(run_pack(me, total0, total1, target0, target1), X1)
    a1_mine, a1_mate = run_back(me, term1, head)
    sums, a1_mate = tie(sums, a1_mate)
    a1_got = send(a1_mate, CORE)
    sums = step(sums, X2)
    sums, a1_got = tie(sums, a1_got)
    p_keep, p_send, q_keep, q_send = run_fold(a0_mine, send(a0_mate, CORE), a1_mine, a1_got)

    p_got, q_got = send(p_send, Y2), send(q_send, X2)
    sums = step(step(step(sums, CORE), ZL, Z2, ZH), Y1, Y2, Y3)
    sums, p_got, q_got = tie(sums, p_got, q_got)
    log_total, own, rest, pick = run_unpack(me, sums, weight)
    p_keep, p_send = run_combine(combine_p, rest, pick, p_keep, p_got, gp_keep, gp_got)
    q_keep, q_send = run_combine(combine_q, rest, pick, q_keep, q_got, gq_keep, gq_got)
    p_got, q_got = send(p_send, X2), send(q_send, Y2)
    log_total, p_keep = tie(log_total, p_keep)
    dlog = run_dlogits(me, capped0, capped1, log_total, weight, ids)
    head_grad = run_head_gradient(head_gradient_low, rows0, rows1, dlog)
    p_got, q_got, head_grad = tie(p_got, q_got, head_grad)
    keep, out = run_join(p_keep, p_got, q_keep, q_got)
    got = send(out, Y1)
    head_grad = run_head_gradient(head_gradient_high, rows0, rows1, dlog, (head_grad,))
    got, head_grad = tie(got, head_grad)
    keep, out = run_halve(keep, got)
    keep, *outs = run_split(keep, send(out, X1))
    z_got = tie(*(send(out, partner) for out, partner in zip(outs, (ZL, Z2, ZH))))
    hidden_grad = run_finish(keep, *z_got)
    return (own[:, 0], head_grad, hidden_grad)


def solution(mesh):
    in_specs = (P("dp", None), P(None, ("dp", "vocab")), P(), P())
    out_specs = (P("dp"), P(None, ("dp", "vocab")), P("dp", "vocab"))
    return jax.shard_map(local, mesh=mesh, in_specs=in_specs, out_specs=out_specs, check_vma=False)
```

time: 129 us -> 114 us (0.88)
  other arithmetic: 12 us -> 0.02 us
  local copies, waits for them, and re-layouts: 8.74 us -> 0.63 us
  starting transfers between devices: 42.9 us -> 44.8 us
  Pallas kernels: 31.5 us -> 33.3 us
  waiting for transfers between devices: 32.2 us -> 33.9 us
    ppermute x31 -> x39, starting transfers between devices: 34.1 us -> 44.8 us  [send(): return lax.ppermute(array, AXES, partner)]
    all_to_all x1 -> x0, starting transfers between devices: 8.88 us -> none  [local(): lax.all_to_all(run_pack(me, total0, total1, target0, target1), AXES, 0, 0...]
    convert_element_type x9 -> x0, other arithmetic: 8.42 us -> none  [add(): return (a.astype(f32) + b.astype(f32)).astype(bf16)]
    unnamed x30 -> x2, local copies, waits for them, and re-layouts: 8.11 us -> 0.01 us
    pallas_call x8 -> x11, Pallas kernels: 17.2 us -> 19.8 us  [the longest x2 9.38 us: run_head_gradient(): call(kernel, 'vvv' + 'h' * len(started), [('h', (D, WIDTH), bf16)], scrat...]
    squeeze x3 -> x0, other arithmetic: 2.09 us -> none  [the longest x1 1.11 us: local(): both = add(both_keep[0], send(both_send[0], X1))]
    ppermute x31 -> x39, waiting for transfers between devices: 32.2 us -> 33.9 us  [send(): return lax.ppermute(array, AXES, partner)]
  transfers between devices with their start and end apart: 32 -> 39, of which waited for: 13 -> 20; matrix products, arithmetic and copies ran while one was open for 9% -> 1% of each run, Pallas kernels for 24% -> 25%
where the time goes in v1:
time: 114 us; the launch traced here: 113 us
  starting transfers between devices  44.8 us (39%)
  waiting for transfers between devices  33.9 us (30%)
  Pallas kernels  33.3 us (29%)
    ppermute x39, starting transfers between devices, send(): return lax.ppermute(array, AXES, partner)  44.8 us
    ppermute x39, waiting for transfers between devices, send(): return lax.ppermute(array, AXES, partner)  33.9 us
    pallas_call x2, Pallas kernels, run_head_gradient(): call(kernel, 'vvv' + 'h' * len(started), [('h', (D, WIDTH), bf16)], scrat...  9.38 us
    pallas_call x1, Pallas kernels, run_begin(): call(begin, 'shhh', [BLOCKS] * 4 + [('v', (D, WIDTH), bf16), column, colu...  8.37 us
    pallas_call x2, Pallas kernels, run_back(): return call(back, 'svv', [BLOCKS, BLOCKS], **BACK_COST)(me, rows, head)  6.03 us
    pallas_call x2, Pallas kernels, run_forward(): call(kernel, 's' + 'v' * 10, [('v', (256, D), bf16), ('v', (256, WIDTH),...  5.99 us
  transfers between devices with their start and end apart: 39, of which 20 were waited for; matrix products, arithmetic and copies ran while one was open for 1% of the time, Pallas kernels for 25%

profile of v1, /device:TPU:0, one launch (start us, length us, event | category | flops | bytes accessed | tf_op | source)
XLA Modules:
  0.0 113.4 jit_solution(14386575141822068710)
XLA Ops:
  0.6 1.7 %collective-permute-start = (bf16[32,4608]{1,0:T(8,128)(2,1)}, bf16[32,4608]{1,0:T(8,128)(2,1)S(1)}, u32[]{:S(2)}, u32[]{:S(2)}) collective-permute-start(bf16[32,4608]{1,0:T(8,128)(2,1)} %refs_1_.1), channel_id=1, source_target_pairs={{0,16},{1,17},{2,18},{3,19},{4,20},{5,21},{6,22},{7,23},{8,56},{9,... | collective-permute-start | bytes 884744 | tf_op jit(solution)/shard_map/ppermute | solution.py:30
  2.3 2.1 %collective-permute-start.1 = (bf16[32,4608]{1,0:T(8,128)(2,1)}, bf16[32,4608]{1,0:T(8,128)(2,1)S(1)}, u32[]{:S(2)}, u32[]{:S(2)}) collective-permute-start(bf16[32,4608]{1,0:T(8,128)(2,1)} %refs_1_.1), channel_id=1, source_target_pairs={{0,48},{1,49},{2,50},{3,51},{4,52},{5,53},{6,54},{7,55},{8,24},{9,... | collective-permute-start | bytes 884744 | tf_op jit(solution)/shard_map/ppermute | solution.py:30
  5.0 4.0 %collective-permute-start.3 = (bf16[32,4608]{1,0:T(8,128)(2,1)}, bf16[32,4608]{1,0:T(8,128)(2,1)S(1)}, u32[]{:S(2)}, u32[]{:S(2)}) collective-permute-start(bf16[32,4608]{1,0:T(8,128)(2,1)} %refs_1_.1), channel_id=1, source_target_pairs={{0,68},{1,69},{2,70},{3,71},{4,64},{5,65},{6,66},{7,67},{8,76},{9,... | collective-permute-start | bytes 884744 | tf_op jit(solution)/shard_map/ppermute | solution.py:30
  9.1 8.4 %begin.1 = (bf16[8,4,32,576]{3,2,1,0:T(8,128)(2,1)S(1)}, bf16[8,4,32,576]{3,2,1,0:T(8,128)(2,1)S(1)}, bf16[8,4,32,576]{3,2,1,0:T(8,128)(2,1)S(1)}, bf16[8,4,32,5...) custom-call(s32[1]{0:T(128)} %bitcast.me_ref.refs_0_, ...), custom_call_target="tpu_custom_call" | custom-call | flops 4831838208 | bytes 9437184 | tf_op jit(solution)/shard_map/begin/pallas_call | solution.py:229
  21.5 1.7 %collective-permute-done.6.refs_3_ = bf16[8,4,32,576]{3,2,1,0:T(8,128)(2,1)S(1)} collective-permute-done((bf16[8,4,32,576]{3,2,1,0:T(8,128)(2,1)S(1)}, bf16[8,4,32,576]{3,2,1,0:T(8,128)(2,1)S(1)}, u32[]{:S(2)}, u32[]{:S(2)}) %collective-permute-start.6) | collective-permute-done | bytes 1179680 | tf_op jit(solution)/shard_map/ppermute | solution.py:30
  23.6 2.0 %collective-permute-done.4.refs_2_ = bf16[32,4608]{1,0:T(8,128)(2,1)S(1)} collective-permute-done((bf16[32,4608]{1,0:T(8,128)(2,1)S(1)}, bf16[32,4608]{1,0:T(8,128)(2,1)S(1)}, u32[]{:S(2)}, u32[]{:S(2)}) %collective-permute-start.4) | collective-permute-done | bytes 294944 | tf_op jit(solution)/shard_map/ppermute | solution.py:30
  25.7 3.1 %collective-permute-start.13 = (bf16[2,2,2,2,2,16,576]{6,5,4,3,2,1,0:T(8,128)(2,1)S(1)}, bf16[2,2,2,2,2,16,576]{6,5,4,3,2,1,0:T(8,128)(2,1)S(1)}, u32[]{:S(2)}, u32[]{:S(2)}) collective-permute-start(bf16[2,2,2,2,2,16,576]{6,5,4,3,2,1,0:T(8,128)(2,1)S(1)} %get-tuple-element.108), channel_id=1, source_target_pairs={{0,3},{1,2},{2,1},{3,0},{4,7},{5,6},{6,5},{7,4},{8,9},{9,8},{10,11... | collective-permute-start | bytes 1769480 | tf_op jit(solution)/shard_map/ppermute | solution.py:30
  28.8 1.8 %collective-permute-start.14 = (bf16[2,2,2,2,2,16,576]{6,5,4,3,2,1,0:T(8,128)(2,1)S(1)}, bf16[2,2,2,2,2,16,576]{6,5,4,3,2,1,0:T(8,128)(2,1)S(1)}, u32[]{:S(2)}, u32[]{:S(2)}) collective-permute-start(bf16[2,2,2,2,2,16,576]{6,5,4,3,2,1,0:T(8,128)(2,1)S(1)} %get-tuple-element.109), channel_id=1, source_target_pairs={{0,48},{1,49},{2,50},{3,51},{4,52},{5,53},{6,54},{7,55},{8,24},{9,... | collective-permute-start | bytes 1769480 | tf_op jit(solution)/shard_map/ppermute | solution.py:30
  30.6 1.4 %collective-permute-start.11 = (bf16[32,4608]{1,0:T(8,128)(2,1)S(1)}, bf16[32,4608]{1,0:T(8,128)(2,1)S(1)}, u32[]{:S(2)}, u32[]{:S(2)}) collective-permute-start(bf16[32,4608]{1,0:T(8,128)(2,1)S(1)} %collective-permute-done.3.refs_1_), channel_id=1, source_target_pairs={{0,48},{1,49},{2,50},{3,51},{4,52},{5,53},{6,54},{7,55},{8,24},{9,... | collective-permute-start | bytes 884744 | tf_op jit(solution)/shard_map/ppermute | solution.py:30
  32.0 4.0 %collective-permute-start.12 = (bf16[32,4608]{1,0:T(8,128)(2,1)S(1)}, bf16[32,4608]{1,0:T(8,128)(2,1)S(1)}, u32[]{:S(2)}, u32[]{:S(2)}) collective-permute-start(bf16[32,4608]{1,0:T(8,128)(2,1)S(1)} %collective-permute-done.2.refs_4_), channel_id=1, source_target_pairs={{0,68},{1,69},{2,70},{3,71},{4,64},{5,65},{6,66},{7,67},{8,76},{9,... | collective-permute-start | bytes 884744 | tf_op jit(solution)/shard_map/ppermute | solution.py:30
  36.1 3.0 %forward_low.1 = (bf16[256,4608]{1,0:T(8,128)(2,1)S(1)}, f32[256,1024]{1,0:T(8,128)S(1)}, bf16[256,1024]{1,0:T(8,128)(2,1)S(1)}, f32[256,128]{1,0:T(8,128)S(1)}, f32[256,128]{1,0:T(8,128)S(1)}) custom-call(s32[1]{0:T(128)} %bitcast.me_ref.refs_0_, bf16[32,4608]{1,0:T(8,128)(2,1)S(1)} %copy-done, bf16[32,4608]{1,0:T(8,128)(2,1)S(1)} %collective-permute-done.refs_2_, ...), custom_call_target="tpu_custom_call" | custom-call | flops 2415919104 | bytes 9437184 | tf_op jit(solution)/shard_map/forward_low/pallas_call | solution.py:116
  39.1 3.0 %back.2 = (bf16[8,4,32,576]{3,2,1,0:T(8,128)(2,1)S(1)}, bf16[8,4,32,576]{3,2,1,0:T(8,128)(2,1)S(1)}) custom-call(s32[1]{0:T(128)} %bitcast.me_ref.refs_0_, bf16[256,1024]{1,0:T(8,128)(2,1)S(1)} %get-tuple-element.110.rows_ref, bf16[4608,1024]{1,0:T(8,128)(2,1)S(1)} %get-tuple-element.105.refs_10_.head_ref), custom_call_target="tpu_custom_call" | custom-call | flops 2415919104 | bytes 9437184 | tf_op jit(solution)/shard_map/back/pallas_call | solution.py:194
  42.1 1.6 %collective-permute-done.11.refs_3_ = bf16[32,4608]{1,0:T(8,128)(2,1)S(1)} collective-permute-done((bf16[32,4608]{1,0:T(8,128)(2,1)S(1)}, bf16[32,4608]{1,0:T(8,128)(2,1)S(1)}, u32[]{:S(2)}, u32[]{:S(2)}) %collective-permute-start.11) | collective-permute-done | bytes 294944 | tf_op jit(solution)/shard_map/ppermute | solution.py:30
  46.3 3.0 %forward_high.1 = (bf16[256,4608]{1,0:T(8,128)(2,1)S(1)}, f32[256,1024]{1,0:T(8,128)S(1)}, bf16[256,1024]{1,0:T(8,128)(2,1)S(1)}, f32[256,128]{1,0:T(8,128)S(1)}, f32[256,128]{1,0:T(8,128)S(1)}) custom-call(s32[1]{0:T(128)} %bitcast.me_ref.refs_0_, bf16[32,4608]{1,0:T(8,128)(2,1)S(1)} %collective-permute-done.3.refs_1_, ...), custom_call_target="tpu_custom_call" | custom-call | flops 2415919104 | bytes 9437184 | tf_op jit(solution)/shard_map/forward_high/pallas_call | solution.py:116
  49.6 3.0 %back.3 = (bf16[8,4,32,576]{3,2,1,0:T(8,128)(2,1)S(1)}, bf16[8,4,32,576]{3,2,1,0:T(8,128)(2,1)S(1)}) custom-call(s32[1]{0:T(128)} %bitcast.me_ref.refs_0_, bf16[256,1024]{1,0:T(8,128)(2,1)S(1)} %get-tuple-element.118.rows_ref, bf16[4608,1024]{1,0:T(8,128)(2,1)S(1)} %get-tuple-element.105.refs_10_.head_ref), custom_call_target="tpu_custom_call" | custom-call | flops 2415919104 | bytes 9437184 | tf_op jit(solution)/shard_map/back/pallas_call | solution.py:194
  54.5 1.4 %collective-permute-start.20 = (f32[8,128]{1,0:T(8,128)S(1)}, f32[8,128]{1,0:T(8,128)S(1)}, u32[]{:S(2)}, u32[]{:S(2)}) collective-permute-start(f32[8,128]{1,0:T(8,128)S(1)} %add.31), channel_id=1, source_target_pairs={{0,48},{1,49},{2,50},{3,51},{4,52},{5,53},{6,54},{7,55},{8,24},{9,... | collective-permute-start | bytes 12296 | tf_op jit(solution)/shard_map/ppermute | solution.py:30
  55.9 3.4 %collective-permute-done.20 = f32[8,128]{1,0:T(8,128)S(1)} collective-permute-done((f32[8,128]{1,0:T(8,128)S(1)}, f32[8,128]{1,0:T(8,128)S(1)}, u32[]{:S(2)}, u32[]{:S(2)}) %collective-permute-start.20) | collective-permute-done | bytes 4128 | tf_op jit(solution)/shard_map/ppermute | solution.py:30
  59.9 1.3 %collective-permute-start.31 = (bf16[2,2,2,2,2,16,576]{6,5,4,3,2,1,0:T(8,128)(2,1)S(1)}, bf16[2,2,2,2,2,16,576]{6,5,4,3,2,1,0:T(8,128)(2,1)S(1)}, u32[]{:S(2)}, u32[]{:S(2)}) collective-permute-start(bf16[2,2,2,2,2,16,576]{6,5,4,3,2,1,0:T(8,128)(2,1)S(1)} %get-tuple-element.134), channel_id=1, source_target_pairs={{0,48},{1,49},{2,50},{3,51},{4,52},{5,53},{6,54},{7,55},{8,24},{9,... | collective-permute-start | bytes 1769480 | tf_op jit(solution)/shard_map/ppermute | solution.py:30
  62.4 2.0 %collective-permute-start.23 = (f32[8,128]{1,0:T(8,128)S(1)}, f32[8,128]{1,0:T(8,128)S(1)}, u32[]{:S(2)}, u32[]{:S(2)}) collective-permute-start(f32[8,128]{1,0:T(8,128)S(1)} %add.33), channel_id=1, source_target_pairs={{0,4},{1,5},{2,6},{3,7},{4,0},{5,1},{6,2},{7,3},{8,12},{9,13},{10,... | collective-permute-start | bytes 12296 | tf_op jit(solution)/shard_map/ppermute | solution.py:30
  64.4 3.6 %collective-permute-start.24 = (f32[8,128]{1,0:T(8,128)S(1)}, f32[8,128]{1,0:T(8,128)S(1)}, u32[]{:S(2)}, u32[]{:S(2)}) collective-permute-start(f32[8,128]{1,0:T(8,128)S(1)} %add.33), channel_id=1, source_target_pairs={{0,64},{1,65},{2,66},{3,67},{4,68},{5,69},{6,70},{7,71},{8,72},{9,... | collective-permute-start | bytes 12296 | tf_op jit(solution)/shard_map/ppermute | solution.py:30
  68.0 1.6 %collective-permute-done.24 = f32[8,128]{1,0:T(8,128)S(1)} collective-permute-done((f32[8,128]{1,0:T(8,128)S(1)}, f32[8,128]{1,0:T(8,128)S(1)}, u32[]{:S(2)}, u32[]{:S(2)}) %collective-permute-start.24) | collective-permute-done | bytes 4128 | tf_op jit(solution)/shard_map/ppermute | solution.py:30
  69.7 3.2 %collective-permute-done.25 = f32[8,128]{1,0:T(8,128)S(1)} collective-permute-done((f32[8,128]{1,0:T(8,128)S(1)}, f32[8,128]{1,0:T(8,128)S(1)}, u32[]{:S(2)}, u32[]{:S(2)}) %collective-permute-start.25) | collective-permute-done | bytes 4128 | tf_op jit(solution)/shard_map/ppermute | solution.py:30
  73.2 2.7 %collective-permute-start.27 = (f32[8,128]{1,0:T(8,128)S(1)}, f32[8,128]{1,0:T(8,128)S(1)}, u32[]{:S(2)}, u32[]{:S(2)}) collective-permute-start(f32[8,128]{1,0:T(8,128)S(1)} %add_add_fusion.1), channel_id=1, source_target_pairs={{0,3},{1,2},{2,1},{3,0},{4,7},{5,6},{6,5},{7,4},{8,9},{9,8},{10,11... | collective-permute-start | bytes 12296 | tf_op jit(solution)/shard_map/ppermute | solution.py:30
  76.0 1.4 %collective-permute-start.28 = (f32[8,128]{1,0:T(8,128)S(1)}, f32[8,128]{1,0:T(8,128)S(1)}, u32[]{:S(2)}, u32[]{:S(2)}) collective-permute-start(f32[8,128]{1,0:T(8,128)S(1)} %add_add_fusion.1), channel_id=1, source_target_pairs={{0,2},{1,3},{2,0},{3,1},{4,6},{5,7},{6,4},{7,5},{8,10},{9,11},{10,... | collective-permute-start | bytes 12296 | tf_op jit(solution)/shard_map/ppermute | solution.py:30
  78.0 3.0 %collective-permute-done.28 = f32[8,128]{1,0:T(8,128)S(1)} collective-permute-done((f32[8,128]{1,0:T(8,128)S(1)}, f32[8,128]{1,0:T(8,128)S(1)}, u32[]{:S(2)}, u32[]{:S(2)}) %collective-permute-start.28) | collective-permute-done | bytes 4128 | tf_op jit(solution)/shard_map/ppermute | solution.py:30
  81.7 1.7 %collective-permute-start.32 = (bf16[2,2,2,2,16,576]{5,4,3,2,1,0:T(8,128)(2,1)S(1)}, bf16[2,2,2,2,16,576]{5,4,3,2,1,0:T(8,128)(2,1)S(1)}, u32[]{:S(2)}, u32[]{:S(2)}) collective-permute-start(bf16[2,2,2,2,16,576]{5,4,3,2,1,0:T(8,128)(2,1)S(1)} %get-tuple-element.147), channel_id=1, source_target_pairs={{0,48},{1,49},{2,50},{3,51},{4,52},{5,53},{6,54},{7,55},{8,24},{9,... | collective-permute-start | bytes 884744 | tf_op jit(solution)/shard_map/ppermute | solution.py:30
  85.2 5.2 %head_gradient_low.1.started_ref = bf16[4608,1024]{1,0:T(8,128)(2,1)} custom-call(bf16[256,4608]{1,0:T(8,128)(2,1)S(1)} %get-tuple-element.153.low_ref, bf16[256,4608]{1,0:T(8,128)(2,1)S(1)} %get-tuple-element.154.high_ref, bf16[512,1024]{1,0:T(8,128)(2,1)S(1)} %dlogits.1.dlog_ref), custom_call_target="tpu_custom_call" | custom-call | flops 2415919104 | bytes 4718592 | tf_op jit(solution)/shard_map/head_gradient_low/pallas_call | solution.py:354
  90.4 2.9 %collective-permute-done.33.q_got = bf16[2,2,2,2,16,576]{5,4,3,2,1,0:T(8,128)(2,1)S(1)} collective-permute-done((bf16[2,2,2,2,16,576]{5,4,3,2,1,0:T(8,128)(2,1)S(1)}, bf16[2,2,2,2,16,576]{5,4,3,2,1,0:T(8,128)(2,1)S(1)}, u32[]{:S(2)}, u32[]{:S(2)}) %collective-permute-start.33) | collective-permute-done | bytes 294944 | tf_op jit(solution)/shard_map/ppermute | solution.py:30
  94.7 4.2 %head_gradient_high.1 = bf16[4608,1024]{1,0:T(8,128)(2,1)} custom-call(bf16[256,4608]{1,0:T(8,128)(2,1)S(1)} %get-tuple-element.153.low_ref, bf16[256,4608]{1,0:T(8,128)(2,1)S(1)} %get-tuple-element.154.high_ref, bf16[512,1024]{1,0:T(8,128)(2,1)S(1)} %dlogits.1.dlog_ref, bf16[4608,1024]{1,0:T(8,128)(2,1)} %head_gradient_low.1.started_ref), custom_call_target="tpu_custom_call", output_to_operand_aliasing={{}: (3, {})} | custom-call | flops 2415919104 | bytes 4718592 | tf_op jit(solution)/shard_map/head_gradient_high/pallas_call | solution.py:354
  98.9 1.7 %collective-permute-done.34.got_ref = bf16[2,2,2,32,576]{4,3,2,1,0:T(8,128)(2,1)S(1)} collective-permute-done((bf16[2,2,2,32,576]{4,3,2,1,0:T(8,128)(2,1)S(1)}, bf16[2,2,2,32,576]{4,3,2,1,0:T(8,128)(2,1)S(1)}, u32[]{:S(2)}, u32[]{:S(2)}) %collective-permute-start.34) | collective-permute-done | bytes 294944 | tf_op jit(solution)/shard_map/ppermute | solution.py:30
  100.7 5.3 %collective-permute-done.35.got = bf16[1,2,2,32,576]{4,3,2,1,0:T(8,128)(2,1)S(1)} collective-permute-done((bf16[1,2,2,32,576]{4,3,2,1,0:T(8,128)(2,1)S(1)}, bf16[1,2,2,32,576]{4,3,2,1,0:T(8,128)(2,1)S(1)}, u32[]{:S(2)}, u32[]{:S(2)}) %collective-permute-start.35) | collective-permute-done | bytes 147488 | tf_op jit(solution)/shard_map/ppermute | solution.py:30
  107.3 3.5 %collective-permute-start.38 = (bf16[32,576]{1,0:T(8,128)(2,1)S(1)}, bf16[32,576]{1,0:T(8,128)(2,1)S(1)}, u32[]{:S(2)}, u32[]{:S(2)}) collective-permute-start(bf16[32,576]{1,0:T(8,128)(2,1)S(1)} %get-tuple-element.171), channel_id=1, source_target_pairs={{0,68},{1,69},{2,70},{3,71},{4,64},{5,65},{6,66},{7,67},{8,76},{9,... | collective-permute-start | bytes 110600 | tf_op jit(solution)/shard_map/ppermute | solution.py:30
  (72 shorter events, 20.5 us)
Async XLA Ops:
  0.6 16.8 %collective-permute-start = (bf16[32,4608]{1,0:T(8,128)(2,1)}, bf16[32,4608]{1,0:T(8,128)(2,1)S(1)}, u32[]{:S(2)}, u32[]{:S(2)}) collective-permute-start(bf16[32,4608]{1,0:T(8,128)(2,1)} %refs_1_.1), channel_id=1, source_target_pairs={{0,16},{1,17},{2,18},{3,19},{4,20},{5,21},{6,22},{7,23},{8,56},{9,... | collective-permute-start | bytes 884744 | tf_op jit(solution)/shard_map/ppermute | solution.py:30
  2.3 15.2 %collective-permute-start.1 = (bf16[32,4608]{1,0:T(8,128)(2,1)}, bf16[32,4608]{1,0:T(8,128)(2,1)S(1)}, u32[]{:S(2)}, u32[]{:S(2)}) collective-permute-start(bf16[32,4608]{1,0:T(8,128)(2,1)} %refs_1_.1), channel_id=1, source_target_pairs={{0,48},{1,49},{2,50},{3,51},{4,52},{5,53},{6,54},{7,55},{8,24},{9,... | collective-permute-start | bytes 884744 | tf_op jit(solution)/shard_map/ppermute | solution.py:30
  4.4 14.0 %collective-permute-start.2 = (bf16[32,4608]{1,0:T(8,128)(2,1)}, bf16[32,4608]{1,0:T(8,128)(2,1)S(1)}, u32[]{:S(2)}, u32[]{:S(2)}) collective-permute-start(bf16[32,4608]{1,0:T(8,128)(2,1)} %refs_1_.1), channel_id=1, source_target_pairs={{0,32},{1,33},{2,34},{3,35},{4,36},{5,37},{6,38},{7,39},{8,40},{9,... | collective-permute-start | bytes 884744 | tf_op jit(solution)/shard_map/ppermute | solution.py:30
  5.0 13.3 %collective-permute-start.3 = (bf16[32,4608]{1,0:T(8,128)(2,1)}, bf16[32,4608]{1,0:T(8,128)(2,1)S(1)}, u32[]{:S(2)}, u32[]{:S(2)}) collective-permute-start(bf16[32,4608]{1,0:T(8,128)(2,1)} %refs_1_.1), channel_id=1, source_target_pairs={{0,68},{1,69},{2,70},{3,71},{4,64},{5,65},{6,66},{7,67},{8,76},{9,... | collective-permute-start | bytes 884744 | tf_op jit(solution)/shard_map/ppermute | solution.py:30
  18.4 4.9 %collective-permute-start.6 = (bf16[8,4,32,576]{3,2,1,0:T(8,128)(2,1)S(1)}, bf16[8,4,32,576]{3,2,1,0:T(8,128)(2,1)S(1)}, u32[]{:S(2)}, u32[]{:S(2)}) collective-permute-start(bf16[8,4,32,576]{3,2,1,0:T(8,128)(2,1)S(1)} %get-tuple-element.97), channel_id=1, source_target_pairs={{0,8},{1,9},{2,10},{3,11},{4,12},{5,13},{6,14},{7,15},{8,0},{9,1},... | collective-permute-start | bytes 3538952 | tf_op jit(solution)/shard_map/ppermute | solution.py:30
  18.9 6.7 %collective-permute-start.4 = (bf16[32,4608]{1,0:T(8,128)(2,1)S(1)}, bf16[32,4608]{1,0:T(8,128)(2,1)S(1)}, u32[]{:S(2)}, u32[]{:S(2)}) collective-permute-start(bf16[32,4608]{1,0:T(8,128)(2,1)S(1)} %collective-permute-done.3.refs_1_), channel_id=1, source_target_pairs={{0,16},{1,17},{2,18},{3,19},{4,20},{5,21},{6,22},{7,23},{8,56},{9,... | collective-permute-start | bytes 884744 | tf_op jit(solution)/shard_map/ppermute | solution.py:30
  19.4 9.4 %collective-permute-start.7 = (bf16[32,4608]{1,0:T(8,128)(2,1)S(1)}, bf16[32,4608]{1,0:T(8,128)(2,1)S(1)}, u32[]{:S(2)}, u32[]{:S(2)}) collective-permute-start(bf16[32,4608]{1,0:T(8,128)(2,1)S(1)} %copy-done), channel_id=1, source_target_pairs={{0,8},{1,9},{2,10},{3,11},{4,12},{5,13},{6,14},{7,15},{8,0},{9,1},... | collective-permute-start | bytes 884744 | tf_op jit(solution)/shard_map/ppermute | solution.py:30
  20.5 10.1 %collective-permute-start.9 = (bf16[32,4608]{1,0:T(8,128)(2,1)S(1)}, bf16[32,4608]{1,0:T(8,128)(2,1)S(1)}, u32[]{:S(2)}, u32[]{:S(2)}) collective-permute-start(bf16[32,4608]{1,0:T(8,128)(2,1)S(1)} %collective-permute-done.1.refs_3_), channel_id=1, source_target_pairs={{0,8},{1,9},{2,10},{3,11},{4,12},{5,13},{6,14},{7,15},{8,0},{9,1},... | collective-permute-start | bytes 884744 | tf_op jit(solution)/shard_map/ppermute | solution.py:30
  21.4 10.6 %collective-permute-start.10 = (bf16[32,4608]{1,0:T(8,128)(2,1)S(1)}, bf16[32,4608]{1,0:T(8,128)(2,1)S(1)}, u32[]{:S(2)}, u32[]{:S(2)}) collective-permute-start(bf16[32,4608]{1,0:T(8,128)(2,1)S(1)} %collective-permute-done.2.refs_4_), channel_id=1, source_target_pairs={{0,8},{1,9},{2,10},{3,11},{4,12},{5,13},{6,14},{7,15},{8,0},{9,1},... | collective-permute-start | bytes 884744 | tf_op jit(solution)/shard_map/ppermute | solution.py:30
  25.6 10.5 %collective-permute-start.8 = (bf16[32,4608]{1,0:T(8,128)(2,1)S(1)}, bf16[32,4608]{1,0:T(8,128)(2,1)S(1)}, u32[]{:S(2)}, u32[]{:S(2)}) collective-permute-start(bf16[32,4608]{1,0:T(8,128)(2,1)S(1)} %collective-permute-done.refs_2_), channel_id=1, source_target_pairs={{0,8},{1,9},{2,10},{3,11},{4,12},{5,13},{6,14},{7,15},{8,0},{9,1},... | collective-permute-start | bytes 884744 | tf_op jit(solution)/shard_map/ppermute | solution.py:30
  25.7 18.1 %collective-permute-start.13 = (bf16[2,2,2,2,2,16,576]{6,5,4,3,2,1,0:T(8,128)(2,1)S(1)}, bf16[2,2,2,2,2,16,576]{6,5,4,3,2,1,0:T(8,128)(2,1)S(1)}, u32[]{:S(2)}, u32[]{:S(2)}) collective-permute-start(bf16[2,2,2,2,2,16,576]{6,5,4,3,2,1,0:T(8,128)(2,1)S(1)} %get-tuple-element.108), channel_id=1, source_target_pairs={{0,3},{1,2},{2,1},{3,0},{4,7},{5,6},{6,5},{7,4},{8,9},{9,8},{10,11... | collective-permute-start | bytes 1769480 | tf_op jit(solution)/shard_map/ppermute | solution.py:30
  28.8 15.0 %collective-permute-start.14 = (bf16[2,2,2,2,2,16,576]{6,5,4,3,2,1,0:T(8,128)(2,1)S(1)}, bf16[2,2,2,2,2,16,576]{6,5,4,3,2,1,0:T(8,128)(2,1)S(1)}, u32[]{:S(2)}, u32[]{:S(2)}) collective-permute-start(bf16[2,2,2,2,2,16,576]{6,5,4,3,2,1,0:T(8,128)(2,1)S(1)} %get-tuple-element.109), channel_id=1, source_target_pairs={{0,48},{1,49},{2,50},{3,51},{4,52},{5,53},{6,54},{7,55},{8,24},{9,... | collective-permute-start | bytes 1769480 | tf_op jit(solution)/shard_map/ppermute | solution.py:30
  30.6 13.1 %collective-permute-start.11 = (bf16[32,4608]{1,0:T(8,128)(2,1)S(1)}, bf16[32,4608]{1,0:T(8,128)(2,1)S(1)}, u32[]{:S(2)}, u32[]{:S(2)}) collective-permute-start(bf16[32,4608]{1,0:T(8,128)(2,1)S(1)} %collective-permute-done.3.refs_1_), channel_id=1, source_target_pairs={{0,48},{1,49},{2,50},{3,51},{4,52},{5,53},{6,54},{7,55},{8,24},{9,... | collective-permute-start | bytes 884744 | tf_op jit(solution)/shard_map/ppermute | solution.py:30
  32.0 11.7 %collective-permute-start.12 = (bf16[32,4608]{1,0:T(8,128)(2,1)S(1)}, bf16[32,4608]{1,0:T(8,128)(2,1)S(1)}, u32[]{:S(2)}, u32[]{:S(2)}) collective-permute-start(bf16[32,4608]{1,0:T(8,128)(2,1)S(1)} %collective-permute-done.2.refs_4_), channel_id=1, source_target_pairs={{0,68},{1,69},{2,70},{3,71},{4,64},{5,65},{6,66},{7,67},{8,76},{9,... | collective-permute-start | bytes 884744 | tf_op jit(solution)/shard_map/ppermute | solution.py:30
  36.1 8.4 %collective-permute-start.15 = (bf16[32,4608]{1,0:T(8,128)(2,1)S(1)}, bf16[32,4608]{1,0:T(8,128)(2,1)S(1)}, u32[]{:S(2)}, u32[]{:S(2)}) collective-permute-start(bf16[32,4608]{1,0:T(8,128)(2,1)S(1)} %collective-permute-done.3.refs_1_), channel_id=1, source_target_pairs={{0,8},{1,9},{2,10},{3,11},{4,12},{5,13},{6,14},{7,15},{8,0},{9,1},... | collective-permute-start | bytes 884744 | tf_op jit(solution)/shard_map/ppermute | solution.py:30
  53.2 6.1 %collective-permute-start.21 = (bf16[8,4,32,576]{3,2,1,0:T(8,128)(2,1)S(1)}, bf16[8,4,32,576]{3,2,1,0:T(8,128)(2,1)S(1)}, u32[]{:S(2)}, u32[]{:S(2)}) collective-permute-start(bf16[8,4,32,576]{3,2,1,0:T(8,128)(2,1)S(1)} %get-tuple-element.121), channel_id=1, source_target_pairs={{0,8},{1,9},{2,10},{3,11},{4,12},{5,13},{6,14},{7,15},{8,0},{9,1},... | collective-permute-start | bytes 3538952 | tf_op jit(solution)/shard_map/ppermute | solution.py:30
  54.4 4.9 %collective-permute-start.29 = (bf16[8,4,32,576]{3,2,1,0:T(8,128)(2,1)S(1)}, bf16[8,4,32,576]{3,2,1,0:T(8,128)(2,1)S(1)}, u32[]{:S(2)}, u32[]{:S(2)}) collective-permute-start(bf16[8,4,32,576]{3,2,1,0:T(8,128)(2,1)S(1)} %get-tuple-element.130), channel_id=1, source_target_pairs={{0,8},{1,9},{2,10},{3,11},{4,12},{5,13},{6,14},{7,15},{8,0},{9,1},... | collective-permute-start | bytes 3538952 | tf_op jit(solution)/shard_map/ppermute | solution.py:30
  54.5 4.8 %collective-permute-start.20 = (f32[8,128]{1,0:T(8,128)S(1)}, f32[8,128]{1,0:T(8,128)S(1)}, u32[]{:S(2)}, u32[]{:S(2)}) collective-permute-start(f32[8,128]{1,0:T(8,128)S(1)} %add.31), channel_id=1, source_target_pairs={{0,48},{1,49},{2,50},{3,51},{4,52},{5,53},{6,54},{7,55},{8,24},{9,... | collective-permute-start | bytes 12296 | tf_op jit(solution)/shard_map/ppermute | solution.py:30
  59.6 21.4 %collective-permute-start.30 = (bf16[2,2,2,2,2,16,576]{6,5,4,3,2,1,0:T(8,128)(2,1)S(1)}, bf16[2,2,2,2,2,16,576]{6,5,4,3,2,1,0:T(8,128)(2,1)S(1)}, u32[]{:S(2)}, u32[]{:S(2)}) collective-permute-start(bf16[2,2,2,2,2,16,576]{6,5,4,3,2,1,0:T(8,128)(2,1)S(1)} %get-tuple-element.133), channel_id=1, source_target_pairs={{0,3},{1,2},{2,1},{3,0},{4,7},{5,6},{6,5},{7,4},{8,9},{9,8},{10,11... | collective-permute-start | bytes 1769480 | tf_op jit(solution)/shard_map/ppermute | solution.py:30
  59.9 21.1 %collective-permute-start.31 = (bf16[2,2,2,2,2,16,576]{6,5,4,3,2,1,0:T(8,128)(2,1)S(1)}, bf16[2,2,2,2,2,16,576]{6,5,4,3,2,1,0:T(8,128)(2,1)S(1)}, u32[]{:S(2)}, u32[]{:S(2)}) collective-permute-start(bf16[2,2,2,2,2,16,576]{6,5,4,3,2,1,0:T(8,128)(2,1)S(1)} %get-tuple-element.134), channel_id=1, source_target_pairs={{0,48},{1,49},{2,50},{3,51},{4,52},{5,53},{6,54},{7,55},{8,24},{9,... | collective-permute-start | bytes 1769480 | tf_op jit(solution)/shard_map/ppermute | solution.py:30
  62.4 5.6 %collective-permute-start.23 = (f32[8,128]{1,0:T(8,128)S(1)}, f32[8,128]{1,0:T(8,128)S(1)}, u32[]{:S(2)}, u32[]{:S(2)}) collective-permute-start(f32[8,128]{1,0:T(8,128)S(1)} %add.33), channel_id=1, source_target_pairs={{0,4},{1,5},{2,6},{3,7},{4,0},{5,1},{6,2},{7,3},{8,12},{9,13},{10,... | collective-permute-start | bytes 12296 | tf_op jit(solution)/shard_map/ppermute | solution.py:30
  64.4 5.2 %collective-permute-start.24 = (f32[8,128]{1,0:T(8,128)S(1)}, f32[8,128]{1,0:T(8,128)S(1)}, u32[]{:S(2)}, u32[]{:S(2)}) collective-permute-start(f32[8,128]{1,0:T(8,128)S(1)} %add.33), channel_id=1, source_target_pairs={{0,64},{1,65},{2,66},{3,67},{4,68},{5,69},{6,70},{7,71},{8,72},{9,... | collective-permute-start | bytes 12296 | tf_op jit(solution)/shard_map/ppermute | solution.py:30
  68.0 4.8 %collective-permute-start.25 = (f32[8,128]{1,0:T(8,128)S(1)}, f32[8,128]{1,0:T(8,128)S(1)}, u32[]{:S(2)}, u32[]{:S(2)}) collective-permute-start(f32[8,128]{1,0:T(8,128)S(1)} %add.33), channel_id=1, source_target_pairs={{0,68},{1,69},{2,70},{3,71},{4,64},{5,65},{6,66},{7,67},{8,76},{9,... | collective-permute-start | bytes 12296 | tf_op jit(solution)/shard_map/ppermute | solution.py:30
  73.2 4.8 %collective-permute-start.27 = (f32[8,128]{1,0:T(8,128)S(1)}, f32[8,128]{1,0:T(8,128)S(1)}, u32[]{:S(2)}, u32[]{:S(2)}) collective-permute-start(f32[8,128]{1,0:T(8,128)S(1)} %add_add_fusion.1), channel_id=1, source_target_pairs={{0,3},{1,2},{2,1},{3,0},{4,7},{5,6},{6,5},{7,4},{8,9},{9,8},{10,11... | collective-permute-start | bytes 12296 | tf_op jit(solution)/shard_map/ppermute | solution.py:30
  76.0 5.1 %collective-permute-start.28 = (f32[8,128]{1,0:T(8,128)S(1)}, f32[8,128]{1,0:T(8,128)S(1)}, u32[]{:S(2)}, u32[]{:S(2)}) collective-permute-start(f32[8,128]{1,0:T(8,128)S(1)} %add_add_fusion.1), channel_id=1, source_target_pairs={{0,2},{1,3},{2,0},{3,1},{4,6},{5,7},{6,4},{7,5},{8,10},{9,11},{10,... | collective-permute-start | bytes 12296 | tf_op jit(solution)/shard_map/ppermute | solution.py:30
  81.7 8.7 %collective-permute-start.32 = (bf16[2,2,2,2,16,576]{5,4,3,2,1,0:T(8,128)(2,1)S(1)}, bf16[2,2,2,2,16,576]{5,4,3,2,1,0:T(8,128)(2,1)S(1)}, u32[]{:S(2)}, u32[]{:S(2)}) collective-permute-start(bf16[2,2,2,2,16,576]{5,4,3,2,1,0:T(8,128)(2,1)S(1)} %get-tuple-element.147), channel_id=1, source_target_pairs={{0,48},{1,49},{2,50},{3,51},{4,52},{5,53},{6,54},{7,55},{8,24},{9,... | collective-permute-start | bytes 884744 | tf_op jit(solution)/shard_map/ppermute | solution.py:30
  83.8 9.5 %collective-permute-start.33 = (bf16[2,2,2,2,16,576]{5,4,3,2,1,0:T(8,128)(2,1)S(1)}, bf16[2,2,2,2,16,576]{5,4,3,2,1,0:T(8,128)(2,1)S(1)}, u32[]{:S(2)}, u32[]{:S(2)}) collective-permute-start(bf16[2,2,2,2,16,576]{5,4,3,2,1,0:T(8,128)(2,1)S(1)} %get-tuple-element.152), channel_id=1, source_target_pairs={{0,3},{1,2},{2,1},{3,0},{4,7},{5,6},{6,5},{7,4},{8,9},{9,8},{10,11... | collective-permute-start | bytes 884744 | tf_op jit(solution)/shard_map/ppermute | solution.py:30
  93.4 7.2 %collective-permute-start.34 = (bf16[2,2,2,32,576]{4,3,2,1,0:T(8,128)(2,1)S(1)}, bf16[2,2,2,32,576]{4,3,2,1,0:T(8,128)(2,1)S(1)}, u32[]{:S(2)}, u32[]{:S(2)}) collective-permute-start(bf16[2,2,2,32,576]{4,3,2,1,0:T(8,128)(2,1)S(1)} %get-tuple-element.161), channel_id=1, source_target_pairs={{0,1},{1,0},{2,3},{3,2},{4,5},{5,4},{6,7},{7,6},{8,11},{9,10},{10,... | collective-permute-start | bytes 884744 | tf_op jit(solution)/shard_map/ppermute | solution.py:30
  100.6 5.4 %collective-permute-start.35 = (bf16[1,2,2,32,576]{4,3,2,1,0:T(8,128)(2,1)S(1)}, bf16[1,2,2,32,576]{4,3,2,1,0:T(8,128)(2,1)S(1)}, u32[]{:S(2)}, u32[]{:S(2)}) collective-permute-start(bf16[1,2,2,32,576]{4,3,2,1,0:T(8,128)(2,1)S(1)} %get-tuple-element.167), channel_id=1, source_target_pairs={{0,16},{1,17},{2,18},{3,19},{4,20},{5,21},{6,22},{7,23},{8,56},{9,... | collective-permute-start | bytes 442376 | tf_op jit(solution)/shard_map/ppermute | solution.py:30
  106.0 5.4 %collective-permute-start.36 = (bf16[32,576]{1,0:T(8,128)(2,1)S(1)}, bf16[32,576]{1,0:T(8,128)(2,1)S(1)}, u32[]{:S(2)}, u32[]{:S(2)}) collective-permute-start(bf16[32,576]{1,0:T(8,128)(2,1)S(1)} %get-tuple-element.169), channel_id=1, source_target_pairs={{0,4},{1,5},{2,6},{3,7},{4,0},{5,1},{6,2},{7,3},{8,12},{9,13},{10,... | collective-permute-start | bytes 110600 | tf_op jit(solution)/shard_map/ppermute | solution.py:30
  106.1 5.6 %collective-permute-start.37 = (bf16[32,576]{1,0:T(8,128)(2,1)S(1)}, bf16[32,576]{1,0:T(8,128)(2,1)S(1)}, u32[]{:S(2)}, u32[]{:S(2)}) collective-permute-start(bf16[32,576]{1,0:T(8,128)(2,1)S(1)} %get-tuple-element.170), channel_id=1, source_target_pairs={{0,64},{1,65},{2,66},{3,67},{4,68},{5,69},{6,70},{7,71},{8,72},{9,... | collective-permute-start | bytes 110600 | tf_op jit(solution)/shard_map/ppermute | solution.py:30
  107.3 5.5 %collective-permute-start.38 = (bf16[32,576]{1,0:T(8,128)(2,1)S(1)}, bf16[32,576]{1,0:T(8,128)(2,1)S(1)}, u32[]{:S(2)}, u32[]{:S(2)}) collective-permute-start(bf16[32,576]{1,0:T(8,128)(2,1)S(1)} %get-tuple-element.171), channel_id=1, source_target_pairs={{0,68},{1,69},{2,70},{3,71},{4,64},{5,65},{6,66},{7,67},{8,76},{9,... | collective-permute-start | bytes 110600 | tf_op jit(solution)/shard_map/ppermute | solution.py:30
  (8 other events, 28.3 us)

commit v2 on v1

--- a/solution.py
+++ b/solution.py
@@ -20,6 +20,7 @@
 
 
 CORE = flips(8, 8)
+XY1 = flips(16 ^ 1, 48 ^ 3)
 X1, X2 = flips(16, 48), flips(48, 16)
 Y1, Y2 = flips(1, 3), flips(3, 1)
 X3, Y3 = flips(32, 32), flips(2, 2)
@@ -244,38 +245,41 @@
 
 
 def fold(*refs):
-    parts, (p_keep, p_send, q_keep, q_send) = refs[:4], refs[4:]
+    parts, (p_keep, p_send, q_keep, q_send) = refs[:8], refs[8:]
     for zr in range(2):
-        mine, got = parts[2 * zr : 2 * zr + 2]
+        a_mine, a_got, g_mine, g_got = parts[4 * zr : 4 * zr + 4]
         for zl in range(2):
             for k in range(4):
+                b = 4 * zl + k
                 for x in range(4):
-                    total = mine[4 * zl + k, x] + got[4 * zl + k, x]
-                    (p_keep if k < 2 else p_send)[x // 2, k % 2, x % 2, zr, zl] = total[:16]
-                    (q_keep if x < 2 else q_send)[k // 2, k % 2, x % 2, zr, zl] = total[16:]
+                    p_at = (p_keep if k < 2 else p_send).at[x // 2, k % 2, x % 2, zr, zl]
+                    q_at = (q_keep if x < 2 else q_send).at[k // 2, k % 2, x % 2, zr, zl]
+                    for first, mine, got in ((0, a_mine, a_got), (16, g_mine, g_got)):
+                        total = mine[b, x] + got[b, x]
+                        p_at[first : first + 16] = total[:16]
+                        q_at[first : first + 16] = total[16:]
 
 
 def run_fold(*parts):
-    return call(fold, "vvvv", [("v", (2, 2, 2, 2, 2, 16, FEATURES), bf16)] * 4, moved=512 * D * 4)(*parts)
-
-
-def combine(first_row, slots, rest_ref, pick_ref, a_ref, a_got, g_ref, g_got, keep, out):
-    for h in range(2):
+    return call(fold, "v" * 8, [("v", (2, 2, 2, 2, 2, 32, FEATURES), bf16)] * 4, moved=512 * D * 8)(*parts)
+
+
+def combine(first_row, slots, rest_ref, pick_ref, held, got, keep, out):
+    for h, target in enumerate((keep, out)):
         for i in range(2):
             for j in range(2):
                 x = slots(h, j)
                 for zr in range(2):
-                    start_row = 128 * zr + 32 * x + first_row
-                    rest = rest_ref[start_row : start_row + 16, :]
-                    pick = pick_ref[start_row : start_row + 16, :]
+                    first = 128 * zr + 32 * x + first_row
+                    rest = rest_ref[first : first + 16, :]
+                    pick = pick_ref[first : first + 16, :]
                     for zl in range(2):
                         for start in range(0, FEATURES, 128):
                             wide = min(128, FEATURES - start)
                             at = (h, i, j, zr, zl, slice(None), slice(start, start + wide))
-                            terms = (a_ref[at] + a_got[at]).astype(f32)
-                            columns = (g_ref[at] + g_got[at]).astype(f32)
-                            total = rest[:, :wide] * terms + pick[:, :wide] * columns
-                            (out if h else keep)[at[1:]] = total.astype(bf16)
+                            both = (held[at] + got[at]).astype(f32)
+                            total = rest[:, :wide] * both[:16] + pick[:, :wide] * both[16:]
+                            target[at[1:]] = total.astype(bf16)
 
 
 def combine_p(*refs):
@@ -286,9 +290,29 @@
     combine(16, lambda h, j: j, *refs)
 
 
-def run_combine(kernel, rest, pick, *parts):
+def run_combine(kernel, *parts):
     half = ("v", (2, 2, 2, 2, 16, FEATURES), bf16)
-    return call(kernel, "v" * 6, [half, half], moved=1 << 22)(rest, pick, *parts)
+    return call(kernel, "v" * 4, [half, half], moved=1 << 22)(*parts)
+
+
+def join(p_keep, p_got, q_keep, q_got, *outs):
+    for n, out in enumerate(outs):
+        out[:, :, :16] = p_keep[n // 2, n % 2] + p_got[n // 2, n % 2]
+        out[:, :, 16:] = q_keep[n // 2, n % 2] + q_got[n // 2, n % 2]
+
+
+def run_join(*parts):
+    return call(join, "v" * 4, [("v", (2, 2, 32, FEATURES), bf16)] * 4, moved=1 << 22)(*parts)
+
+
+def split(*refs):
+    terms, outs = refs[:4], refs[4:]
+    for z, out in enumerate(outs):
+        out[...] = sum(term[z // 2, z % 2].astype(f32) for term in terms).astype(bf16)
+
+
+def run_split(*parts):
+    return call(split, "vvvv", [("v", (32, FEATURES), bf16)] * 4, moved=1 << 20)(*parts)
 
 
 def finish(*refs):
@@ -370,38 +394,6 @@
     return lax.optimization_barrier(arrays)
 
 
-def halve(keep_ref, got_ref, keep, out):
-    n = keep.shape[0]
-    keep[...] = keep_ref[:n] + got_ref[:n]
-    out[...] = keep_ref[n:] + got_ref[n:]
-
-
-def run_halve(held, got):
-    n = held.shape[0] // 2
-    half = ("v", (n,) + held.shape[1:], bf16)
-    return call(halve, "vv", [half, half], moved=held.size * 6)(held, got)
-
-
-def join(p_keep, p_got, q_keep, q_got, keep, out):
-    for k, target in enumerate((keep, out)):
-        target[:, :, :, :16] = p_keep[k] + p_got[k]
-        target[:, :, :, 16:] = q_keep[k] + q_got[k]
-
-
-def run_join(*parts):
-    half = ("v", (2, 2, 2, 32, FEATURES), bf16)
-    return call(join, "v" * 4, [half, half], moved=1 << 22)(*parts)
-
-
-def split(keep, got, *outs):
-    for z, out in enumerate(outs):
-        out[...] = keep[0, z // 2, z % 2] + got[0, z // 2, z % 2]
-
-
-def run_split(*parts):
-    return call(split, "vv", [("v", (32, FEATURES), bf16)] * 4, moved=1 << 20)(*parts)
-
-
 def local(hidden, head, verdict_ids, row_weight):
     me = (lax.axis_index("dp") * 8 + lax.axis_index("vocab")).astype(jnp.int32).reshape(1)
     a1, a2, a3 = send(hidden, X1), send(hidden, X2), send(hidden, X3)
@@ -412,14 +404,12 @@
     a1, a2, a3, o0, g0_mine, g0_mate, g1_mine, g1_mate = tie(a1, a2, a3, o0, g0_mine, g0_mate, g1_mine, g1_mate)
     o1, o2, o3 = send(o0, X1), send(o0, X2), send(a3, ZH)
     g0_got, g1_got = send(g0_mate, CORE), send(g1_mate, CORE)
-    gp_keep, gp_send, gq_keep, gq_send = run_fold(g0_mine, g0_got, g1_mine, g1_got)
-    o1, gp_send, gq_send, a1 = tie(o1, gp_send, gq_send, a1)
-    gp_got, gq_got = send(gp_send, Y2), send(gq_send, X2)
     own_half = [hidden, a1, a2, a3]
     own_half += [send(piece, CORE) for piece in own_half]
     rows0, capped0, term0, total0, target0 = run_forward(forward_low, me, own_half, ids, head)
+    o1, term0 = tie(o1, term0)
     a0_mine, a0_mate = run_back(me, term0, head)
-    o1, o2, o3, gp_got, gq_got, a0_mate = tie(o1, o2, o3, gp_got, gq_got, a0_mate)
+    o1, o2, o3, g0_got, g1_got, a0_mate = tie(o1, o2, o3, g0_got, g1_got, a0_mate)
     other_half = [o0, o1, o2, o3]
     other_half += [send(piece, CORE) for piece in other_half]
     rows1, capped1, term1, total1, target1 = run_forward(forward_high, me, other_half, ids, head)
@@ -434,25 +424,26 @@
     a1_got = send(a1_mate, CORE)
     sums = step(sums, X2)
     sums, a1_got = tie(sums, a1_got)
-    p_keep, p_send, q_keep, q_send = run_fold(a0_mine, send(a0_mate, CORE), a1_mine, a1_got)
+    p_keep, p_send, q_keep, q_send = run_fold(
+        a0_mine, send(a0_mate, CORE), g0_mine, g0_got, a1_mine, a1_got, g1_mine, g1_got
+    )
 
     p_got, q_got = send(p_send, Y2), send(q_send, X2)
     sums = step(step(step(sums, CORE), ZL, Z2, ZH), Y1, Y2, Y3)
     sums, p_got, q_got = tie(sums, p_got, q_got)
     log_total, own, rest, pick = run_unpack(me, sums, weight)
-    p_keep, p_send = run_combine(combine_p, rest, pick, p_keep, p_got, gp_keep, gp_got)
-    q_keep, q_send = run_combine(combine_q, rest, pick, q_keep, q_got, gq_keep, gq_got)
+    p_keep, p_send = run_combine(combine_p, rest, pick, p_keep, p_got)
+    q_keep, q_send = run_combine(combine_q, rest, pick, q_keep, q_got)
     p_got, q_got = send(p_send, X2), send(q_send, Y2)
     log_total, p_keep = tie(log_total, p_keep)
     dlog = run_dlogits(me, capped0, capped1, log_total, weight, ids)
     head_grad = run_head_gradient(head_gradient_low, rows0, rows1, dlog)
     p_got, q_got, head_grad = tie(p_got, q_got, head_grad)
-    keep, out = run_join(p_keep, p_got, q_keep, q_got)
-    got = send(out, Y1)
+    keep, *outs = run_join(p_keep, p_got, q_keep, q_got)
+    got = [send(out, partner) for out, partner in zip(outs, (X1, Y1, XY1))]
     head_grad = run_head_gradient(head_gradient_high, rows0, rows1, dlog, (head_grad,))
-    got, head_grad = tie(got, head_grad)
-    keep, out = run_halve(keep, got)
-    keep, *outs = run_split(keep, send(out, X1))
+    *got, head_grad = tie(*got, head_grad)
+    keep, *outs = run_split(keep, *got)
     z_got = tie(*(send(out, partner) for out, partner in zip(outs, (ZL, Z2, ZH))))
     hidden_grad = run_finish(keep, *z_got)
     return (own[:, 0], head_grad, hidden_grad)

time: 114 us -> 107 us (0.939)
  waiting for transfers between devices: 33.9 us -> 24.2 us
  starting transfers between devices: 44.8 us -> 47.6 us
    ppermute x39 -> x38, waiting for transfers between devices: 33.9 us -> 24.2 us  [send(): return lax.ppermute(array, AXES, partner)]
    ppermute x39 -> x38, starting transfers between devices: 44.8 us -> 47.6 us  [send(): return lax.ppermute(array, AXES, partner)]
  transfers between devices with their start and end apart: 39 -> 38, of which waited for: 20 -> 16; matrix products, arithmetic and copies ran while one was open for 1% -> 1% of each run, Pallas kernels for 25% -> 26%
where the time goes in v2:
time: 107 us
  starting transfers between devices  47.6 us (44%)
  Pallas kernels  33.5 us (31%)
  waiting for transfers between devices  24.2 us (23%)
    ppermute x38, starting transfers between devices, send(): return lax.ppermute(array, AXES, partner)  47.6 us
    ppermute x38, waiting for transfers between devices, send(): return lax.ppermute(array, AXES, partner)  24.2 us
    pallas_call x2, Pallas kernels, run_head_gradient(): call(kernel, 'vvv' + 'h' * len(started), [('h', (D, WIDTH), bf16)], scrat...  9.37 us
    pallas_call x1, Pallas kernels, run_begin(): call(begin, 'shhh', [BLOCKS] * 4 + [('v', (D, WIDTH), bf16), column, colu...  8.37 us
    pallas_call x2, Pallas kernels, run_back(): return call(back, 'svv', [BLOCKS, BLOCKS], **BACK_COST)(me, rows, head)  6.11 us
    pallas_call x2, Pallas kernels, run_forward(): call(kernel, 's' + 'v' * 10, [('v', (256, D), bf16), ('v', (256, WIDTH),...  5.97 us
  transfers between devices with their start and end apart: 38, of which 16 were waited for; matrix products, arithmetic and copies ran while one was open for 1% of the time, Pallas kernels for 26%

profile of v2, /device:TPU:0, one launch (start us, length us, event | category | flops | bytes accessed | tf_op | source)
XLA Modules:
  0.0 106.8 jit_solution(14470736848647892752)
XLA Ops:
  0.6 1.7 %collective-permute-start = (bf16[32,4608]{1,0:T(8,128)(2,1)}, bf16[32,4608]{1,0:T(8,128)(2,1)S(1)}, u32[]{:S(2)}, u32[]{:S(2)}) collective-permute-start(bf16[32,4608]{1,0:T(8,128)(2,1)} %refs_1_.1), channel_id=1, source_target_pairs={{0,16},{1,17},{2,18},{3,19},{4,20},{5,21},{6,22},{7,23},{8,56},{9,... | collective-permute-start | bytes 884744 | tf_op jit(solution)/shard_map/ppermute | solution.py:31
  2.3 2.1 %collective-permute-start.1 = (bf16[32,4608]{1,0:T(8,128)(2,1)}, bf16[32,4608]{1,0:T(8,128)(2,1)S(1)}, u32[]{:S(2)}, u32[]{:S(2)}) collective-permute-start(bf16[32,4608]{1,0:T(8,128)(2,1)} %refs_1_.1), channel_id=1, source_target_pairs={{0,48},{1,49},{2,50},{3,51},{4,52},{5,53},{6,54},{7,55},{8,24},{9,... | collective-permute-start | bytes 884744 | tf_op jit(solution)/shard_map/ppermute | solution.py:31
  5.0 4.0 %collective-permute-start.3 = (bf16[32,4608]{1,0:T(8,128)(2,1)}, bf16[32,4608]{1,0:T(8,128)(2,1)S(1)}, u32[]{:S(2)}, u32[]{:S(2)}) collective-permute-start(bf16[32,4608]{1,0:T(8,128)(2,1)} %refs_1_.1), channel_id=1, source_target_pairs={{0,68},{1,69},{2,70},{3,71},{4,64},{5,65},{6,66},{7,67},{8,76},{9,... | collective-permute-start | bytes 884744 | tf_op jit(solution)/shard_map/ppermute | solution.py:31
  9.1 8.4 %begin.1 = (bf16[8,4,32,576]{3,2,1,0:T(8,128)(2,1)S(1)}, bf16[8,4,32,576]{3,2,1,0:T(8,128)(2,1)S(1)}, bf16[8,4,32,576]{3,2,1,0:T(8,128)(2,1)S(1)}, bf16[8,4,32,5...) custom-call(s32[1]{0:T(128)} %bitcast.me_ref.refs_0_, ...), custom_call_target="tpu_custom_call" | custom-call | flops 4831838208 | bytes 9437184 | tf_op jit(solution)/shard_map/begin/pallas_call | solution.py:230
  19.4 4.3 %collective-permute-done.4.refs_5_ = bf16[32,4608]{1,0:T(8,128)(2,1)S(1)} collective-permute-done((bf16[32,4608]{1,0:T(8,128)(2,1)S(1)}, bf16[32,4608]{1,0:T(8,128)(2,1)S(1)}, u32[]{:S(2)}, u32[]{:S(2)}) %collective-permute-start.4) | collective-permute-done | bytes 294944 | tf_op jit(solution)/shard_map/ppermute | solution.py:31
  24.7 2.1 %collective-permute-start.9 = (bf16[32,4608]{1,0:T(8,128)(2,1)S(1)}, bf16[32,4608]{1,0:T(8,128)(2,1)S(1)}, u32[]{:S(2)}, u32[]{:S(2)}) collective-permute-start(bf16[32,4608]{1,0:T(8,128)(2,1)S(1)} %collective-permute-done.3.refs_1_), channel_id=1, source_target_pairs={{0,48},{1,49},{2,50},{3,51},{4,52},{5,53},{6,54},{7,55},{8,24},{9,... | collective-permute-start | bytes 884744 | tf_op jit(solution)/shard_map/ppermute | solution.py:31
  26.8 3.6 %collective-permute-start.10 = (bf16[32,4608]{1,0:T(8,128)(2,1)S(1)}, bf16[32,4608]{1,0:T(8,128)(2,1)S(1)}, u32[]{:S(2)}, u32[]{:S(2)}) collective-permute-start(bf16[32,4608]{1,0:T(8,128)(2,1)S(1)} %collective-permute-done.2.refs_4_), channel_id=1, source_target_pairs={{0,68},{1,69},{2,70},{3,71},{4,64},{5,65},{6,66},{7,67},{8,76},{9,... | collective-permute-start | bytes 884744 | tf_op jit(solution)/shard_map/ppermute | solution.py:31
  30.4 3.0 %forward_low.1 = (bf16[256,4608]{1,0:T(8,128)(2,1)S(1)}, f32[256,1024]{1,0:T(8,128)S(1)}, bf16[256,1024]{1,0:T(8,128)(2,1)S(1)}, f32[256,128]{1,0:T(8,128)S(1)}, f32[256,128]{1,0:T(8,128)S(1)}) custom-call(s32[1]{0:T(128)} %bitcast.me_ref.refs_0_, bf16[32,4608]{1,0:T(8,128)(2,1)S(1)} %copy-done, bf16[32,4608]{1,0:T(8,128)(2,1)S(1)} %collective-permute-done.refs_2_, ...), custom_call_target="tpu_custom_call" | custom-call | flops 2415919104 | bytes 9437184 | tf_op jit(solution)/shard_map/forward_low/pallas_call | solution.py:117
  33.5 3.0 %back.2 = (bf16[8,4,32,576]{3,2,1,0:T(8,128)(2,1)S(1)}, bf16[8,4,32,576]{3,2,1,0:T(8,128)(2,1)S(1)}) custom-call(s32[1]{0:T(128)} %bitcast.me_ref.refs_0_, bf16[256,1024]{1,0:T(8,128)(2,1)S(1)} %get-tuple-element.100.rows_ref, bf16[4608,1024]{1,0:T(8,128)(2,1)S(1)} %get-tuple-element.93.refs_10_.head_ref), custom_call_target="tpu_custom_call" | custom-call | flops 2415919104 | bytes 9437184 | tf_op jit(solution)/shard_map/back/pallas_call | solution.py:195
  39.6 3.0 %forward_high.1 = (bf16[256,4608]{1,0:T(8,128)(2,1)S(1)}, f32[256,1024]{1,0:T(8,128)S(1)}, bf16[256,1024]{1,0:T(8,128)(2,1)S(1)}, f32[256,128]{1,0:T(8,128)S(1)}, f32[256,128]{1,0:T(8,128)S(1)}) custom-call(s32[1]{0:T(128)} %bitcast.me_ref.refs_0_, bf16[32,4608]{1,0:T(8,128)(2,1)S(1)} %collective-permute-done.3.refs_1_, ...), custom_call_target="tpu_custom_call" | custom-call | flops 2415919104 | bytes 9437184 | tf_op jit(solution)/shard_map/forward_high/pallas_call | solution.py:117
  42.8 1.6 %collective-permute-start.17 = (f32[8,128]{1,0:T(8,128)S(1)}, f32[8,128]{1,0:T(8,128)S(1)}, u32[]{:S(2)}, u32[]{:S(2)}) collective-permute-start(f32[8,128]{1,0:T(8,128)S(1)} %pack.1), channel_id=1, source_target_pairs={{0,16},{1,17},{2,18},{3,19},{4,20},{5,21},{6,22},{7,23},{8,56},{9,... | collective-permute-start | bytes 12296 | tf_op jit(solution)/shard_map/ppermute | solution.py:31
  44.4 3.1 %back.3 = (bf16[8,4,32,576]{3,2,1,0:T(8,128)(2,1)S(1)}, bf16[8,4,32,576]{3,2,1,0:T(8,128)(2,1)S(1)}) custom-call(s32[1]{0:T(128)} %bitcast.me_ref.refs_0_, bf16[256,1024]{1,0:T(8,128)(2,1)S(1)} %get-tuple-element.108.rows_ref, bf16[4608,1024]{1,0:T(8,128)(2,1)S(1)} %get-tuple-element.93.refs_10_.head_ref), custom_call_target="tpu_custom_call" | custom-call | flops 2415919104 | bytes 9437184 | tf_op jit(solution)/shard_map/back/pallas_call | solution.py:195
  48.1 1.7 %collective-permute-start.18 = (f32[8,128]{1,0:T(8,128)S(1)}, f32[8,128]{1,0:T(8,128)S(1)}, u32[]{:S(2)}, u32[]{:S(2)}) collective-permute-start(f32[8,128]{1,0:T(8,128)S(1)} %add.31), channel_id=1, source_target_pairs={{0,48},{1,49},{2,50},{3,51},{4,52},{5,53},{6,54},{7,55},{8,24},{9,... | collective-permute-start | bytes 12296 | tf_op jit(solution)/shard_map/ppermute | solution.py:31
  49.7 3.2 %collective-permute-done.18 = f32[8,128]{1,0:T(8,128)S(1)} collective-permute-done((f32[8,128]{1,0:T(8,128)S(1)}, f32[8,128]{1,0:T(8,128)S(1)}, u32[]{:S(2)}, u32[]{:S(2)}) %collective-permute-start.18) | collective-permute-done | bytes 4128 | tf_op jit(solution)/shard_map/ppermute | solution.py:31
  53.7 3.1 %collective-permute-start.28 = (bf16[2,2,2,2,2,32,576]{6,5,4,3,2,1,0:T(8,128)(2,1)S(1)}, bf16[2,2,2,2,2,32,576]{6,5,4,3,2,1,0:T(8,128)(2,1)S(1)}, u32[]{:S(2)}, u32[]{:S(2)}) collective-permute-start(bf16[2,2,2,2,2,32,576]{6,5,4,3,2,1,0:T(8,128)(2,1)S(1)} %get-tuple-element.127), channel_id=1, source_target_pairs={{0,3},{1,2},{2,1},{3,0},{4,7},{5,6},{6,5},{7,4},{8,9},{9,8},{10,11... | collective-permute-start | bytes 3538952 | tf_op jit(solution)/shard_map/ppermute | solution.py:31
  56.8 1.7 %collective-permute-start.29 = (bf16[2,2,2,2,2,32,576]{6,5,4,3,2,1,0:T(8,128)(2,1)S(1)}, bf16[2,2,2,2,2,32,576]{6,5,4,3,2,1,0:T(8,128)(2,1)S(1)}, u32[]{:S(2)}, u32[]{:S(2)}) collective-permute-start(bf16[2,2,2,2,2,32,576]{6,5,4,3,2,1,0:T(8,128)(2,1)S(1)} %get-tuple-element.128), channel_id=1, source_target_pairs={{0,48},{1,49},{2,50},{3,51},{4,52},{5,53},{6,54},{7,55},{8,24},{9,... | collective-permute-start | bytes 3538952 | tf_op jit(solution)/shard_map/ppermute | solution.py:31
  58.5 1.2 %collective-permute-done.20 = f32[8,128]{1,0:T(8,128)S(1)} collective-permute-done((f32[8,128]{1,0:T(8,128)S(1)}, f32[8,128]{1,0:T(8,128)S(1)}, u32[]{:S(2)}, u32[]{:S(2)}) %collective-permute-start.20) | collective-permute-done | bytes 4128 | tf_op jit(solution)/shard_map/ppermute | solution.py:31
  59.6 1.5 %collective-permute-start.21 = (f32[8,128]{1,0:T(8,128)S(1)}, f32[8,128]{1,0:T(8,128)S(1)}, u32[]{:S(2)}, u32[]{:S(2)}) collective-permute-start(f32[8,128]{1,0:T(8,128)S(1)} %add.33), channel_id=1, source_target_pairs={{0,4},{1,5},{2,6},{3,7},{4,0},{5,1},{6,2},{7,3},{8,12},{9,13},{10,... | collective-permute-start | bytes 12296 | tf_op jit(solution)/shard_map/ppermute | solution.py:31
  61.2 3.6 %collective-permute-start.22 = (f32[8,128]{1,0:T(8,128)S(1)}, f32[8,128]{1,0:T(8,128)S(1)}, u32[]{:S(2)}, u32[]{:S(2)}) collective-permute-start(f32[8,128]{1,0:T(8,128)S(1)} %add.33), channel_id=1, source_target_pairs={{0,64},{1,65},{2,66},{3,67},{4,68},{5,69},{6,70},{7,71},{8,72},{9,... | collective-permute-start | bytes 12296 | tf_op jit(solution)/shard_map/ppermute | solution.py:31
  64.8 1.6 %collective-permute-done.22 = f32[8,128]{1,0:T(8,128)S(1)} collective-permute-done((f32[8,128]{1,0:T(8,128)S(1)}, f32[8,128]{1,0:T(8,128)S(1)}, u32[]{:S(2)}, u32[]{:S(2)}) %collective-permute-start.22) | collective-permute-done | bytes 4128 | tf_op jit(solution)/shard_map/ppermute | solution.py:31
  66.4 3.2 %collective-permute-done.23 = f32[8,128]{1,0:T(8,128)S(1)} collective-permute-done((f32[8,128]{1,0:T(8,128)S(1)}, f32[8,128]{1,0:T(8,128)S(1)}, u32[]{:S(2)}, u32[]{:S(2)}) %collective-permute-start.23) | collective-permute-done | bytes 4128 | tf_op jit(solution)/shard_map/ppermute | solution.py:31
  70.8 2.9 %collective-permute-start.26 = (f32[8,128]{1,0:T(8,128)S(1)}, f32[8,128]{1,0:T(8,128)S(1)}, u32[]{:S(2)}, u32[]{:S(2)}) collective-permute-start(f32[8,128]{1,0:T(8,128)S(1)} %add_add_fusion.1), channel_id=1, source_target_pairs={{0,2},{1,3},{2,0},{3,1},{4,6},{5,7},{6,4},{7,5},{8,10},{9,11},{10,... | collective-permute-start | bytes 12296 | tf_op jit(solution)/shard_map/ppermute | solution.py:31
  74.5 1.3 %collective-permute-done.26 = f32[8,128]{1,0:T(8,128)S(1)} collective-permute-done((f32[8,128]{1,0:T(8,128)S(1)}, f32[8,128]{1,0:T(8,128)S(1)}, u32[]{:S(2)}, u32[]{:S(2)}) %collective-permute-start.26) | collective-permute-done | bytes 4128 | tf_op jit(solution)/shard_map/ppermute | solution.py:31
  76.5 1.6 %collective-permute-start.30 = (bf16[2,2,2,2,16,576]{5,4,3,2,1,0:T(8,128)(2,1)S(1)}, bf16[2,2,2,2,16,576]{5,4,3,2,1,0:T(8,128)(2,1)S(1)}, u32[]{:S(2)}, u32[]{:S(2)}) collective-permute-start(bf16[2,2,2,2,16,576]{5,4,3,2,1,0:T(8,128)(2,1)S(1)} %get-tuple-element.139), channel_id=1, source_target_pairs={{0,48},{1,49},{2,50},{3,51},{4,52},{5,53},{6,54},{7,55},{8,24},{9,... | collective-permute-start | bytes 884744 | tf_op jit(solution)/shard_map/ppermute | solution.py:31
  78.5 2.3 %collective-permute-start.31 = (bf16[2,2,2,2,16,576]{5,4,3,2,1,0:T(8,128)(2,1)S(1)}, bf16[2,2,2,2,16,576]{5,4,3,2,1,0:T(8,128)(2,1)S(1)}, u32[]{:S(2)}, u32[]{:S(2)}) collective-permute-start(bf16[2,2,2,2,16,576]{5,4,3,2,1,0:T(8,128)(2,1)S(1)} %get-tuple-element.142), channel_id=1, source_target_pairs={{0,3},{1,2},{2,1},{3,0},{4,7},{5,6},{6,5},{7,4},{8,9},{9,8},{10,11... | collective-permute-start | bytes 884744 | tf_op jit(solution)/shard_map/ppermute | solution.py:31
  81.6 5.2 %head_gradient_low.1.started_ref = bf16[4608,1024]{1,0:T(8,128)(2,1)} custom-call(bf16[256,4608]{1,0:T(8,128)(2,1)S(1)} %get-tuple-element.143.low_ref, bf16[256,4608]{1,0:T(8,128)(2,1)S(1)} %get-tuple-element.144.high_ref, bf16[512,1024]{1,0:T(8,128)(2,1)S(1)} %dlogits.1.dlog_ref), custom_call_target="tpu_custom_call" | custom-call | flops 2415919104 | bytes 4718592 | tf_op jit(solution)/shard_map/head_gradient_low/pallas_call | solution.py:378
  87.7 3.0 %collective-permute-start.34 = (bf16[2,2,32,576]{3,2,1,0:T(8,128)(2,1)S(1)}, bf16[2,2,32,576]{3,2,1,0:T(8,128)(2,1)S(1)}, u32[]{:S(2)}, u32[]{:S(2)}) collective-permute-start(bf16[2,2,32,576]{3,2,1,0:T(8,128)(2,1)S(1)} %get-tuple-element.153), channel_id=1, source_target_pairs={{0,17},{1,16},{2,19},{3,18},{4,21},{5,20},{6,23},{7,22},{8,59},{9,... | collective-permute-start | bytes 442376 | tf_op jit(solution)/shard_map/ppermute | solution.py:31
  90.7 4.2 %head_gradient_high.1 = bf16[4608,1024]{1,0:T(8,128)(2,1)} custom-call(bf16[256,4608]{1,0:T(8,128)(2,1)S(1)} %get-tuple-element.143.low_ref, bf16[256,4608]{1,0:T(8,128)(2,1)S(1)} %get-tuple-element.144.high_ref, bf16[512,1024]{1,0:T(8,128)(2,1)S(1)} %dlogits.1.dlog_ref, bf16[4608,1024]{1,0:T(8,128)(2,1)} %head_gradient_low.1.started_ref), custom_call_target="tpu_custom_call", output_to_operand_aliasing={{}: (3, {})} | custom-call | flops 2415919104 | bytes 4718592 | tf_op jit(solution)/shard_map/head_gradient_high/pallas_call | solution.py:378
  95.0 2.2 %collective-permute-start.35 = (bf16[32,576]{1,0:T(8,128)(2,1)S(1)}, bf16[32,576]{1,0:T(8,128)(2,1)S(1)}, u32[]{:S(2)}, u32[]{:S(2)}) collective-permute-start(bf16[32,576]{1,0:T(8,128)(2,1)S(1)} %get-tuple-element.161), channel_id=1, source_target_pairs={{0,4},{1,5},{2,6},{3,7},{4,0},{5,1},{6,2},{7,3},{8,12},{9,13},{10,... | collective-permute-start | bytes 110600 | tf_op jit(solution)/shard_map/ppermute | solution.py:31
  97.2 3.7 %collective-permute-start.36 = (bf16[32,576]{1,0:T(8,128)(2,1)S(1)}, bf16[32,576]{1,0:T(8,128)(2,1)S(1)}, u32[]{:S(2)}, u32[]{:S(2)}) collective-permute-start(bf16[32,576]{1,0:T(8,128)(2,1)S(1)} %get-tuple-element.162), channel_id=1, source_target_pairs={{0,64},{1,65},{2,66},{3,67},{4,68},{5,69},{6,70},{7,71},{8,72},{9,... | collective-permute-start | bytes 110600 | tf_op jit(solution)/shard_map/ppermute | solution.py:31
  101.6 1.8 %collective-permute-done.36.refs_2_ = bf16[32,576]{1,0:T(8,128)(2,1)S(1)} collective-permute-done((bf16[32,576]{1,0:T(8,128)(2,1)S(1)}, bf16[32,576]{1,0:T(8,128)(2,1)S(1)}, u32[]{:S(2)}, u32[]{:S(2)}) %collective-permute-start.36) | collective-permute-done | bytes 36896 | tf_op jit(solution)/shard_map/ppermute | solution.py:31
  103.4 2.8 %collective-permute-done.37.refs_3_ = bf16[32,576]{1,0:T(8,128)(2,1)S(1)} collective-permute-done((bf16[32,576]{1,0:T(8,128)(2,1)S(1)}, bf16[32,576]{1,0:T(8,128)(2,1)S(1)}, u32[]{:S(2)}, u32[]{:S(2)}) %collective-permute-start.37) | collective-permute-done | bytes 36896 | tf_op jit(solution)/shard_map/ppermute | solution.py:31
  (68 shorter events, 14.5 us)
Async XLA Ops:
  0.6 16.8 %collective-permute-start = (bf16[32,4608]{1,0:T(8,128)(2,1)}, bf16[32,4608]{1,0:T(8,128)(2,1)S(1)}, u32[]{:S(2)}, u32[]{:S(2)}) collective-permute-start(bf16[32,4608]{1,0:T(8,128)(2,1)} %refs_1_.1), channel_id=1, source_target_pairs={{0,16},{1,17},{2,18},{3,19},{4,20},{5,21},{6,22},{7,23},{8,56},{9,... | collective-permute-start | bytes 884744 | tf_op jit(solution)/shard_map/ppermute | solution.py:31
  2.3 15.2 %collective-permute-start.1 = (bf16[32,4608]{1,0:T(8,128)(2,1)}, bf16[32,4608]{1,0:T(8,128)(2,1)S(1)}, u32[]{:S(2)}, u32[]{:S(2)}) collective-permute-start(bf16[32,4608]{1,0:T(8,128)(2,1)} %refs_1_.1), channel_id=1, source_target_pairs={{0,48},{1,49},{2,50},{3,51},{4,52},{5,53},{6,54},{7,55},{8,24},{9,... | collective-permute-start | bytes 884744 | tf_op jit(solution)/shard_map/ppermute | solution.py:31
  4.4 14.0 %collective-permute-start.2 = (bf16[32,4608]{1,0:T(8,128)(2,1)}, bf16[32,4608]{1,0:T(8,128)(2,1)S(1)}, u32[]{:S(2)}, u32[]{:S(2)}) collective-permute-start(bf16[32,4608]{1,0:T(8,128)(2,1)} %refs_1_.1), channel_id=1, source_target_pairs={{0,32},{1,33},{2,34},{3,35},{4,36},{5,37},{6,38},{7,39},{8,40},{9,... | collective-permute-start | bytes 884744 | tf_op jit(solution)/shard_map/ppermute | solution.py:31
  5.0 13.3 %collective-permute-start.3 = (bf16[32,4608]{1,0:T(8,128)(2,1)}, bf16[32,4608]{1,0:T(8,128)(2,1)S(1)}, u32[]{:S(2)}, u32[]{:S(2)}) collective-permute-start(bf16[32,4608]{1,0:T(8,128)(2,1)} %refs_1_.1), channel_id=1, source_target_pairs={{0,68},{1,69},{2,70},{3,71},{4,64},{5,65},{6,66},{7,67},{8,76},{9,... | collective-permute-start | bytes 884744 | tf_op jit(solution)/shard_map/ppermute | solution.py:31
  18.4 18.8 %collective-permute-start.11 = (bf16[8,4,32,576]{3,2,1,0:T(8,128)(2,1)S(1)}, bf16[8,4,32,576]{3,2,1,0:T(8,128)(2,1)S(1)}, u32[]{:S(2)}, u32[]{:S(2)}) collective-permute-start(bf16[8,4,32,576]{3,2,1,0:T(8,128)(2,1)S(1)} %get-tuple-element.98), channel_id=1, source_target_pairs={{0,8},{1,9},{2,10},{3,11},{4,12},{5,13},{6,14},{7,15},{8,0},{9,1},... | collective-permute-start | bytes 3538952 | tf_op jit(solution)/shard_map/ppermute | solution.py:31
  18.4 18.8 %collective-permute-start.12 = (bf16[8,4,32,576]{3,2,1,0:T(8,128)(2,1)S(1)}, bf16[8,4,32,576]{3,2,1,0:T(8,128)(2,1)S(1)}, u32[]{:S(2)}, u32[]{:S(2)}) collective-permute-start(bf16[8,4,32,576]{3,2,1,0:T(8,128)(2,1)S(1)} %get-tuple-element.99), channel_id=1, source_target_pairs={{0,8},{1,9},{2,10},{3,11},{4,12},{5,13},{6,14},{7,15},{8,0},{9,1},... | collective-permute-start | bytes 3538952 | tf_op jit(solution)/shard_map/ppermute | solution.py:31
  18.9 4.8 %collective-permute-start.4 = (bf16[32,4608]{1,0:T(8,128)(2,1)S(1)}, bf16[32,4608]{1,0:T(8,128)(2,1)S(1)}, u32[]{:S(2)}, u32[]{:S(2)}) collective-permute-start(bf16[32,4608]{1,0:T(8,128)(2,1)S(1)} %copy-done), channel_id=1, source_target_pairs={{0,8},{1,9},{2,10},{3,11},{4,12},{5,13},{6,14},{7,15},{8,0},{9,1},... | collective-permute-start | bytes 884744 | tf_op jit(solution)/shard_map/ppermute | solution.py:31
  18.9 5.2 %collective-permute-start.5 = (bf16[32,4608]{1,0:T(8,128)(2,1)S(1)}, bf16[32,4608]{1,0:T(8,128)(2,1)S(1)}, u32[]{:S(2)}, u32[]{:S(2)}) collective-permute-start(bf16[32,4608]{1,0:T(8,128)(2,1)S(1)} %collective-permute-done.refs_2_), channel_id=1, source_target_pairs={{0,8},{1,9},{2,10},{3,11},{4,12},{5,13},{6,14},{7,15},{8,0},{9,1},... | collective-permute-start | bytes 884744 | tf_op jit(solution)/shard_map/ppermute | solution.py:31
  19.4 5.3 %collective-permute-start.6 = (bf16[32,4608]{1,0:T(8,128)(2,1)S(1)}, bf16[32,4608]{1,0:T(8,128)(2,1)S(1)}, u32[]{:S(2)}, u32[]{:S(2)}) collective-permute-start(bf16[32,4608]{1,0:T(8,128)(2,1)S(1)} %collective-permute-done.1.refs_3_), channel_id=1, source_target_pairs={{0,8},{1,9},{2,10},{3,11},{4,12},{5,13},{6,14},{7,15},{8,0},{9,1},... | collective-permute-start | bytes 884744 | tf_op jit(solution)/shard_map/ppermute | solution.py:31
  24.1 9.3 %collective-permute-start.8 = (bf16[32,4608]{1,0:T(8,128)(2,1)S(1)}, bf16[32,4608]{1,0:T(8,128)(2,1)S(1)}, u32[]{:S(2)}, u32[]{:S(2)}) collective-permute-start(bf16[32,4608]{1,0:T(8,128)(2,1)S(1)} %collective-permute-done.3.refs_1_), channel_id=1, source_target_pairs={{0,16},{1,17},{2,18},{3,19},{4,20},{5,21},{6,22},{7,23},{8,56},{9,... | collective-permute-start | bytes 884744 | tf_op jit(solution)/shard_map/ppermute | solution.py:31
  24.7 11.8 %collective-permute-start.9 = (bf16[32,4608]{1,0:T(8,128)(2,1)S(1)}, bf16[32,4608]{1,0:T(8,128)(2,1)S(1)}, u32[]{:S(2)}, u32[]{:S(2)}) collective-permute-start(bf16[32,4608]{1,0:T(8,128)(2,1)S(1)} %collective-permute-done.3.refs_1_), channel_id=1, source_target_pairs={{0,48},{1,49},{2,50},{3,51},{4,52},{5,53},{6,54},{7,55},{8,24},{9,... | collective-permute-start | bytes 884744 | tf_op jit(solution)/shard_map/ppermute | solution.py:31
  26.8 10.4 %collective-permute-start.10 = (bf16[32,4608]{1,0:T(8,128)(2,1)S(1)}, bf16[32,4608]{1,0:T(8,128)(2,1)S(1)}, u32[]{:S(2)}, u32[]{:S(2)}) collective-permute-start(bf16[32,4608]{1,0:T(8,128)(2,1)S(1)} %collective-permute-done.2.refs_4_), channel_id=1, source_target_pairs={{0,68},{1,69},{2,70},{3,71},{4,64},{5,65},{6,66},{7,67},{8,76},{9,... | collective-permute-start | bytes 884744 | tf_op jit(solution)/shard_map/ppermute | solution.py:31
  33.4 4.3 %collective-permute-start.13 = (bf16[32,4608]{1,0:T(8,128)(2,1)S(1)}, bf16[32,4608]{1,0:T(8,128)(2,1)S(1)}, u32[]{:S(2)}, u32[]{:S(2)}) collective-permute-start(bf16[32,4608]{1,0:T(8,128)(2,1)S(1)} %collective-permute-done.3.refs_1_), channel_id=1, source_target_pairs={{0,8},{1,9},{2,10},{3,11},{4,12},{5,13},{6,14},{7,15},{8,0},{9,1},... | collective-permute-start | bytes 884744 | tf_op jit(solution)/shard_map/ppermute | solution.py:31
  42.8 4.7 %collective-permute-start.17 = (f32[8,128]{1,0:T(8,128)S(1)}, f32[8,128]{1,0:T(8,128)S(1)}, u32[]{:S(2)}, u32[]{:S(2)}) collective-permute-start(f32[8,128]{1,0:T(8,128)S(1)} %pack.1), channel_id=1, source_target_pairs={{0,16},{1,17},{2,18},{3,19},{4,20},{5,21},{6,22},{7,23},{8,56},{9,... | collective-permute-start | bytes 12296 | tf_op jit(solution)/shard_map/ppermute | solution.py:31
  47.5 5.4 %collective-permute-start.19 = (bf16[8,4,32,576]{3,2,1,0:T(8,128)(2,1)S(1)}, bf16[8,4,32,576]{3,2,1,0:T(8,128)(2,1)S(1)}, u32[]{:S(2)}, u32[]{:S(2)}) collective-permute-start(bf16[8,4,32,576]{3,2,1,0:T(8,128)(2,1)S(1)} %get-tuple-element.111), channel_id=1, source_target_pairs={{0,8},{1,9},{2,10},{3,11},{4,12},{5,13},{6,14},{7,15},{8,0},{9,1},... | collective-permute-start | bytes 3538952 | tf_op jit(solution)/shard_map/ppermute | solution.py:31
  47.8 5.1 %collective-permute-start.27 = (bf16[8,4,32,576]{3,2,1,0:T(8,128)(2,1)S(1)}, bf16[8,4,32,576]{3,2,1,0:T(8,128)(2,1)S(1)}, u32[]{:S(2)}, u32[]{:S(2)}) collective-permute-start(bf16[8,4,32,576]{3,2,1,0:T(8,128)(2,1)S(1)} %get-tuple-element.120), channel_id=1, source_target_pairs={{0,8},{1,9},{2,10},{3,11},{4,12},{5,13},{6,14},{7,15},{8,0},{9,1},... | collective-permute-start | bytes 3538952 | tf_op jit(solution)/shard_map/ppermute | solution.py:31
  48.1 4.8 %collective-permute-start.18 = (f32[8,128]{1,0:T(8,128)S(1)}, f32[8,128]{1,0:T(8,128)S(1)}, u32[]{:S(2)}, u32[]{:S(2)}) collective-permute-start(f32[8,128]{1,0:T(8,128)S(1)} %add.31), channel_id=1, source_target_pairs={{0,48},{1,49},{2,50},{3,51},{4,52},{5,53},{6,54},{7,55},{8,24},{9,... | collective-permute-start | bytes 12296 | tf_op jit(solution)/shard_map/ppermute | solution.py:31
  53.7 22.2 %collective-permute-start.28 = (bf16[2,2,2,2,2,32,576]{6,5,4,3,2,1,0:T(8,128)(2,1)S(1)}, bf16[2,2,2,2,2,32,576]{6,5,4,3,2,1,0:T(8,128)(2,1)S(1)}, u32[]{:S(2)}, u32[]{:S(2)}) collective-permute-start(bf16[2,2,2,2,2,32,576]{6,5,4,3,2,1,0:T(8,128)(2,1)S(1)} %get-tuple-element.127), channel_id=1, source_target_pairs={{0,3},{1,2},{2,1},{3,0},{4,7},{5,6},{6,5},{7,4},{8,9},{9,8},{10,11... | collective-permute-start | bytes 3538952 | tf_op jit(solution)/shard_map/ppermute | solution.py:31
  56.8 19.1 %collective-permute-start.29 = (bf16[2,2,2,2,2,32,576]{6,5,4,3,2,1,0:T(8,128)(2,1)S(1)}, bf16[2,2,2,2,2,32,576]{6,5,4,3,2,1,0:T(8,128)(2,1)S(1)}, u32[]{:S(2)}, u32[]{:S(2)}) collective-permute-start(bf16[2,2,2,2,2,32,576]{6,5,4,3,2,1,0:T(8,128)(2,1)S(1)} %get-tuple-element.128), channel_id=1, source_target_pairs={{0,48},{1,49},{2,50},{3,51},{4,52},{5,53},{6,54},{7,55},{8,24},{9,... | collective-permute-start | bytes 3538952 | tf_op jit(solution)/shard_map/ppermute | solution.py:31
  59.6 5.1 %collective-permute-start.21 = (f32[8,128]{1,0:T(8,128)S(1)}, f32[8,128]{1,0:T(8,128)S(1)}, u32[]{:S(2)}, u32[]{:S(2)}) collective-permute-start(f32[8,128]{1,0:T(8,128)S(1)} %add.33), channel_id=1, source_target_pairs={{0,4},{1,5},{2,6},{3,7},{4,0},{5,1},{6,2},{7,3},{8,12},{9,13},{10,... | collective-permute-start | bytes 12296 | tf_op jit(solution)/shard_map/ppermute | solution.py:31
  61.2 5.2 %collective-permute-start.22 = (f32[8,128]{1,0:T(8,128)S(1)}, f32[8,128]{1,0:T(8,128)S(1)}, u32[]{:S(2)}, u32[]{:S(2)}) collective-permute-start(f32[8,128]{1,0:T(8,128)S(1)} %add.33), channel_id=1, source_target_pairs={{0,64},{1,65},{2,66},{3,67},{4,68},{5,69},{6,70},{7,71},{8,72},{9,... | collective-permute-start | bytes 12296 | tf_op jit(solution)/shard_map/ppermute | solution.py:31
  64.8 4.8 %collective-permute-start.23 = (f32[8,128]{1,0:T(8,128)S(1)}, f32[8,128]{1,0:T(8,128)S(1)}, u32[]{:S(2)}, u32[]{:S(2)}) collective-permute-start(f32[8,128]{1,0:T(8,128)S(1)} %add.33), channel_id=1, source_target_pairs={{0,68},{1,69},{2,70},{3,71},{4,64},{5,65},{6,66},{7,67},{8,76},{9,... | collective-permute-start | bytes 12296 | tf_op jit(solution)/shard_map/ppermute | solution.py:31
  69.7 4.8 %collective-permute-start.25 = (f32[8,128]{1,0:T(8,128)S(1)}, f32[8,128]{1,0:T(8,128)S(1)}, u32[]{:S(2)}, u32[]{:S(2)}) collective-permute-start(f32[8,128]{1,0:T(8,128)S(1)} %add_add_fusion.1), channel_id=1, source_target_pairs={{0,3},{1,2},{2,1},{3,0},{4,7},{5,6},{6,5},{7,4},{8,9},{9,8},{10,11... | collective-permute-start | bytes 12296 | tf_op jit(solution)/shard_map/ppermute | solution.py:31
  70.8 5.1 %collective-permute-start.26 = (f32[8,128]{1,0:T(8,128)S(1)}, f32[8,128]{1,0:T(8,128)S(1)}, u32[]{:S(2)}, u32[]{:S(2)}) collective-permute-start(f32[8,128]{1,0:T(8,128)S(1)} %add_add_fusion.1), channel_id=1, source_target_pairs={{0,2},{1,3},{2,0},{3,1},{4,6},{5,7},{6,4},{7,5},{8,10},{9,11},{10,... | collective-permute-start | bytes 12296 | tf_op jit(solution)/shard_map/ppermute | solution.py:31
  76.5 10.2 %collective-permute-start.30 = (bf16[2,2,2,2,16,576]{5,4,3,2,1,0:T(8,128)(2,1)S(1)}, bf16[2,2,2,2,16,576]{5,4,3,2,1,0:T(8,128)(2,1)S(1)}, u32[]{:S(2)}, u32[]{:S(2)}) collective-permute-start(bf16[2,2,2,2,16,576]{5,4,3,2,1,0:T(8,128)(2,1)S(1)} %get-tuple-element.139), channel_id=1, source_target_pairs={{0,48},{1,49},{2,50},{3,51},{4,52},{5,53},{6,54},{7,55},{8,24},{9,... | collective-permute-start | bytes 884744 | tf_op jit(solution)/shard_map/ppermute | solution.py:31
  78.5 8.6 %collective-permute-start.31 = (bf16[2,2,2,2,16,576]{5,4,3,2,1,0:T(8,128)(2,1)S(1)}, bf16[2,2,2,2,16,576]{5,4,3,2,1,0:T(8,128)(2,1)S(1)}, u32[]{:S(2)}, u32[]{:S(2)}) collective-permute-start(bf16[2,2,2,2,16,576]{5,4,3,2,1,0:T(8,128)(2,1)S(1)} %get-tuple-element.142), channel_id=1, source_target_pairs={{0,3},{1,2},{2,1},{3,0},{4,7},{5,6},{6,5},{7,4},{8,9},{9,8},{10,11... | collective-permute-start | bytes 884744 | tf_op jit(solution)/shard_map/ppermute | solution.py:31
  87.1 7.8 %collective-permute-start.32 = (bf16[2,2,32,576]{3,2,1,0:T(8,128)(2,1)S(1)}, bf16[2,2,32,576]{3,2,1,0:T(8,128)(2,1)S(1)}, u32[]{:S(2)}, u32[]{:S(2)}) collective-permute-start(bf16[2,2,32,576]{3,2,1,0:T(8,128)(2,1)S(1)} %get-tuple-element.151), channel_id=1, source_target_pairs={{0,16},{1,17},{2,18},{3,19},{4,20},{5,21},{6,22},{7,23},{8,56},{9,... | collective-permute-start | bytes 442376 | tf_op jit(solution)/shard_map/ppermute | solution.py:31
  87.2 7.7 %collective-permute-start.33 = (bf16[2,2,32,576]{3,2,1,0:T(8,128)(2,1)S(1)}, bf16[2,2,32,576]{3,2,1,0:T(8,128)(2,1)S(1)}, u32[]{:S(2)}, u32[]{:S(2)}) collective-permute-start(bf16[2,2,32,576]{3,2,1,0:T(8,128)(2,1)S(1)} %get-tuple-element.152), channel_id=1, source_target_pairs={{0,1},{1,0},{2,3},{3,2},{4,5},{5,4},{6,7},{7,6},{8,11},{9,10},{10,... | collective-permute-start | bytes 442376 | tf_op jit(solution)/shard_map/ppermute | solution.py:31
  87.7 7.2 %collective-permute-start.34 = (bf16[2,2,32,576]{3,2,1,0:T(8,128)(2,1)S(1)}, bf16[2,2,32,576]{3,2,1,0:T(8,128)(2,1)S(1)}, u32[]{:S(2)}, u32[]{:S(2)}) collective-permute-start(bf16[2,2,32,576]{3,2,1,0:T(8,128)(2,1)S(1)} %get-tuple-element.153), channel_id=1, source_target_pairs={{0,17},{1,16},{2,19},{3,18},{4,21},{5,20},{6,23},{7,22},{8,59},{9,... | collective-permute-start | bytes 442376 | tf_op jit(solution)/shard_map/ppermute | solution.py:31
  95.0 6.6 %collective-permute-start.35 = (bf16[32,576]{1,0:T(8,128)(2,1)S(1)}, bf16[32,576]{1,0:T(8,128)(2,1)S(1)}, u32[]{:S(2)}, u32[]{:S(2)}) collective-permute-start(bf16[32,576]{1,0:T(8,128)(2,1)S(1)} %get-tuple-element.161), channel_id=1, source_target_pairs={{0,4},{1,5},{2,6},{3,7},{4,0},{5,1},{6,2},{7,3},{8,12},{9,13},{10,... | collective-permute-start | bytes 110600 | tf_op jit(solution)/shard_map/ppermute | solution.py:31
  97.2 6.1 %collective-permute-start.36 = (bf16[32,576]{1,0:T(8,128)(2,1)S(1)}, bf16[32,576]{1,0:T(8,128)(2,1)S(1)}, u32[]{:S(2)}, u32[]{:S(2)}) collective-permute-start(bf16[32,576]{1,0:T(8,128)(2,1)S(1)} %get-tuple-element.162), channel_id=1, source_target_pairs={{0,64},{1,65},{2,66},{3,67},{4,68},{5,69},{6,70},{7,71},{8,72},{9,... | collective-permute-start | bytes 110600 | tf_op jit(solution)/shard_map/ppermute | solution.py:31
  100.9 5.2 %collective-permute-start.37 = (bf16[32,576]{1,0:T(8,128)(2,1)S(1)}, bf16[32,576]{1,0:T(8,128)(2,1)S(1)}, u32[]{:S(2)}, u32[]{:S(2)}) collective-permute-start(bf16[32,576]{1,0:T(8,128)(2,1)S(1)} %get-tuple-element.163), channel_id=1, source_target_pairs={{0,68},{1,69},{2,70},{3,71},{4,64},{5,65},{6,66},{7,67},{8,76},{9,... | collective-permute-start | bytes 110600 | tf_op jit(solution)/shard_map/ppermute | solution.py:31
  (7 other events, 23.7 us)

commit v3 on v2

--- a/solution.py
+++ b/solution.py
@@ -44,8 +44,7 @@
 def feature_slot(me, i, other):
     core = ((me >> 3) & 1) ^ other
     apart = (me & 3) ^ (i & 3)
-    slot = jnp.where(apart == 1 + 2 * core, 1, jnp.where(apart == 3 - 2 * core, 2, jnp.where(apart == 2, 3, 0)))
-    return (((me >> 2) & 1) ^ (i >> 2)) * 4 + slot
+    return jnp.where(apart == 1 + 2 * core, 1, jnp.where(apart == 3 - 2 * core, 2, jnp.where(apart == 2, 3, 0)))
 
 
 def call(kernel, ins, outs, scratch=(), flops=0, moved=0, mib=16, aliases={}):
@@ -178,8 +177,10 @@
     ).astype(bf16)
     for i in range(2):
         part = out[:, FEATURES * i : FEATURES * i + FEATURES]
-        mine_ref[feature_slot(me, 2 * n + i, 0)] = part[:128].reshape(4, 32, FEATURES)
-        mate_ref[feature_slot(me, 2 * n + i, 1)] = part[128:].reshape(4, 32, FEATURES)
+        block = 2 * n + i
+        spot = slice(FEATURES * (block // 4), FEATURES * (block // 4) + FEATURES)
+        mine_ref[feature_slot(me, block, 0), :, :, spot] = part[:128].reshape(4, 32, FEATURES)
+        mate_ref[feature_slot(me, block, 1), :, :, spot] = part[128:].reshape(4, 32, FEATURES)
 
 
 def back(me_ref, rows_ref, head_ref, mine_ref, mate_ref):
@@ -187,7 +188,7 @@
         back_part(me_ref[0], n, rows_ref[...], head_ref, mine_ref, mate_ref)
 
 
-BLOCKS = ("v", (8, 4, 32, FEATURES), bf16)
+BLOCKS = ("v", (4, 4, 32, 2 * FEATURES), bf16)
 BACK_COST = dict(flops=2 * 256 * D * WIDTH, moved=2 * D * WIDTH)
 
 
@@ -248,20 +249,18 @@
     parts, (p_keep, p_send, q_keep, q_send) = refs[:8], refs[8:]
     for zr in range(2):
         a_mine, a_got, g_mine, g_got = parts[4 * zr : 4 * zr + 4]
-        for zl in range(2):
-            for k in range(4):
-                b = 4 * zl + k
-                for x in range(4):
-                    p_at = (p_keep if k < 2 else p_send).at[x // 2, k % 2, x % 2, zr, zl]
-                    q_at = (q_keep if x < 2 else q_send).at[k // 2, k % 2, x % 2, zr, zl]
-                    for first, mine, got in ((0, a_mine, a_got), (16, g_mine, g_got)):
-                        total = mine[b, x] + got[b, x]
-                        p_at[first : first + 16] = total[:16]
-                        q_at[first : first + 16] = total[16:]
+        for k in range(4):
+            for x in range(4):
+                p_at = (p_keep if k < 2 else p_send).at[x // 2, k % 2, x % 2, zr]
+                q_at = (q_keep if x < 2 else q_send).at[k // 2, k % 2, x % 2, zr]
+                for first, mine, got in ((0, a_mine, a_got), (16, g_mine, g_got)):
+                    total = mine[k, x] + got[k, x]
+                    p_at[first : first + 16] = total[:16]
+                    q_at[first : first + 16] = total[16:]
 
 
 def run_fold(*parts):
-    return call(fold, "v" * 8, [("v", (2, 2, 2, 2, 2, 32, FEATURES), bf16)] * 4, moved=512 * D * 8)(*parts)
+    return call(fold, "v" * 8, [("v", (2, 2, 2, 2, 32, 2 * FEATURES), bf16)] * 4, moved=512 * D * 8)(*parts)
 
 
 def combine(first_row, slots, rest_ref, pick_ref, held, got, keep, out):
@@ -273,13 +272,10 @@
                     first = 128 * zr + 32 * x + first_row
                     rest = rest_ref[first : first + 16, :]
                     pick = pick_ref[first : first + 16, :]
-                    for zl in range(2):
-                        for start in range(0, FEATURES, 128):
-                            wide = min(128, FEATURES - start)
-                            at = (h, i, j, zr, zl, slice(None), slice(start, start + wide))
-                            both = (held[at] + got[at]).astype(f32)
-                            total = rest[:, :wide] * both[:16] + pick[:, :wide] * both[16:]
-                            target[at[1:]] = total.astype(bf16)
+                    for start in range(0, 2 * FEATURES, 128):
+                        at = (h, i, j, zr, slice(None), slice(start, start + 128))
+                        both = (held[at] + got[at]).astype(f32)
+                        target[at[1:]] = (rest * both[:16] + pick * both[16:]).astype(bf16)
 
 
 def combine_p(*refs):
@@ -291,28 +287,32 @@
 
 
 def run_combine(kernel, *parts):
-    half = ("v", (2, 2, 2, 2, 16, FEATURES), bf16)
+    half = ("v", (2, 2, 2, 16, 2 * FEATURES), bf16)
     return call(kernel, "v" * 4, [half, half], moved=1 << 22)(*parts)
 
 
 def join(p_keep, p_got, q_keep, q_got, *outs):
     for n, out in enumerate(outs):
-        out[:, :, :16] = p_keep[n // 2, n % 2] + p_got[n // 2, n % 2]
-        out[:, :, 16:] = q_keep[n // 2, n % 2] + q_got[n // 2, n % 2]
+        out[:, :16] = p_keep[n // 2, n % 2] + p_got[n // 2, n % 2]
+        out[:, 16:] = q_keep[n // 2, n % 2] + q_got[n // 2, n % 2]
 
 
 def run_join(*parts):
-    return call(join, "v" * 4, [("v", (2, 2, 32, FEATURES), bf16)] * 4, moved=1 << 22)(*parts)
-
-
-def split(*refs):
+    return call(join, "v" * 4, [("v", (2, 32, 2 * FEATURES), bf16)] * 4, moved=1 << 22)(*parts)
+
+
+def split(me_ref, *refs):
     terms, outs = refs[:4], refs[4:]
-    for z, out in enumerate(outs):
-        out[...] = sum(term[z // 2, z % 2].astype(f32) for term in terms).astype(bf16)
-
-
-def run_split(*parts):
-    return call(split, "vvvv", [("v", (32, FEATURES), bf16)] * 4, moved=1 << 20)(*parts)
+    low = ((me_ref[0] >> 2) & 1) == 0
+    for zr in range(2):
+        total = sum(term[zr].astype(f32) for term in terms)
+        halves = (total[:, :FEATURES], total[:, FEATURES:])
+        for zl in range(2):
+            outs[2 * zr + zl][...] = jnp.where(low, halves[zl], halves[1 - zl]).astype(bf16)
+
+
+def run_split(me, *parts):
+    return call(split, "svvvv", [("v", (32, FEATURES), bf16)] * 4, moved=1 << 20)(me, *parts)
 
 
 def finish(*refs):
@@ -403,33 +403,36 @@
     )
     a1, a2, a3, o0, g0_mine, g0_mate, g1_mine, g1_mate = tie(a1, a2, a3, o0, g0_mine, g0_mate, g1_mine, g1_mate)
     o1, o2, o3 = send(o0, X1), send(o0, X2), send(a3, ZH)
-    g0_got, g1_got = send(g0_mate, CORE), send(g1_mate, CORE)
     own_half = [hidden, a1, a2, a3]
     own_half += [send(piece, CORE) for piece in own_half]
     rows0, capped0, term0, total0, target0 = run_forward(forward_low, me, own_half, ids, head)
     o1, term0 = tie(o1, term0)
     a0_mine, a0_mate = run_back(me, term0, head)
-    o1, o2, o3, g0_got, g1_got, a0_mate = tie(o1, o2, o3, g0_got, g1_got, a0_mate)
+    o1, o2, o3, a0_mate = tie(o1, o2, o3, a0_mate)
     other_half = [o0, o1, o2, o3]
-    other_half += [send(piece, CORE) for piece in other_half]
+    *swapped, a0_mate = tie(*(send(piece, CORE) for piece in other_half), a0_mate)
+    other_half += swapped
+    a0_got = send(a0_mate, CORE)
     rows1, capped1, term1, total1, target1 = run_forward(forward_high, me, other_half, ids, head)
 
     def step(sums, *partners):
         got = tie(*(send(sums, partner) for partner in partners))
         return sums + sum(got)
 
+    total1, a0_got, g0_mate, g1_mate = tie(total1, a0_got, g0_mate, g1_mate)
+    g0_got, g1_got = send(g0_mate, CORE), send(g1_mate, CORE)
     sums = step(run_pack(me, total0, total1, target0, target1), X1)
     a1_mine, a1_mate = run_back(me, term1, head)
-    sums, a1_mate = tie(sums, a1_mate)
+    sums, a1_mate, g0_got, g1_got = tie(sums, a1_mate, g0_got, g1_got)
     a1_got = send(a1_mate, CORE)
     sums = step(sums, X2)
     sums, a1_got = tie(sums, a1_got)
     p_keep, p_send, q_keep, q_send = run_fold(
-        a0_mine, send(a0_mate, CORE), g0_mine, g0_got, a1_mine, a1_got, g1_mine, g1_got
+        a0_mine, a0_got, g0_mine, g0_got, a1_mine, a1_got, g1_mine, g1_got
     )
 
     p_got, q_got = send(p_send, Y2), send(q_send, X2)
-    sums = step(step(step(sums, CORE), ZL, Z2, ZH), Y1, Y2, Y3)
+    sums = step(step(step(step(sums, CORE), ZL), ZH), Y1, Y2, Y3)
     sums, p_got, q_got = tie(sums, p_got, q_got)
     log_total, own, rest, pick = run_unpack(me, sums, weight)
     p_keep, p_send = run_combine(combine_p, rest, pick, p_keep, p_got)
@@ -443,7 +446,7 @@
     got = [send(out, partner) for out, partner in zip(outs, (X1, Y1, XY1))]
     head_grad = run_head_gradient(head_gradient_high, rows0, rows1, dlog, (head_grad,))
     *got, head_grad = tie(*got, head_grad)
-    keep, *outs = run_split(keep, *got)
+    keep, *outs = run_split(me, keep, *got)
     z_got = tie(*(send(out, partner) for out, partner in zip(outs, (ZL, Z2, ZH))))
     hidden_grad = run_finish(keep, *z_got)
     return (own[:, 0], head_grad, hidden_grad)

time: 107 us -> 101 us (0.944)
  starting transfers between devices: 47.6 us -> 39 us
  waiting for transfers between devices: 24.2 us -> 27.7 us
    ppermute x38 -> x37, starting transfers between devices: 47.6 us -> 39 us  [send(): return lax.ppermute(array, AXES, partner)]
    ppermute x38 -> x37, waiting for transfers between devices: 24.2 us -> 27.7 us  [send(): return lax.ppermute(array, AXES, partner)]
  transfers between devices with their start and end apart: 38 -> 37, of which waited for: 16 -> 18; matrix products, arithmetic and copies ran while one was open for 1% -> 1% of each run, Pallas kernels for 26% -> 30%
where the time goes in v3:
time: 101 us
  starting transfers between devices  39 us (39%)
  Pallas kernels  33 us (33%)
  waiting for transfers between devices  27.7 us (27%)
    ppermute x37, starting transfers between devices, send(): return lax.ppermute(array, AXES, partner)  39 us
    ppermute x37, waiting for transfers between devices, send(): return lax.ppermute(array, AXES, partner)  27.7 us
    pallas_call x2, Pallas kernels, run_head_gradient(): call(kernel, 'vvv' + 'h' * len(started), [('h', (D, WIDTH), bf16)], scrat...  9.39 us
    pallas_call x1, Pallas kernels, run_begin(): call(begin, 'shhh', [BLOCKS] * 4 + [('v', (D, WIDTH), bf16), column, colu...  8.25 us
    pallas_call x2, Pallas kernels, run_forward(): call(kernel, 's' + 'v' * 10, [('v', (256, D), bf16), ('v', (256, WIDTH),...  5.97 us
    pallas_call x2, Pallas kernels, run_back(): return call(back, 'svv', [BLOCKS, BLOCKS], **BACK_COST)(me, rows, head)  5.87 us
  transfers between devices with their start and end apart: 37, of which 18 were waited for; matrix products, arithmetic and copies ran while one was open for 1% of the time, Pallas kernels for 30%

profile of v3, /device:TPU:0, one launch (start us, length us, event | category | flops | bytes accessed | tf_op | source)
XLA Modules:
  0.0 101.2 jit_solution(3650120729318563139)
XLA Ops:
  0.6 4.2 %collective-permute-start.3 = (bf16[32,4608]{1,0:T(8,128)(2,1)}, bf16[32,4608]{1,0:T(8,128)(2,1)S(1)}, u32[]{:S(2)}, u32[]{:S(2)}) collective-permute-start(bf16[32,4608]{1,0:T(8,128)(2,1)} %refs_1_.1), channel_id=1, source_target_pairs={{0,68},{1,69},{2,70},{3,71},{4,64},{5,65},{6,66},{7,67},{8,76},{9,... | collective-permute-start | bytes 884744 | tf_op jit(solution)/shard_map/ppermute | solution.py:31
  4.8 3.0 %collective-permute-start.2 = (bf16[32,4608]{1,0:T(8,128)(2,1)}, bf16[32,4608]{1,0:T(8,128)(2,1)S(1)}, u32[]{:S(2)}, u32[]{:S(2)}) collective-permute-start(bf16[32,4608]{1,0:T(8,128)(2,1)} %refs_1_.1), channel_id=1, source_target_pairs={{0,32},{1,33},{2,34},{3,35},{4,36},{5,37},{6,38},{7,39},{8,40},{9,... | collective-permute-start | bytes 884744 | tf_op jit(solution)/shard_map/ppermute | solution.py:31
  7.9 1.1 %collective-permute-start.1 = (bf16[32,4608]{1,0:T(8,128)(2,1)}, bf16[32,4608]{1,0:T(8,128)(2,1)S(1)}, u32[]{:S(2)}, u32[]{:S(2)}) collective-permute-start(bf16[32,4608]{1,0:T(8,128)(2,1)} %refs_1_.1), channel_id=1, source_target_pairs={{0,48},{1,49},{2,50},{3,51},{4,52},{5,53},{6,54},{7,55},{8,24},{9,... | collective-permute-start | bytes 884744 | tf_op jit(solution)/shard_map/ppermute | solution.py:31
  9.0 8.2 %begin.1 = (bf16[4,4,32,1152]{3,2,1,0:T(8,128)(2,1)S(1)}, bf16[4,4,32,1152]{3,2,1,0:T(8,128)(2,1)S(1)}, bf16[4,4,32,1152]{3,2,1,0:T(8,128)(2,1)S(1)}, bf16[4,4,3...) custom-call(s32[1]{0:T(128)} %bitcast.me_ref.refs_0_, ...), custom_call_target="tpu_custom_call" | custom-call | flops 4831838208 | bytes 9437184 | tf_op jit(solution)/shard_map/begin/pallas_call | solution.py:231
  17.3 4.1 %collective-permute-done.1.refs_3_ = bf16[32,4608]{1,0:T(8,128)(2,1)S(1)} collective-permute-done((bf16[32,4608]{1,0:T(8,128)(2,1)}, bf16[32,4608]{1,0:T(8,128)(2,1)S(1)}, u32[]{:S(2)}, u32[]{:S(2)}) %collective-permute-start.1) | collective-permute-done | bytes 294944 | tf_op jit(solution)/shard_map/ppermute | solution.py:31
  22.0 1.4 %collective-permute-start.8 = (bf16[32,4608]{1,0:T(8,128)(2,1)S(1)}, bf16[32,4608]{1,0:T(8,128)(2,1)S(1)}, u32[]{:S(2)}, u32[]{:S(2)}) collective-permute-start(bf16[32,4608]{1,0:T(8,128)(2,1)S(1)} %collective-permute-done.3.refs_1_), channel_id=1, source_target_pairs={{0,16},{1,17},{2,18},{3,19},{4,20},{5,21},{6,22},{7,23},{8,56},{9,... | collective-permute-start | bytes 884744 | tf_op jit(solution)/shard_map/ppermute | solution.py:31
  23.8 1.1 %collective-permute-start.11 = (bf16[32,4608]{1,0:T(8,128)(2,1)S(1)}, bf16[32,4608]{1,0:T(8,128)(2,1)S(1)}, u32[]{:S(2)}, u32[]{:S(2)}) collective-permute-start(bf16[32,4608]{1,0:T(8,128)(2,1)S(1)} %collective-permute-done.3.refs_1_), channel_id=1, source_target_pairs={{0,8},{1,9},{2,10},{3,11},{4,12},{5,13},{6,14},{7,15},{8,0},{9,1},... | collective-permute-start | bytes 884744 | tf_op jit(solution)/shard_map/ppermute | solution.py:31
  24.9 1.2 %collective-permute-start.9 = (bf16[32,4608]{1,0:T(8,128)(2,1)S(1)}, bf16[32,4608]{1,0:T(8,128)(2,1)S(1)}, u32[]{:S(2)}, u32[]{:S(2)}) collective-permute-start(bf16[32,4608]{1,0:T(8,128)(2,1)S(1)} %collective-permute-done.3.refs_1_), channel_id=1, source_target_pairs={{0,48},{1,49},{2,50},{3,51},{4,52},{5,53},{6,54},{7,55},{8,24},{9,... | collective-permute-start | bytes 884744 | tf_op jit(solution)/shard_map/ppermute | solution.py:31
  26.2 3.0 %forward_low.1 = (bf16[256,4608]{1,0:T(8,128)(2,1)S(1)}, f32[256,1024]{1,0:T(8,128)S(1)}, bf16[256,1024]{1,0:T(8,128)(2,1)S(1)}, f32[256,128]{1,0:T(8,128)S(1)}, f32[256,128]{1,0:T(8,128)S(1)}) custom-call(s32[1]{0:T(128)} %bitcast.me_ref.refs_0_, bf16[32,4608]{1,0:T(8,128)(2,1)S(1)} %copy-done, bf16[32,4608]{1,0:T(8,128)(2,1)S(1)} %collective-permute-done.refs_2_, ...), custom_call_target="tpu_custom_call" | custom-call | flops 2415919104 | bytes 9437184 | tf_op jit(solution)/shard_map/forward_low/pallas_call | solution.py:116
  29.7 2.9 %back.2 = (bf16[4,4,32,1152]{3,2,1,0:T(8,128)(2,1)S(1)}, bf16[4,4,32,1152]{3,2,1,0:T(8,128)(2,1)S(1)}) custom-call(s32[1]{0:T(128)} %bitcast.me_ref.refs_0_, bf16[256,1024]{1,0:T(8,128)(2,1)S(1)} %get-tuple-element.104.rows_ref, bf16[4608,1024]{1,0:T(8,128)(2,1)S(1)} %get-tuple-element.99.refs_10_.head_ref), custom_call_target="tpu_custom_call" | custom-call | flops 2415919104 | bytes 9437184 | tf_op jit(solution)/shard_map/back/pallas_call | solution.py:196
  32.6 1.5 %collective-permute-done.10.refs_4_ = bf16[32,4608]{1,0:T(8,128)(2,1)S(1)} collective-permute-done((bf16[32,4608]{1,0:T(8,128)(2,1)S(1)}, bf16[32,4608]{1,0:T(8,128)(2,1)S(1)}, u32[]{:S(2)}, u32[]{:S(2)}) %collective-permute-start.10) | collective-permute-done | bytes 294944 | tf_op jit(solution)/shard_map/ppermute | solution.py:31
  36.8 3.0 %forward_high.1 = (bf16[256,4608]{1,0:T(8,128)(2,1)S(1)}, f32[256,1024]{1,0:T(8,128)S(1)}, bf16[256,1024]{1,0:T(8,128)(2,1)S(1)}, f32[256,128]{1,0:T(8,128)S(1)}, f32[256,128]{1,0:T(8,128)S(1)}) custom-call(s32[1]{0:T(128)} %bitcast.me_ref.refs_0_, bf16[32,4608]{1,0:T(8,128)(2,1)S(1)} %collective-permute-done.3.refs_1_, ...), custom_call_target="tpu_custom_call" | custom-call | flops 2415919104 | bytes 9437184 | tf_op jit(solution)/shard_map/forward_high/pallas_call | solution.py:116
  40.6 1.1 %collective-permute-start.16 = (f32[8,128]{1,0:T(8,128)S(1)}, f32[8,128]{1,0:T(8,128)S(1)}, u32[]{:S(2)}, u32[]{:S(2)}) collective-permute-start(f32[8,128]{1,0:T(8,128)S(1)} %pack.1), channel_id=1, source_target_pairs={{0,16},{1,17},{2,18},{3,19},{4,20},{5,21},{6,22},{7,23},{8,56},{9,... | collective-permute-start | bytes 12296 | tf_op jit(solution)/shard_map/ppermute | solution.py:31
  41.7 2.9 %back.3 = (bf16[4,4,32,1152]{3,2,1,0:T(8,128)(2,1)S(1)}, bf16[4,4,32,1152]{3,2,1,0:T(8,128)(2,1)S(1)}) custom-call(s32[1]{0:T(128)} %bitcast.me_ref.refs_0_, bf16[256,1024]{1,0:T(8,128)(2,1)S(1)} %get-tuple-element.121.rows_ref, bf16[4608,1024]{1,0:T(8,128)(2,1)S(1)} %get-tuple-element.99.refs_10_.head_ref), custom_call_target="tpu_custom_call" | custom-call | flops 2415919104 | bytes 9437184 | tf_op jit(solution)/shard_map/back/pallas_call | solution.py:196
  44.7 1.9 %collective-permute-start.20 = (bf16[4,4,32,1152]{3,2,1,0:T(8,128)(2,1)S(1)}, bf16[4,4,32,1152]{3,2,1,0:T(8,128)(2,1)S(1)}, u32[]{:S(2)}, u32[]{:S(2)}) collective-permute-start(bf16[4,4,32,1152]{3,2,1,0:T(8,128)(2,1)S(1)} %get-tuple-element.126), channel_id=1, source_target_pairs={{0,8},{1,9},{2,10},{3,11},{4,12},{5,13},{6,14},{7,15},{8,0},{9,1},... | collective-permute-start | bytes 3538952 | tf_op jit(solution)/shard_map/ppermute | solution.py:31
  47.6 3.8 %collective-permute-done.19 = f32[8,128]{1,0:T(8,128)S(1)} collective-permute-done((f32[8,128]{1,0:T(8,128)S(1)}, f32[8,128]{1,0:T(8,128)S(1)}, u32[]{:S(2)}, u32[]{:S(2)}) %collective-permute-start.19) | collective-permute-done | bytes 4128 | tf_op jit(solution)/shard_map/ppermute | solution.py:31
  52.0 3.1 %collective-permute-start.27 = (bf16[2,2,2,2,32,1152]{5,4,3,2,1,0:T(8,128)(2,1)S(1)}, bf16[2,2,2,2,32,1152]{5,4,3,2,1,0:T(8,128)(2,1)S(1)}, u32[]{:S(2)}, u32[]{:S(2)}) collective-permute-start(bf16[2,2,2,2,32,1152]{5,4,3,2,1,0:T(8,128)(2,1)S(1)} %get-tuple-element.139), channel_id=1, source_target_pairs={{0,3},{1,2},{2,1},{3,0},{4,7},{5,6},{6,5},{7,4},{8,9},{9,8},{10,11... | collective-permute-start | bytes 3538952 | tf_op jit(solution)/shard_map/ppermute | solution.py:31
  56.1 1.2 %collective-permute-done.21 = f32[8,128]{1,0:T(8,128)S(1)} collective-permute-done((f32[8,128]{1,0:T(8,128)S(1)}, f32[8,128]{1,0:T(8,128)S(1)}, u32[]{:S(2)}, u32[]{:S(2)}) %collective-permute-start.21) | collective-permute-done | bytes 4128 | tf_op jit(solution)/shard_map/ppermute | solution.py:31
  57.3 3.6 %collective-permute-done.22 = f32[8,128]{1,0:T(8,128)S(1)} collective-permute-done((f32[8,128]{1,0:T(8,128)S(1)}, f32[8,128]{1,0:T(8,128)S(1)}, u32[]{:S(2)}, u32[]{:S(2)}) %collective-permute-start.22) | collective-permute-done | bytes 4128 | tf_op jit(solution)/shard_map/ppermute | solution.py:31
  60.9 1.3 %collective-permute-start.23 = (f32[8,128]{1,0:T(8,128)S(1)}, f32[8,128]{1,0:T(8,128)S(1)}, u32[]{:S(2)}, u32[]{:S(2)}) collective-permute-start(f32[8,128]{1,0:T(8,128)S(1)} %add.31), channel_id=1, source_target_pairs={{0,68},{1,69},{2,70},{3,71},{4,64},{5,65},{6,66},{7,67},{8,76},{9,... | collective-permute-start | bytes 12296 | tf_op jit(solution)/shard_map/ppermute | solution.py:31
  62.2 3.5 %collective-permute-done.23 = f32[8,128]{1,0:T(8,128)S(1)} collective-permute-done((f32[8,128]{1,0:T(8,128)S(1)}, f32[8,128]{1,0:T(8,128)S(1)}, u32[]{:S(2)}, u32[]{:S(2)}) %collective-permute-start.23) | collective-permute-done | bytes 4128 | tf_op jit(solution)/shard_map/ppermute | solution.py:31
  66.4 2.2 %collective-permute-start.25 = (f32[8,128]{1,0:T(8,128)S(1)}, f32[8,128]{1,0:T(8,128)S(1)}, u32[]{:S(2)}, u32[]{:S(2)}) collective-permute-start(f32[8,128]{1,0:T(8,128)S(1)} %add.32), channel_id=1, source_target_pairs={{0,3},{1,2},{2,1},{3,0},{4,7},{5,6},{6,5},{7,4},{8,9},{9,8},{10,11... | collective-permute-start | bytes 12296 | tf_op jit(solution)/shard_map/ppermute | solution.py:31
  69.2 1.6 %collective-permute-done.26 = f32[8,128]{1,0:T(8,128)S(1)} collective-permute-done((f32[8,128]{1,0:T(8,128)S(1)}, f32[8,128]{1,0:T(8,128)S(1)}, u32[]{:S(2)}, u32[]{:S(2)}) %collective-permute-start.26) | collective-permute-done | bytes 4128 | tf_op jit(solution)/shard_map/ppermute | solution.py:31
  71.2 1.0 collective-permute-done.24
  74.4 2.3 %collective-permute-start.29 = (bf16[2,2,2,16,1152]{4,3,2,1,0:T(8,128)(2,1)S(1)}, bf16[2,2,2,16,1152]{4,3,2,1,0:T(8,128)(2,1)S(1)}, u32[]{:S(2)}, u32[]{:S(2)}) collective-permute-start(bf16[2,2,2,16,1152]{4,3,2,1,0:T(8,128)(2,1)S(1)} %get-tuple-element.151), channel_id=1, source_target_pairs={{0,48},{1,49},{2,50},{3,51},{4,52},{5,53},{6,54},{7,55},{8,24},{9,... | collective-permute-start | bytes 884744 | tf_op jit(solution)/shard_map/ppermute | solution.py:31
  77.5 5.2 %head_gradient_low.1.started_ref = bf16[4608,1024]{1,0:T(8,128)(2,1)} custom-call(bf16[256,4608]{1,0:T(8,128)(2,1)S(1)} %get-tuple-element.155.low_ref, bf16[256,4608]{1,0:T(8,128)(2,1)S(1)} %get-tuple-element.156.high_ref, bf16[512,1024]{1,0:T(8,128)(2,1)S(1)} %dlogits.1.dlog_ref), custom_call_target="tpu_custom_call" | custom-call | flops 2415919104 | bytes 4718592 | tf_op jit(solution)/shard_map/head_gradient_low/pallas_call | solution.py:378
  82.7 1.2 %collective-permute-done.29.p_got = bf16[2,2,2,16,1152]{4,3,2,1,0:T(8,128)(2,1)S(1)} collective-permute-done((bf16[2,2,2,16,1152]{4,3,2,1,0:T(8,128)(2,1)S(1)}, bf16[2,2,2,16,1152]{4,3,2,1,0:T(8,128)(2,1)S(1)}, u32[]{:S(2)}, u32[]{:S(2)}) %collective-permute-start.29) | collective-permute-done | bytes 294944 | tf_op jit(solution)/shard_map/ppermute | solution.py:31
  84.2 3.4 %collective-permute-start.33 = (bf16[2,32,1152]{2,1,0:T(8,128)(2,1)S(1)}, bf16[2,32,1152]{2,1,0:T(8,128)(2,1)S(1)}, u32[]{:S(2)}, u32[]{:S(2)}) collective-permute-start(bf16[2,32,1152]{2,1,0:T(8,128)(2,1)S(1)} %get-tuple-element.165), channel_id=1, source_target_pairs={{0,17},{1,16},{2,19},{3,18},{4,21},{5,20},{6,23},{7,22},{8,59},{9,... | collective-permute-start | bytes 442376 | tf_op jit(solution)/shard_map/ppermute | solution.py:31
  87.6 4.2 %head_gradient_high.1 = bf16[4608,1024]{1,0:T(8,128)(2,1)} custom-call(bf16[256,4608]{1,0:T(8,128)(2,1)S(1)} %get-tuple-element.155.low_ref, bf16[256,4608]{1,0:T(8,128)(2,1)S(1)} %get-tuple-element.156.high_ref, bf16[512,1024]{1,0:T(8,128)(2,1)S(1)} %dlogits.1.dlog_ref, bf16[4608,1024]{1,0:T(8,128)(2,1)} %head_gradient_low.1.started_ref), custom_call_target="tpu_custom_call", output_to_operand_aliasing={{}: (3, {})} | custom-call | flops 2415919104 | bytes 4718592 | tf_op jit(solution)/shard_map/head_gradient_high/pallas_call | solution.py:378
  92.2 3.1 %collective-permute-start.35 = (bf16[32,576]{1,0:T(8,128)(2,1)S(1)}, bf16[32,576]{1,0:T(8,128)(2,1)S(1)}, u32[]{:S(2)}, u32[]{:S(2)}) collective-permute-start(bf16[32,576]{1,0:T(8,128)(2,1)S(1)} %get-tuple-element.174), channel_id=1, source_target_pairs={{0,64},{1,65},{2,66},{3,67},{4,68},{5,69},{6,70},{7,71},{8,72},{9,... | collective-permute-start | bytes 110600 | tf_op jit(solution)/shard_map/ppermute | solution.py:31
  95.3 1.5 %collective-permute-start.36 = (bf16[32,576]{1,0:T(8,128)(2,1)S(1)}, bf16[32,576]{1,0:T(8,128)(2,1)S(1)}, u32[]{:S(2)}, u32[]{:S(2)}) collective-permute-start(bf16[32,576]{1,0:T(8,128)(2,1)S(1)} %get-tuple-element.175), channel_id=1, source_target_pairs={{0,68},{1,69},{2,70},{3,71},{4,64},{5,65},{6,66},{7,67},{8,76},{9,... | collective-permute-start | bytes 110600 | tf_op jit(solution)/shard_map/ppermute | solution.py:31
  97.7 2.8 %collective-permute-done.36.refs_3_ = bf16[32,576]{1,0:T(8,128)(2,1)S(1)} collective-permute-done((bf16[32,576]{1,0:T(8,128)(2,1)S(1)}, bf16[32,576]{1,0:T(8,128)(2,1)S(1)}, u32[]{:S(2)}, u32[]{:S(2)}) %collective-permute-start.36) | collective-permute-done | bytes 36896 | tf_op jit(solution)/shard_map/ppermute | solution.py:31
  (67 shorter events, 14.4 us)
Async XLA Ops:
  0.6 16.6 %collective-permute-start.3 = (bf16[32,4608]{1,0:T(8,128)(2,1)}, bf16[32,4608]{1,0:T(8,128)(2,1)S(1)}, u32[]{:S(2)}, u32[]{:S(2)}) collective-permute-start(bf16[32,4608]{1,0:T(8,128)(2,1)} %refs_1_.1), channel_id=1, source_target_pairs={{0,68},{1,69},{2,70},{3,71},{4,64},{5,65},{6,66},{7,67},{8,76},{9,... | collective-permute-start | bytes 884744 | tf_op jit(solution)/shard_map/ppermute | solution.py:31
  4.8 12.4 %collective-permute-start.2 = (bf16[32,4608]{1,0:T(8,128)(2,1)}, bf16[32,4608]{1,0:T(8,128)(2,1)S(1)}, u32[]{:S(2)}, u32[]{:S(2)}) collective-permute-start(bf16[32,4608]{1,0:T(8,128)(2,1)} %refs_1_.1), channel_id=1, source_target_pairs={{0,32},{1,33},{2,34},{3,35},{4,36},{5,37},{6,38},{7,39},{8,40},{9,... | collective-permute-start | bytes 884744 | tf_op jit(solution)/shard_map/ppermute | solution.py:31
  7.9 13.5 %collective-permute-start.1 = (bf16[32,4608]{1,0:T(8,128)(2,1)}, bf16[32,4608]{1,0:T(8,128)(2,1)S(1)}, u32[]{:S(2)}, u32[]{:S(2)}) collective-permute-start(bf16[32,4608]{1,0:T(8,128)(2,1)} %refs_1_.1), channel_id=1, source_target_pairs={{0,48},{1,49},{2,50},{3,51},{4,52},{5,53},{6,54},{7,55},{8,24},{9,... | collective-permute-start | bytes 884744 | tf_op jit(solution)/shard_map/ppermute | solution.py:31
  9.0 12.5 %collective-permute-start = (bf16[32,4608]{1,0:T(8,128)(2,1)}, bf16[32,4608]{1,0:T(8,128)(2,1)S(1)}, u32[]{:S(2)}, u32[]{:S(2)}) collective-permute-start(bf16[32,4608]{1,0:T(8,128)(2,1)} %refs_1_.1), channel_id=1, source_target_pairs={{0,16},{1,17},{2,18},{3,19},{4,20},{5,21},{6,22},{7,23},{8,56},{9,... | collective-permute-start | bytes 884744 | tf_op jit(solution)/shard_map/ppermute | solution.py:31
  9.0 14.4 %collective-permute-start.4 = (bf16[32,4608]{1,0:T(8,128)(2,1)}, bf16[32,4608]{1,0:T(8,128)(2,1)S(1)}, u32[]{:S(2)}, u32[]{:S(2)}) collective-permute-start(bf16[32,4608]{1,0:T(8,128)(2,1)} %refs_1_.1), channel_id=1, source_target_pairs={{0,8},{1,9},{2,10},{3,11},{4,12},{5,13},{6,14},{7,15},{8,0},{9,1},... | collective-permute-start | bytes 884744 | tf_op jit(solution)/shard_map/ppermute | solution.py:31
  21.5 3.5 %collective-permute-start.6 = (bf16[32,4608]{1,0:T(8,128)(2,1)S(1)}, bf16[32,4608]{1,0:T(8,128)(2,1)S(1)}, u32[]{:S(2)}, u32[]{:S(2)}) collective-permute-start(bf16[32,4608]{1,0:T(8,128)(2,1)S(1)} %collective-permute-done.1.refs_3_), channel_id=1, source_target_pairs={{0,8},{1,9},{2,10},{3,11},{4,12},{5,13},{6,14},{7,15},{8,0},{9,1},... | collective-permute-start | bytes 884744 | tf_op jit(solution)/shard_map/ppermute | solution.py:31
  22.0 4.2 %collective-permute-start.7 = (bf16[32,4608]{1,0:T(8,128)(2,1)S(1)}, bf16[32,4608]{1,0:T(8,128)(2,1)S(1)}, u32[]{:S(2)}, u32[]{:S(2)}) collective-permute-start(bf16[32,4608]{1,0:T(8,128)(2,1)S(1)} %collective-permute-done.2.refs_4_), channel_id=1, source_target_pairs={{0,8},{1,9},{2,10},{3,11},{4,12},{5,13},{6,14},{7,15},{8,0},{9,1},... | collective-permute-start | bytes 884744 | tf_op jit(solution)/shard_map/ppermute | solution.py:31
  22.0 7.7 %collective-permute-start.8 = (bf16[32,4608]{1,0:T(8,128)(2,1)S(1)}, bf16[32,4608]{1,0:T(8,128)(2,1)S(1)}, u32[]{:S(2)}, u32[]{:S(2)}) collective-permute-start(bf16[32,4608]{1,0:T(8,128)(2,1)S(1)} %collective-permute-done.3.refs_1_), channel_id=1, source_target_pairs={{0,16},{1,17},{2,18},{3,19},{4,20},{5,21},{6,22},{7,23},{8,56},{9,... | collective-permute-start | bytes 884744 | tf_op jit(solution)/shard_map/ppermute | solution.py:31
  23.4 10.7 %collective-permute-start.10 = (bf16[32,4608]{1,0:T(8,128)(2,1)S(1)}, bf16[32,4608]{1,0:T(8,128)(2,1)S(1)}, u32[]{:S(2)}, u32[]{:S(2)}) collective-permute-start(bf16[32,4608]{1,0:T(8,128)(2,1)S(1)} %collective-permute-done.2.refs_4_), channel_id=1, source_target_pairs={{0,68},{1,69},{2,70},{3,71},{4,64},{5,65},{6,66},{7,67},{8,76},{9,... | collective-permute-start | bytes 884744 | tf_op jit(solution)/shard_map/ppermute | solution.py:31
  23.8 11.0 %collective-permute-start.11 = (bf16[32,4608]{1,0:T(8,128)(2,1)S(1)}, bf16[32,4608]{1,0:T(8,128)(2,1)S(1)}, u32[]{:S(2)}, u32[]{:S(2)}) collective-permute-start(bf16[32,4608]{1,0:T(8,128)(2,1)S(1)} %collective-permute-done.3.refs_1_), channel_id=1, source_target_pairs={{0,8},{1,9},{2,10},{3,11},{4,12},{5,13},{6,14},{7,15},{8,0},{9,1},... | collective-permute-start | bytes 884744 | tf_op jit(solution)/shard_map/ppermute | solution.py:31
  24.9 9.2 %collective-permute-start.9 = (bf16[32,4608]{1,0:T(8,128)(2,1)S(1)}, bf16[32,4608]{1,0:T(8,128)(2,1)S(1)}, u32[]{:S(2)}, u32[]{:S(2)}) collective-permute-start(bf16[32,4608]{1,0:T(8,128)(2,1)S(1)} %collective-permute-done.3.refs_1_), channel_id=1, source_target_pairs={{0,48},{1,49},{2,50},{3,51},{4,52},{5,53},{6,54},{7,55},{8,24},{9,... | collective-permute-start | bytes 884744 | tf_op jit(solution)/shard_map/ppermute | solution.py:31
  36.6 3.2 %collective-permute-start.15 = (bf16[4,4,32,1152]{3,2,1,0:T(8,128)(2,1)S(1)}, bf16[4,4,32,1152]{3,2,1,0:T(8,128)(2,1)S(1)}, u32[]{:S(2)}, u32[]{:S(2)}) collective-permute-start(bf16[4,4,32,1152]{3,2,1,0:T(8,128)(2,1)S(1)} %get-tuple-element.115), channel_id=1, source_target_pairs={{0,8},{1,9},{2,10},{3,11},{4,12},{5,13},{6,14},{7,15},{8,0},{9,1},... | collective-permute-start | bytes 3538952 | tf_op jit(solution)/shard_map/ppermute | solution.py:31
  39.8 4.9 %collective-permute-start.17 = (bf16[4,4,32,1152]{3,2,1,0:T(8,128)(2,1)S(1)}, bf16[4,4,32,1152]{3,2,1,0:T(8,128)(2,1)S(1)}, u32[]{:S(2)}, u32[]{:S(2)}) collective-permute-start(bf16[4,4,32,1152]{3,2,1,0:T(8,128)(2,1)S(1)} %get-tuple-element.123), channel_id=1, source_target_pairs={{0,8},{1,9},{2,10},{3,11},{4,12},{5,13},{6,14},{7,15},{8,0},{9,1},... | collective-permute-start | bytes 3538952 | tf_op jit(solution)/shard_map/ppermute | solution.py:31
  40.1 4.5 %collective-permute-start.18 = (bf16[4,4,32,1152]{3,2,1,0:T(8,128)(2,1)S(1)}, bf16[4,4,32,1152]{3,2,1,0:T(8,128)(2,1)S(1)}, u32[]{:S(2)}, u32[]{:S(2)}) collective-permute-start(bf16[4,4,32,1152]{3,2,1,0:T(8,128)(2,1)S(1)} %get-tuple-element.124), channel_id=1, source_target_pairs={{0,8},{1,9},{2,10},{3,11},{4,12},{5,13},{6,14},{7,15},{8,0},{9,1},... | collective-permute-start | bytes 3538952 | tf_op jit(solution)/shard_map/ppermute | solution.py:31
  40.6 4.0 %collective-permute-start.16 = (f32[8,128]{1,0:T(8,128)S(1)}, f32[8,128]{1,0:T(8,128)S(1)}, u32[]{:S(2)}, u32[]{:S(2)}) collective-permute-start(f32[8,128]{1,0:T(8,128)S(1)} %pack.1), channel_id=1, source_target_pairs={{0,16},{1,17},{2,18},{3,19},{4,20},{5,21},{6,22},{7,23},{8,56},{9,... | collective-permute-start | bytes 12296 | tf_op jit(solution)/shard_map/ppermute | solution.py:31
  44.7 6.7 %collective-permute-start.20 = (bf16[4,4,32,1152]{3,2,1,0:T(8,128)(2,1)S(1)}, bf16[4,4,32,1152]{3,2,1,0:T(8,128)(2,1)S(1)}, u32[]{:S(2)}, u32[]{:S(2)}) collective-permute-start(bf16[4,4,32,1152]{3,2,1,0:T(8,128)(2,1)S(1)} %get-tuple-element.126), channel_id=1, source_target_pairs={{0,8},{1,9},{2,10},{3,11},{4,12},{5,13},{6,14},{7,15},{8,0},{9,1},... | collective-permute-start | bytes 3538952 | tf_op jit(solution)/shard_map/ppermute | solution.py:31
  46.6 4.8 %collective-permute-start.19 = (f32[8,128]{1,0:T(8,128)S(1)}, f32[8,128]{1,0:T(8,128)S(1)}, u32[]{:S(2)}, u32[]{:S(2)}) collective-permute-start(f32[8,128]{1,0:T(8,128)S(1)} %add.28), channel_id=1, source_target_pairs={{0,48},{1,49},{2,50},{3,51},{4,52},{5,53},{6,54},{7,55},{8,24},{9,... | collective-permute-start | bytes 12296 | tf_op jit(solution)/shard_map/ppermute | solution.py:31
  52.0 20.1 %collective-permute-start.27 = (bf16[2,2,2,2,32,1152]{5,4,3,2,1,0:T(8,128)(2,1)S(1)}, bf16[2,2,2,2,32,1152]{5,4,3,2,1,0:T(8,128)(2,1)S(1)}, u32[]{:S(2)}, u32[]{:S(2)}) collective-permute-start(bf16[2,2,2,2,32,1152]{5,4,3,2,1,0:T(8,128)(2,1)S(1)} %get-tuple-element.139), channel_id=1, source_target_pairs={{0,3},{1,2},{2,1},{3,0},{4,7},{5,6},{6,5},{7,4},{8,9},{9,8},{10,11... | collective-permute-start | bytes 3538952 | tf_op jit(solution)/shard_map/ppermute | solution.py:31
  55.1 17.4 %collective-permute-start.28 = (bf16[2,2,2,2,32,1152]{5,4,3,2,1,0:T(8,128)(2,1)S(1)}, bf16[2,2,2,2,32,1152]{5,4,3,2,1,0:T(8,128)(2,1)S(1)}, u32[]{:S(2)}, u32[]{:S(2)}) collective-permute-start(bf16[2,2,2,2,32,1152]{5,4,3,2,1,0:T(8,128)(2,1)S(1)} %get-tuple-element.140), channel_id=1, source_target_pairs={{0,48},{1,49},{2,50},{3,51},{4,52},{5,53},{6,54},{7,55},{8,24},{9,... | collective-permute-start | bytes 3538952 | tf_op jit(solution)/shard_map/ppermute | solution.py:31
  57.3 3.6 %collective-permute-start.22 = (f32[8,128]{1,0:T(8,128)S(1)}, f32[8,128]{1,0:T(8,128)S(1)}, u32[]{:S(2)}, u32[]{:S(2)}) collective-permute-start(f32[8,128]{1,0:T(8,128)S(1)} %add.30), channel_id=1, source_target_pairs={{0,4},{1,5},{2,6},{3,7},{4,0},{5,1},{6,2},{7,3},{8,12},{9,13},{10,... | collective-permute-start | bytes 12296 | tf_op jit(solution)/shard_map/ppermute | solution.py:31
  60.9 4.8 %collective-permute-start.23 = (f32[8,128]{1,0:T(8,128)S(1)}, f32[8,128]{1,0:T(8,128)S(1)}, u32[]{:S(2)}, u32[]{:S(2)}) collective-permute-start(f32[8,128]{1,0:T(8,128)S(1)} %add.31), channel_id=1, source_target_pairs={{0,68},{1,69},{2,70},{3,71},{4,64},{5,65},{6,66},{7,67},{8,76},{9,... | collective-permute-start | bytes 12296 | tf_op jit(solution)/shard_map/ppermute | solution.py:31
  65.7 5.1 %collective-permute-start.26 = (f32[8,128]{1,0:T(8,128)S(1)}, f32[8,128]{1,0:T(8,128)S(1)}, u32[]{:S(2)}, u32[]{:S(2)}) collective-permute-start(f32[8,128]{1,0:T(8,128)S(1)} %add.32), channel_id=1, source_target_pairs={{0,2},{1,3},{2,0},{3,1},{4,6},{5,7},{6,4},{7,5},{8,10},{9,11},{10,... | collective-permute-start | bytes 12296 | tf_op jit(solution)/shard_map/ppermute | solution.py:31
  66.4 4.8 %collective-permute-start.25 = (f32[8,128]{1,0:T(8,128)S(1)}, f32[8,128]{1,0:T(8,128)S(1)}, u32[]{:S(2)}, u32[]{:S(2)}) collective-permute-start(f32[8,128]{1,0:T(8,128)S(1)} %add.32), channel_id=1, source_target_pairs={{0,3},{1,2},{2,1},{3,0},{4,7},{5,6},{6,5},{7,4},{8,9},{9,8},{10,11... | collective-permute-start | bytes 12296 | tf_op jit(solution)/shard_map/ppermute | solution.py:31
  68.5 3.6 %collective-permute-start.24 = (f32[8,128]{1,0:T(8,128)S(1)}, f32[8,128]{1,0:T(8,128)S(1)}, u32[]{:S(2)}, u32[]{:S(2)}) collective-permute-start(f32[8,128]{1,0:T(8,128)S(1)} %add.32), channel_id=1, source_target_pairs={{0,1},{1,0},{2,3},{3,2},{4,5},{5,4},{6,7},{7,6},{8,11},{9,10},{10,... | collective-permute-start | bytes 12296 | tf_op jit(solution)/shard_map/ppermute | solution.py:31
  73.1 9.6 %collective-permute-start.30 = (bf16[2,2,2,16,1152]{4,3,2,1,0:T(8,128)(2,1)S(1)}, bf16[2,2,2,16,1152]{4,3,2,1,0:T(8,128)(2,1)S(1)}, u32[]{:S(2)}, u32[]{:S(2)}) collective-permute-start(bf16[2,2,2,16,1152]{4,3,2,1,0:T(8,128)(2,1)S(1)} %get-tuple-element.154), channel_id=1, source_target_pairs={{0,3},{1,2},{2,1},{3,0},{4,7},{5,6},{6,5},{7,4},{8,9},{9,8},{10,11... | collective-permute-start | bytes 884744 | tf_op jit(solution)/shard_map/ppermute | solution.py:31
  74.4 9.6 %collective-permute-start.29 = (bf16[2,2,2,16,1152]{4,3,2,1,0:T(8,128)(2,1)S(1)}, bf16[2,2,2,16,1152]{4,3,2,1,0:T(8,128)(2,1)S(1)}, u32[]{:S(2)}, u32[]{:S(2)}) collective-permute-start(bf16[2,2,2,16,1152]{4,3,2,1,0:T(8,128)(2,1)S(1)} %get-tuple-element.151), channel_id=1, source_target_pairs={{0,48},{1,49},{2,50},{3,51},{4,52},{5,53},{6,54},{7,55},{8,24},{9,... | collective-permute-start | bytes 884744 | tf_op jit(solution)/shard_map/ppermute | solution.py:31
  84.0 7.8 %collective-permute-start.31 = (bf16[2,32,1152]{2,1,0:T(8,128)(2,1)S(1)}, bf16[2,32,1152]{2,1,0:T(8,128)(2,1)S(1)}, u32[]{:S(2)}, u32[]{:S(2)}) collective-permute-start(bf16[2,32,1152]{2,1,0:T(8,128)(2,1)S(1)} %get-tuple-element.163), channel_id=1, source_target_pairs={{0,16},{1,17},{2,18},{3,19},{4,20},{5,21},{6,22},{7,23},{8,56},{9,... | collective-permute-start | bytes 442376 | tf_op jit(solution)/shard_map/ppermute | solution.py:31
  84.1 7.7 %collective-permute-start.32 = (bf16[2,32,1152]{2,1,0:T(8,128)(2,1)S(1)}, bf16[2,32,1152]{2,1,0:T(8,128)(2,1)S(1)}, u32[]{:S(2)}, u32[]{:S(2)}) collective-permute-start(bf16[2,32,1152]{2,1,0:T(8,128)(2,1)S(1)} %get-tuple-element.164), channel_id=1, source_target_pairs={{0,1},{1,0},{2,3},{3,2},{4,5},{5,4},{6,7},{7,6},{8,11},{9,10},{10,... | collective-permute-start | bytes 442376 | tf_op jit(solution)/shard_map/ppermute | solution.py:31
  84.2 7.6 %collective-permute-start.33 = (bf16[2,32,1152]{2,1,0:T(8,128)(2,1)S(1)}, bf16[2,32,1152]{2,1,0:T(8,128)(2,1)S(1)}, u32[]{:S(2)}, u32[]{:S(2)}) collective-permute-start(bf16[2,32,1152]{2,1,0:T(8,128)(2,1)S(1)} %get-tuple-element.165), channel_id=1, source_target_pairs={{0,17},{1,16},{2,19},{3,18},{4,21},{5,20},{6,23},{7,22},{8,59},{9,... | collective-permute-start | bytes 442376 | tf_op jit(solution)/shard_map/ppermute | solution.py:31
  92.1 5.4 %collective-permute-start.34 = (bf16[32,576]{1,0:T(8,128)(2,1)S(1)}, bf16[32,576]{1,0:T(8,128)(2,1)S(1)}, u32[]{:S(2)}, u32[]{:S(2)}) collective-permute-start(bf16[32,576]{1,0:T(8,128)(2,1)S(1)} %get-tuple-element.173), channel_id=1, source_target_pairs={{0,4},{1,5},{2,6},{3,7},{4,0},{5,1},{6,2},{7,3},{8,12},{9,13},{10,... | collective-permute-start | bytes 110600 | tf_op jit(solution)/shard_map/ppermute | solution.py:31
  92.2 5.6 %collective-permute-start.35 = (bf16[32,576]{1,0:T(8,128)(2,1)S(1)}, bf16[32,576]{1,0:T(8,128)(2,1)S(1)}, u32[]{:S(2)}, u32[]{:S(2)}) collective-permute-start(bf16[32,576]{1,0:T(8,128)(2,1)S(1)} %get-tuple-element.174), channel_id=1, source_target_pairs={{0,64},{1,65},{2,66},{3,67},{4,68},{5,69},{6,70},{7,71},{8,72},{9,... | collective-permute-start | bytes 110600 | tf_op jit(solution)/shard_map/ppermute | solution.py:31
  95.3 5.2 %collective-permute-start.36 = (bf16[32,576]{1,0:T(8,128)(2,1)S(1)}, bf16[32,576]{1,0:T(8,128)(2,1)S(1)}, u32[]{:S(2)}, u32[]{:S(2)}) collective-permute-start(bf16[32,576]{1,0:T(8,128)(2,1)S(1)} %get-tuple-element.175), channel_id=1, source_target_pairs={{0,68},{1,69},{2,70},{3,71},{4,64},{5,65},{6,66},{7,67},{8,76},{9,... | collective-permute-start | bytes 110600 | tf_op jit(solution)/shard_map/ppermute | solution.py:31
  (6 other events, 26.0 us)

commit v4 on v3

--- a/solution.py
+++ b/solution.py
@@ -401,14 +401,14 @@
     g0_mine, g0_mate, g1_mine, g1_mate, head, ids, weight = run_begin(
         me, verdict_ids.reshape(4, 128), row_weight.reshape(4, 128), head
     )
-    a1, a2, a3, o0, g0_mine, g0_mate, g1_mine, g1_mate = tie(a1, a2, a3, o0, g0_mine, g0_mate, g1_mine, g1_mate)
+    o0, a3, a2, a1, g0_mine, g0_mate, g1_mine, g1_mate = tie(o0, a3, a2, a1, g0_mine, g0_mate, g1_mine, g1_mate)
     o1, o2, o3 = send(o0, X1), send(o0, X2), send(a3, ZH)
     own_half = [hidden, a1, a2, a3]
     own_half += [send(piece, CORE) for piece in own_half]
     rows0, capped0, term0, total0, target0 = run_forward(forward_low, me, own_half, ids, head)
     o1, term0 = tie(o1, term0)
     a0_mine, a0_mate = run_back(me, term0, head)
-    o1, o2, o3, a0_mate = tie(o1, o2, o3, a0_mate)
+    o1, o3, o2, a0_mate = tie(o1, o3, o2, a0_mate)
     other_half = [o0, o1, o2, o3]
     *swapped, a0_mate = tie(*(send(piece, CORE) for piece in other_half), a0_mate)
     other_half += swapped
@@ -426,13 +426,15 @@
     sums, a1_mate, g0_got, g1_got = tie(sums, a1_mate, g0_got, g1_got)
     a1_got = send(a1_mate, CORE)
     sums = step(sums, X2)
-    sums, a1_got = tie(sums, a1_got)
+    a1_got, sums = tie(a1_got, sums)
     p_keep, p_send, q_keep, q_send = run_fold(
         a0_mine, a0_got, g0_mine, g0_got, a1_mine, a1_got, g1_mine, g1_got
     )
+    sums = step(sums, CORE)
+    p_send, q_send, sums = tie(p_send, q_send, sums)
 
     p_got, q_got = send(p_send, Y2), send(q_send, X2)
-    sums = step(step(step(step(sums, CORE), ZL), ZH), Y1, Y2, Y3)
+    sums = step(step(step(sums, ZL), ZH), Y1, Y2, Y3)
     sums, p_got, q_got = tie(sums, p_got, q_got)
     log_total, own, rest, pick = run_unpack(me, sums, weight)
     p_keep, p_send = run_combine(combine_p, rest, pick, p_keep, p_got)
@@ -447,7 +449,7 @@
     head_grad = run_head_gradient(head_gradient_high, rows0, rows1, dlog, (head_grad,))
     *got, head_grad = tie(*got, head_grad)
     keep, *outs = run_split(me, keep, *got)
-    z_got = tie(*(send(out, partner) for out, partner in zip(outs, (ZL, Z2, ZH))))
+    z_got = tie(send(outs[1], Z2), send(outs[0], ZL), send(outs[2], ZH))
     hidden_grad = run_finish(keep, *z_got)
     return (own[:, 0], head_grad, hidden_grad)
 

time: 101 us -> 98.4 us (0.974); the launches traced: 101 us -> 97.4 us
  waiting for transfers between devices: 27.7 us -> 22.3 us
  starting transfers between devices: 39 us -> 40.6 us
    ppermute x37, waiting for transfers between devices: 27.7 us -> 22.3 us  [send(): return lax.ppermute(array, AXES, partner)]
    ppermute x37, starting transfers between devices: 39 us -> 40.6 us  [send(): return lax.ppermute(array, AXES, partner)]
  transfers between devices with their start and end apart: 37 -> 37, of which waited for: 18 -> 19; matrix products, arithmetic and copies ran while one was open for 1% -> 1% of each run, Pallas kernels for 30% -> 32%
where the time goes in v4:
time: 98.4 us; the launch traced here: 97.4 us
  starting transfers between devices  40.6 us (41%)
  Pallas kernels  33 us (34%)
  waiting for transfers between devices  22.3 us (23%)
    ppermute x37, starting transfers between devices, send(): return lax.ppermute(array, AXES, partner)  40.6 us
    ppermute x37, waiting for transfers between devices, send(): return lax.ppermute(array, AXES, partner)  22.3 us
    pallas_call x2, Pallas kernels, run_head_gradient(): call(kernel, 'vvv' + 'h' * len(started), [('h', (D, WIDTH), bf16)], scrat...  9.38 us
    pallas_call x1, Pallas kernels, run_begin(): call(begin, 'shhh', [BLOCKS] * 4 + [('v', (D, WIDTH), bf16), column, colu...  8.24 us
    pallas_call x2, Pallas kernels, run_forward(): call(kernel, 's' + 'v' * 10, [('v', (256, D), bf16), ('v', (256, WIDTH),...  5.96 us
    pallas_call x2, Pallas kernels, run_back(): return call(back, 'svv', [BLOCKS, BLOCKS], **BACK_COST)(me, rows, head)  5.87 us
  transfers between devices with their start and end apart: 37, of which 19 were waited for; matrix products, arithmetic and copies ran while one was open for 1% of the time, Pallas kernels for 32%

profile of v4, /device:TPU:0, one launch (start us, length us, event | category | flops | bytes accessed | tf_op | source)
XLA Modules:
  0.0 97.4 jit_solution(11641108980054078607)
XLA Ops:
  0.6 1.7 %collective-permute-start.3 = (bf16[32,4608]{1,0:T(8,128)(2,1)}, bf16[32,4608]{1,0:T(8,128)(2,1)S(1)}, u32[]{:S(2)}, u32[]{:S(2)}) collective-permute-start(bf16[32,4608]{1,0:T(8,128)(2,1)} %refs_1_.1), channel_id=1, source_target_pairs={{0,16},{1,17},{2,18},{3,19},{4,20},{5,21},{6,22},{7,23},{8,56},{9,... | collective-permute-start | bytes 884744 | tf_op jit(solution)/shard_map/ppermute | solution.py:31
  2.3 2.1 %collective-permute-start.2 = (bf16[32,4608]{1,0:T(8,128)(2,1)}, bf16[32,4608]{1,0:T(8,128)(2,1)S(1)}, u32[]{:S(2)}, u32[]{:S(2)}) collective-permute-start(bf16[32,4608]{1,0:T(8,128)(2,1)} %refs_1_.1), channel_id=1, source_target_pairs={{0,48},{1,49},{2,50},{3,51},{4,52},{5,53},{6,54},{7,55},{8,24},{9,... | collective-permute-start | bytes 884744 | tf_op jit(solution)/shard_map/ppermute | solution.py:31
  5.0 4.0 %collective-permute-start = (bf16[32,4608]{1,0:T(8,128)(2,1)}, bf16[32,4608]{1,0:T(8,128)(2,1)S(1)}, u32[]{:S(2)}, u32[]{:S(2)}) collective-permute-start(bf16[32,4608]{1,0:T(8,128)(2,1)} %refs_1_.1), channel_id=1, source_target_pairs={{0,68},{1,69},{2,70},{3,71},{4,64},{5,65},{6,66},{7,67},{8,76},{9,... | collective-permute-start | bytes 884744 | tf_op jit(solution)/shard_map/ppermute | solution.py:31
  9.1 8.2 %begin.1 = (bf16[4,4,32,1152]{3,2,1,0:T(8,128)(2,1)S(1)}, bf16[4,4,32,1152]{3,2,1,0:T(8,128)(2,1)S(1)}, bf16[4,4,32,1152]{3,2,1,0:T(8,128)(2,1)S(1)}, bf16[4,4,3...) custom-call(s32[1]{0:T(128)} %bitcast.me_ref.refs_0_, ...), custom_call_target="tpu_custom_call" | custom-call | flops 4831838208 | bytes 9437184 | tf_op jit(solution)/shard_map/begin/pallas_call | solution.py:231
  17.3 1.0 %collective-permute-done.1.refs_4_ = bf16[32,4608]{1,0:T(8,128)(2,1)S(1)} collective-permute-done((bf16[32,4608]{1,0:T(8,128)(2,1)}, bf16[32,4608]{1,0:T(8,128)(2,1)S(1)}, u32[]{:S(2)}, u32[]{:S(2)}) %collective-permute-start.1) | collective-permute-done | bytes 294944 | tf_op jit(solution)/shard_map/ppermute | solution.py:31
  19.8 3.5 %collective-permute-start.9 = (bf16[32,4608]{1,0:T(8,128)(2,1)S(1)}, bf16[32,4608]{1,0:T(8,128)(2,1)S(1)}, u32[]{:S(2)}, u32[]{:S(2)}) collective-permute-start(bf16[32,4608]{1,0:T(8,128)(2,1)S(1)} %collective-permute-done.1.refs_4_), channel_id=1, source_target_pairs={{0,68},{1,69},{2,70},{3,71},{4,64},{5,65},{6,66},{7,67},{8,76},{9,... | collective-permute-start | bytes 884744 | tf_op jit(solution)/shard_map/ppermute | solution.py:31
  23.3 1.2 %collective-permute-start.11 = (bf16[32,4608]{1,0:T(8,128)(2,1)S(1)}, bf16[32,4608]{1,0:T(8,128)(2,1)S(1)}, u32[]{:S(2)}, u32[]{:S(2)}) collective-permute-start(bf16[32,4608]{1,0:T(8,128)(2,1)S(1)} %collective-permute-done.refs_1_), channel_id=1, source_target_pairs={{0,8},{1,9},{2,10},{3,11},{4,12},{5,13},{6,14},{7,15},{8,0},{9,1},... | collective-permute-start | bytes 884744 | tf_op jit(solution)/shard_map/ppermute | solution.py:31
  24.6 1.7 %collective-permute-start.10 = (bf16[32,4608]{1,0:T(8,128)(2,1)S(1)}, bf16[32,4608]{1,0:T(8,128)(2,1)S(1)}, u32[]{:S(2)}, u32[]{:S(2)}) collective-permute-start(bf16[32,4608]{1,0:T(8,128)(2,1)S(1)} %collective-permute-done.refs_1_), channel_id=1, source_target_pairs={{0,48},{1,49},{2,50},{3,51},{4,52},{5,53},{6,54},{7,55},{8,24},{9,... | collective-permute-start | bytes 884744 | tf_op jit(solution)/shard_map/ppermute | solution.py:31
  26.2 3.0 %forward_low.1 = (bf16[256,4608]{1,0:T(8,128)(2,1)S(1)}, f32[256,1024]{1,0:T(8,128)S(1)}, bf16[256,1024]{1,0:T(8,128)(2,1)S(1)}, f32[256,128]{1,0:T(8,128)S(1)}, f32[256,128]{1,0:T(8,128)S(1)}) custom-call(s32[1]{0:T(128)} %bitcast.me_ref.refs_0_, bf16[32,4608]{1,0:T(8,128)(2,1)S(1)} %copy-done, bf16[32,4608]{1,0:T(8,128)(2,1)S(1)} %collective-permute-done.3.refs_2_, ...), custom_call_target="tpu_custom_call" | custom-call | flops 2415919104 | bytes 9437184 | tf_op jit(solution)/shard_map/forward_low/pallas_call | solution.py:116
  29.2 2.9 %back.2 = (bf16[4,4,32,1152]{3,2,1,0:T(8,128)(2,1)S(1)}, bf16[4,4,32,1152]{3,2,1,0:T(8,128)(2,1)S(1)}) custom-call(s32[1]{0:T(128)} %bitcast.me_ref.refs_0_, bf16[256,1024]{1,0:T(8,128)(2,1)S(1)} %get-tuple-element.105.rows_ref, bf16[4608,1024]{1,0:T(8,128)(2,1)S(1)} %get-tuple-element.103.refs_10_.head_ref), custom_call_target="tpu_custom_call" | custom-call | flops 2415919104 | bytes 9437184 | tf_op jit(solution)/shard_map/back/pallas_call | solution.py:196
  33.0 1.1 %collective-permute-done.12.refs_6_ = bf16[32,4608]{1,0:T(8,128)(2,1)S(1)} collective-permute-done((bf16[32,4608]{1,0:T(8,128)(2,1)S(1)}, bf16[32,4608]{1,0:T(8,128)(2,1)S(1)}, u32[]{:S(2)}, u32[]{:S(2)}) %collective-permute-start.12) | collective-permute-done | bytes 294944 | tf_op jit(solution)/shard_map/ppermute | solution.py:31
  35.1 3.0 %forward_high.1 = (bf16[256,4608]{1,0:T(8,128)(2,1)S(1)}, f32[256,1024]{1,0:T(8,128)S(1)}, bf16[256,1024]{1,0:T(8,128)(2,1)S(1)}, f32[256,128]{1,0:T(8,128)S(1)}, f32[256,128]{1,0:T(8,128)S(1)}) custom-call(s32[1]{0:T(128)} %bitcast.me_ref.refs_0_, bf16[32,4608]{1,0:T(8,128)(2,1)S(1)} %collective-permute-done.refs_1_, ...), custom_call_target="tpu_custom_call" | custom-call | flops 2415919104 | bytes 9437184 | tf_op jit(solution)/shard_map/forward_high/pallas_call | solution.py:116
  39.0 2.9 %back.3 = (bf16[4,4,32,1152]{3,2,1,0:T(8,128)(2,1)S(1)}, bf16[4,4,32,1152]{3,2,1,0:T(8,128)(2,1)S(1)}) custom-call(s32[1]{0:T(128)} %bitcast.me_ref.refs_0_, bf16[256,1024]{1,0:T(8,128)(2,1)S(1)} %get-tuple-element.127.rows_ref, bf16[4608,1024]{1,0:T(8,128)(2,1)S(1)} %get-tuple-element.103.refs_10_.head_ref), custom_call_target="tpu_custom_call" | custom-call | flops 2415919104 | bytes 9437184 | tf_op jit(solution)/shard_map/back/pallas_call | solution.py:196
  42.7 1.3 %collective-permute-start.19 = (bf16[4,4,32,1152]{3,2,1,0:T(8,128)(2,1)S(1)}, bf16[4,4,32,1152]{3,2,1,0:T(8,128)(2,1)S(1)}, u32[]{:S(2)}, u32[]{:S(2)}) collective-permute-start(bf16[4,4,32,1152]{3,2,1,0:T(8,128)(2,1)S(1)} %get-tuple-element.133), channel_id=1, source_target_pairs={{0,8},{1,9},{2,10},{3,11},{4,12},{5,13},{6,14},{7,15},{8,0},{9,1},... | collective-permute-start | bytes 3538952 | tf_op jit(solution)/shard_map/ppermute | solution.py:31
  44.0 1.6 %collective-permute-start.20 = (f32[8,128]{1,0:T(8,128)S(1)}, f32[8,128]{1,0:T(8,128)S(1)}, u32[]{:S(2)}, u32[]{:S(2)}) collective-permute-start(f32[8,128]{1,0:T(8,128)S(1)} %add.28), channel_id=1, source_target_pairs={{0,48},{1,49},{2,50},{3,51},{4,52},{5,53},{6,54},{7,55},{8,24},{9,... | collective-permute-start | bytes 12296 | tf_op jit(solution)/shard_map/ppermute | solution.py:31
  45.6 3.2 %collective-permute-done.20 = f32[8,128]{1,0:T(8,128)S(1)} collective-permute-done((f32[8,128]{1,0:T(8,128)S(1)}, f32[8,128]{1,0:T(8,128)S(1)}, u32[]{:S(2)}, u32[]{:S(2)}) %collective-permute-start.20) | collective-permute-done | bytes 4128 | tf_op jit(solution)/shard_map/ppermute | solution.py:31
  50.0 3.0 %collective-permute-start.27 = (bf16[2,2,2,2,32,1152]{5,4,3,2,1,0:T(8,128)(2,1)S(1)}, bf16[2,2,2,2,32,1152]{5,4,3,2,1,0:T(8,128)(2,1)S(1)}, u32[]{:S(2)}, u32[]{:S(2)}) collective-permute-start(bf16[2,2,2,2,32,1152]{5,4,3,2,1,0:T(8,128)(2,1)S(1)} %get-tuple-element.145), channel_id=1, source_target_pairs={{0,3},{1,2},{2,1},{3,0},{4,7},{5,6},{6,5},{7,4},{8,9},{9,8},{10,11... | collective-permute-start | bytes 3538952 | tf_op jit(solution)/shard_map/ppermute | solution.py:31
  53.0 1.6 %collective-permute-start.28 = (bf16[2,2,2,2,32,1152]{5,4,3,2,1,0:T(8,128)(2,1)S(1)}, bf16[2,2,2,2,32,1152]{5,4,3,2,1,0:T(8,128)(2,1)S(1)}, u32[]{:S(2)}, u32[]{:S(2)}) collective-permute-start(bf16[2,2,2,2,32,1152]{5,4,3,2,1,0:T(8,128)(2,1)S(1)} %get-tuple-element.146), channel_id=1, source_target_pairs={{0,48},{1,49},{2,50},{3,51},{4,52},{5,53},{6,54},{7,55},{8,24},{9,... | collective-permute-start | bytes 3538952 | tf_op jit(solution)/shard_map/ppermute | solution.py:31
  54.6 3.6 %collective-permute-done.22 = f32[8,128]{1,0:T(8,128)S(1)} collective-permute-done((f32[8,128]{1,0:T(8,128)S(1)}, f32[8,128]{1,0:T(8,128)S(1)}, u32[]{:S(2)}, u32[]{:S(2)}) %collective-permute-start.22) | collective-permute-done | bytes 4128 | tf_op jit(solution)/shard_map/ppermute | solution.py:31
  58.2 2.2 %collective-permute-start.23 = (f32[8,128]{1,0:T(8,128)S(1)}, f32[8,128]{1,0:T(8,128)S(1)}, u32[]{:S(2)}, u32[]{:S(2)}) collective-permute-start(f32[8,128]{1,0:T(8,128)S(1)} %add.31), channel_id=1, source_target_pairs={{0,68},{1,69},{2,70},{3,71},{4,64},{5,65},{6,66},{7,67},{8,76},{9,... | collective-permute-start | bytes 12296 | tf_op jit(solution)/shard_map/ppermute | solution.py:31
  60.4 2.6 %collective-permute-done.23 = f32[8,128]{1,0:T(8,128)S(1)} collective-permute-done((f32[8,128]{1,0:T(8,128)S(1)}, f32[8,128]{1,0:T(8,128)S(1)}, u32[]{:S(2)}, u32[]{:S(2)}) %collective-permute-start.23) | collective-permute-done | bytes 4128 | tf_op jit(solution)/shard_map/ppermute | solution.py:31
  63.7 2.2 %collective-permute-start.25 = (f32[8,128]{1,0:T(8,128)S(1)}, f32[8,128]{1,0:T(8,128)S(1)}, u32[]{:S(2)}, u32[]{:S(2)}) collective-permute-start(f32[8,128]{1,0:T(8,128)S(1)} %add.32), channel_id=1, source_target_pairs={{0,3},{1,2},{2,1},{3,0},{4,7},{5,6},{6,5},{7,4},{8,9},{9,8},{10,11... | collective-permute-start | bytes 12296 | tf_op jit(solution)/shard_map/ppermute | solution.py:31
  66.5 1.6 %collective-permute-done.26 = f32[8,128]{1,0:T(8,128)S(1)} collective-permute-done((f32[8,128]{1,0:T(8,128)S(1)}, f32[8,128]{1,0:T(8,128)S(1)}, u32[]{:S(2)}, u32[]{:S(2)}) %collective-permute-start.26) | collective-permute-done | bytes 4128 | tf_op jit(solution)/shard_map/ppermute | solution.py:31
  68.5 1.0 collective-permute-done.24
  71.7 1.7 %collective-permute-start.29 = (bf16[2,2,2,16,1152]{4,3,2,1,0:T(8,128)(2,1)S(1)}, bf16[2,2,2,16,1152]{4,3,2,1,0:T(8,128)(2,1)S(1)}, u32[]{:S(2)}, u32[]{:S(2)}) collective-permute-start(bf16[2,2,2,16,1152]{4,3,2,1,0:T(8,128)(2,1)S(1)} %get-tuple-element.157), channel_id=1, source_target_pairs={{0,48},{1,49},{2,50},{3,51},{4,52},{5,53},{6,54},{7,55},{8,24},{9,... | collective-permute-start | bytes 884744 | tf_op jit(solution)/shard_map/ppermute | solution.py:31
  74.3 5.2 %head_gradient_low.1.started_ref = bf16[4608,1024]{1,0:T(8,128)(2,1)} custom-call(bf16[256,4608]{1,0:T(8,128)(2,1)S(1)} %get-tuple-element.161.low_ref, bf16[256,4608]{1,0:T(8,128)(2,1)S(1)} %get-tuple-element.162.high_ref, bf16[512,1024]{1,0:T(8,128)(2,1)S(1)} %dlogits.1.dlog_ref), custom_call_target="tpu_custom_call" | custom-call | flops 2415919104 | bytes 4718592 | tf_op jit(solution)/shard_map/head_gradient_low/pallas_call | solution.py:378
  80.6 3.4 %collective-permute-start.33 = (bf16[2,32,1152]{2,1,0:T(8,128)(2,1)S(1)}, bf16[2,32,1152]{2,1,0:T(8,128)(2,1)S(1)}, u32[]{:S(2)}, u32[]{:S(2)}) collective-permute-start(bf16[2,32,1152]{2,1,0:T(8,128)(2,1)S(1)} %get-tuple-element.171), channel_id=1, source_target_pairs={{0,17},{1,16},{2,19},{3,18},{4,21},{5,20},{6,23},{7,22},{8,59},{9,... | collective-permute-start | bytes 442376 | tf_op jit(solution)/shard_map/ppermute | solution.py:31
  83.9 4.2 %head_gradient_high.1 = bf16[4608,1024]{1,0:T(8,128)(2,1)} custom-call(bf16[256,4608]{1,0:T(8,128)(2,1)S(1)} %get-tuple-element.161.low_ref, bf16[256,4608]{1,0:T(8,128)(2,1)S(1)} %get-tuple-element.162.high_ref, bf16[512,1024]{1,0:T(8,128)(2,1)S(1)} %dlogits.1.dlog_ref, bf16[4608,1024]{1,0:T(8,128)(2,1)} %head_gradient_low.1.started_ref), custom_call_target="tpu_custom_call", output_to_operand_aliasing={{}: (3, {})} | custom-call | flops 2415919104 | bytes 4718592 | tf_op jit(solution)/shard_map/head_gradient_high/pallas_call | solution.py:378
  88.4 2.0 %collective-permute-start.34 = (bf16[32,576]{1,0:T(8,128)(2,1)S(1)}, bf16[32,576]{1,0:T(8,128)(2,1)S(1)}, u32[]{:S(2)}, u32[]{:S(2)}) collective-permute-start(bf16[32,576]{1,0:T(8,128)(2,1)S(1)} %get-tuple-element.179), channel_id=1, source_target_pairs={{0,64},{1,65},{2,66},{3,67},{4,68},{5,69},{6,70},{7,71},{8,72},{9,... | collective-permute-start | bytes 110600 | tf_op jit(solution)/shard_map/ppermute | solution.py:31
  90.4 1.1 %collective-permute-start.35 = (bf16[32,576]{1,0:T(8,128)(2,1)S(1)}, bf16[32,576]{1,0:T(8,128)(2,1)S(1)}, u32[]{:S(2)}, u32[]{:S(2)}) collective-permute-start(bf16[32,576]{1,0:T(8,128)(2,1)S(1)} %get-tuple-element.180), channel_id=1, source_target_pairs={{0,4},{1,5},{2,6},{3,7},{4,0},{5,1},{6,2},{7,3},{8,12},{9,13},{10,... | collective-permute-start | bytes 110600 | tf_op jit(solution)/shard_map/ppermute | solution.py:31
  91.6 1.0 %collective-permute-start.36 = (bf16[32,576]{1,0:T(8,128)(2,1)S(1)}, bf16[32,576]{1,0:T(8,128)(2,1)S(1)}, u32[]{:S(2)}, u32[]{:S(2)}) collective-permute-start(bf16[32,576]{1,0:T(8,128)(2,1)S(1)} %get-tuple-element.181), channel_id=1, source_target_pairs={{0,68},{1,69},{2,70},{3,71},{4,64},{5,65},{6,66},{7,67},{8,76},{9,... | collective-permute-start | bytes 110600 | tf_op jit(solution)/shard_map/ppermute | solution.py:31
  94.4 2.4 %collective-permute-done.36.refs_3_ = bf16[32,576]{1,0:T(8,128)(2,1)S(1)} collective-permute-done((bf16[32,576]{1,0:T(8,128)(2,1)S(1)}, bf16[32,576]{1,0:T(8,128)(2,1)S(1)}, u32[]{:S(2)}, u32[]{:S(2)}) %collective-permute-start.36) | collective-permute-done | bytes 36896 | tf_op jit(solution)/shard_map/ppermute | solution.py:31
  (67 shorter events, 15.2 us)
Async XLA Ops:
  0.6 16.7 %collective-permute-start.3 = (bf16[32,4608]{1,0:T(8,128)(2,1)}, bf16[32,4608]{1,0:T(8,128)(2,1)S(1)}, u32[]{:S(2)}, u32[]{:S(2)}) collective-permute-start(bf16[32,4608]{1,0:T(8,128)(2,1)} %refs_1_.1), channel_id=1, source_target_pairs={{0,16},{1,17},{2,18},{3,19},{4,20},{5,21},{6,22},{7,23},{8,56},{9,... | collective-permute-start | bytes 884744 | tf_op jit(solution)/shard_map/ppermute | solution.py:31
  2.3 15.0 %collective-permute-start.2 = (bf16[32,4608]{1,0:T(8,128)(2,1)}, bf16[32,4608]{1,0:T(8,128)(2,1)S(1)}, u32[]{:S(2)}, u32[]{:S(2)}) collective-permute-start(bf16[32,4608]{1,0:T(8,128)(2,1)} %refs_1_.1), channel_id=1, source_target_pairs={{0,48},{1,49},{2,50},{3,51},{4,52},{5,53},{6,54},{7,55},{8,24},{9,... | collective-permute-start | bytes 884744 | tf_op jit(solution)/shard_map/ppermute | solution.py:31
  4.4 14.0 %collective-permute-start.1 = (bf16[32,4608]{1,0:T(8,128)(2,1)}, bf16[32,4608]{1,0:T(8,128)(2,1)S(1)}, u32[]{:S(2)}, u32[]{:S(2)}) collective-permute-start(bf16[32,4608]{1,0:T(8,128)(2,1)} %refs_1_.1), channel_id=1, source_target_pairs={{0,32},{1,33},{2,34},{3,35},{4,36},{5,37},{6,38},{7,39},{8,40},{9,... | collective-permute-start | bytes 884744 | tf_op jit(solution)/shard_map/ppermute | solution.py:31
  5.0 13.3 %collective-permute-start = (bf16[32,4608]{1,0:T(8,128)(2,1)}, bf16[32,4608]{1,0:T(8,128)(2,1)S(1)}, u32[]{:S(2)}, u32[]{:S(2)}) collective-permute-start(bf16[32,4608]{1,0:T(8,128)(2,1)} %refs_1_.1), channel_id=1, source_target_pairs={{0,68},{1,69},{2,70},{3,71},{4,64},{5,65},{6,66},{7,67},{8,76},{9,... | collective-permute-start | bytes 884744 | tf_op jit(solution)/shard_map/ppermute | solution.py:31
  9.1 10.8 %collective-permute-start.5 = (bf16[32,4608]{1,0:T(8,128)(2,1)}, bf16[32,4608]{1,0:T(8,128)(2,1)S(1)}, u32[]{:S(2)}, u32[]{:S(2)}) collective-permute-start(bf16[32,4608]{1,0:T(8,128)(2,1)} %refs_1_.1), channel_id=1, source_target_pairs={{0,8},{1,9},{2,10},{3,11},{4,12},{5,13},{6,14},{7,15},{8,0},{9,1},... | collective-permute-start | bytes 884744 | tf_op jit(solution)/shard_map/ppermute | solution.py:31
  18.4 4.9 %collective-permute-start.6 = (bf16[32,4608]{1,0:T(8,128)(2,1)S(1)}, bf16[32,4608]{1,0:T(8,128)(2,1)S(1)}, u32[]{:S(2)}, u32[]{:S(2)}) collective-permute-start(bf16[32,4608]{1,0:T(8,128)(2,1)S(1)} %collective-permute-done.3.refs_2_), channel_id=1, source_target_pairs={{0,8},{1,9},{2,10},{3,11},{4,12},{5,13},{6,14},{7,15},{8,0},{9,1},... | collective-permute-start | bytes 884744 | tf_op jit(solution)/shard_map/ppermute | solution.py:31
  18.4 6.2 %collective-permute-start.7 = (bf16[32,4608]{1,0:T(8,128)(2,1)S(1)}, bf16[32,4608]{1,0:T(8,128)(2,1)S(1)}, u32[]{:S(2)}, u32[]{:S(2)}) collective-permute-start(bf16[32,4608]{1,0:T(8,128)(2,1)S(1)} %collective-permute-done.2.refs_3_), channel_id=1, source_target_pairs={{0,8},{1,9},{2,10},{3,11},{4,12},{5,13},{6,14},{7,15},{8,0},{9,1},... | collective-permute-start | bytes 884744 | tf_op jit(solution)/shard_map/ppermute | solution.py:31
  18.9 7.3 %collective-permute-start.8 = (bf16[32,4608]{1,0:T(8,128)(2,1)S(1)}, bf16[32,4608]{1,0:T(8,128)(2,1)S(1)}, u32[]{:S(2)}, u32[]{:S(2)}) collective-permute-start(bf16[32,4608]{1,0:T(8,128)(2,1)S(1)} %collective-permute-done.1.refs_4_), channel_id=1, source_target_pairs={{0,8},{1,9},{2,10},{3,11},{4,12},{5,13},{6,14},{7,15},{8,0},{9,1},... | collective-permute-start | bytes 884744 | tf_op jit(solution)/shard_map/ppermute | solution.py:31
  18.9 10.4 %collective-permute-start.4 = (bf16[32,4608]{1,0:T(8,128)(2,1)S(1)}, bf16[32,4608]{1,0:T(8,128)(2,1)S(1)}, u32[]{:S(2)}, u32[]{:S(2)}) collective-permute-start(bf16[32,4608]{1,0:T(8,128)(2,1)S(1)} %collective-permute-done.refs_1_), channel_id=1, source_target_pairs={{0,16},{1,17},{2,18},{3,19},{4,20},{5,21},{6,22},{7,23},{8,56},{9,... | collective-permute-start | bytes 884744 | tf_op jit(solution)/shard_map/ppermute | solution.py:31
  19.8 12.4 %collective-permute-start.9 = (bf16[32,4608]{1,0:T(8,128)(2,1)S(1)}, bf16[32,4608]{1,0:T(8,128)(2,1)S(1)}, u32[]{:S(2)}, u32[]{:S(2)}) collective-permute-start(bf16[32,4608]{1,0:T(8,128)(2,1)S(1)} %collective-permute-done.1.refs_4_), channel_id=1, source_target_pairs={{0,68},{1,69},{2,70},{3,71},{4,64},{5,65},{6,66},{7,67},{8,76},{9,... | collective-permute-start | bytes 884744 | tf_op jit(solution)/shard_map/ppermute | solution.py:31
  23.3 9.7 %collective-permute-start.11 = (bf16[32,4608]{1,0:T(8,128)(2,1)S(1)}, bf16[32,4608]{1,0:T(8,128)(2,1)S(1)}, u32[]{:S(2)}, u32[]{:S(2)}) collective-permute-start(bf16[32,4608]{1,0:T(8,128)(2,1)S(1)} %collective-permute-done.refs_1_), channel_id=1, source_target_pairs={{0,8},{1,9},{2,10},{3,11},{4,12},{5,13},{6,14},{7,15},{8,0},{9,1},... | collective-permute-start | bytes 884744 | tf_op jit(solution)/shard_map/ppermute | solution.py:31
  24.6 7.9 %collective-permute-start.10 = (bf16[32,4608]{1,0:T(8,128)(2,1)S(1)}, bf16[32,4608]{1,0:T(8,128)(2,1)S(1)}, u32[]{:S(2)}, u32[]{:S(2)}) collective-permute-start(bf16[32,4608]{1,0:T(8,128)(2,1)S(1)} %collective-permute-done.refs_1_), channel_id=1, source_target_pairs={{0,48},{1,49},{2,50},{3,51},{4,52},{5,53},{6,54},{7,55},{8,24},{9,... | collective-permute-start | bytes 884744 | tf_op jit(solution)/shard_map/ppermute | solution.py:31
  38.0 4.5 %collective-permute-start.17 = (bf16[4,4,32,1152]{3,2,1,0:T(8,128)(2,1)S(1)}, bf16[4,4,32,1152]{3,2,1,0:T(8,128)(2,1)S(1)}, u32[]{:S(2)}, u32[]{:S(2)}) collective-permute-start(bf16[4,4,32,1152]{3,2,1,0:T(8,128)(2,1)S(1)} %get-tuple-element.129), channel_id=1, source_target_pairs={{0,8},{1,9},{2,10},{3,11},{4,12},{5,13},{6,14},{7,15},{8,0},{9,1},... | collective-permute-start | bytes 3538952 | tf_op jit(solution)/shard_map/ppermute | solution.py:31
  38.5 4.2 %collective-permute-start.18 = (bf16[4,4,32,1152]{3,2,1,0:T(8,128)(2,1)S(1)}, bf16[4,4,32,1152]{3,2,1,0:T(8,128)(2,1)S(1)}, u32[]{:S(2)}, u32[]{:S(2)}) collective-permute-start(bf16[4,4,32,1152]{3,2,1,0:T(8,128)(2,1)S(1)} %get-tuple-element.130), channel_id=1, source_target_pairs={{0,8},{1,9},{2,10},{3,11},{4,12},{5,13},{6,14},{7,15},{8,0},{9,1},... | collective-permute-start | bytes 3538952 | tf_op jit(solution)/shard_map/ppermute | solution.py:31
  38.9 3.7 %collective-permute-start.16 = (f32[8,128]{1,0:T(8,128)S(1)}, f32[8,128]{1,0:T(8,128)S(1)}, u32[]{:S(2)}, u32[]{:S(2)}) collective-permute-start(f32[8,128]{1,0:T(8,128)S(1)} %pack.1), channel_id=1, source_target_pairs={{0,16},{1,17},{2,18},{3,19},{4,20},{5,21},{6,22},{7,23},{8,56},{9,... | collective-permute-start | bytes 12296 | tf_op jit(solution)/shard_map/ppermute | solution.py:31
  42.7 6.2 %collective-permute-start.19 = (bf16[4,4,32,1152]{3,2,1,0:T(8,128)(2,1)S(1)}, bf16[4,4,32,1152]{3,2,1,0:T(8,128)(2,1)S(1)}, u32[]{:S(2)}, u32[]{:S(2)}) collective-permute-start(bf16[4,4,32,1152]{3,2,1,0:T(8,128)(2,1)S(1)} %get-tuple-element.133), channel_id=1, source_target_pairs={{0,8},{1,9},{2,10},{3,11},{4,12},{5,13},{6,14},{7,15},{8,0},{9,1},... | collective-permute-start | bytes 3538952 | tf_op jit(solution)/shard_map/ppermute | solution.py:31
  44.0 4.8 %collective-permute-start.20 = (f32[8,128]{1,0:T(8,128)S(1)}, f32[8,128]{1,0:T(8,128)S(1)}, u32[]{:S(2)}, u32[]{:S(2)}) collective-permute-start(f32[8,128]{1,0:T(8,128)S(1)} %add.28), channel_id=1, source_target_pairs={{0,48},{1,49},{2,50},{3,51},{4,52},{5,53},{6,54},{7,55},{8,24},{9,... | collective-permute-start | bytes 12296 | tf_op jit(solution)/shard_map/ppermute | solution.py:31
  50.0 19.5 %collective-permute-start.27 = (bf16[2,2,2,2,32,1152]{5,4,3,2,1,0:T(8,128)(2,1)S(1)}, bf16[2,2,2,2,32,1152]{5,4,3,2,1,0:T(8,128)(2,1)S(1)}, u32[]{:S(2)}, u32[]{:S(2)}) collective-permute-start(bf16[2,2,2,2,32,1152]{5,4,3,2,1,0:T(8,128)(2,1)S(1)} %get-tuple-element.145), channel_id=1, source_target_pairs={{0,3},{1,2},{2,1},{3,0},{4,7},{5,6},{6,5},{7,4},{8,9},{9,8},{10,11... | collective-permute-start | bytes 3538952 | tf_op jit(solution)/shard_map/ppermute | solution.py:31
  53.0 17.4 %collective-permute-start.28 = (bf16[2,2,2,2,32,1152]{5,4,3,2,1,0:T(8,128)(2,1)S(1)}, bf16[2,2,2,2,32,1152]{5,4,3,2,1,0:T(8,128)(2,1)S(1)}, u32[]{:S(2)}, u32[]{:S(2)}) collective-permute-start(bf16[2,2,2,2,32,1152]{5,4,3,2,1,0:T(8,128)(2,1)S(1)} %get-tuple-element.146), channel_id=1, source_target_pairs={{0,48},{1,49},{2,50},{3,51},{4,52},{5,53},{6,54},{7,55},{8,24},{9,... | collective-permute-start | bytes 3538952 | tf_op jit(solution)/shard_map/ppermute | solution.py:31
  54.6 3.6 %collective-permute-start.22 = (f32[8,128]{1,0:T(8,128)S(1)}, f32[8,128]{1,0:T(8,128)S(1)}, u32[]{:S(2)}, u32[]{:S(2)}) collective-permute-start(f32[8,128]{1,0:T(8,128)S(1)} %add.30), channel_id=1, source_target_pairs={{0,4},{1,5},{2,6},{3,7},{4,0},{5,1},{6,2},{7,3},{8,12},{9,13},{10,... | collective-permute-start | bytes 12296 | tf_op jit(solution)/shard_map/ppermute | solution.py:31
  58.2 4.8 %collective-permute-start.23 = (f32[8,128]{1,0:T(8,128)S(1)}, f32[8,128]{1,0:T(8,128)S(1)}, u32[]{:S(2)}, u32[]{:S(2)}) collective-permute-start(f32[8,128]{1,0:T(8,128)S(1)} %add.31), channel_id=1, source_target_pairs={{0,68},{1,69},{2,70},{3,71},{4,64},{5,65},{6,66},{7,67},{8,76},{9,... | collective-permute-start | bytes 12296 | tf_op jit(solution)/shard_map/ppermute | solution.py:31
  63.0 5.1 %collective-permute-start.26 = (f32[8,128]{1,0:T(8,128)S(1)}, f32[8,128]{1,0:T(8,128)S(1)}, u32[]{:S(2)}, u32[]{:S(2)}) collective-permute-start(f32[8,128]{1,0:T(8,128)S(1)} %add.32), channel_id=1, source_target_pairs={{0,2},{1,3},{2,0},{3,1},{4,6},{5,7},{6,4},{7,5},{8,10},{9,11},{10,... | collective-permute-start | bytes 12296 | tf_op jit(solution)/shard_map/ppermute | solution.py:31
  63.7 4.8 %collective-permute-start.25 = (f32[8,128]{1,0:T(8,128)S(1)}, f32[8,128]{1,0:T(8,128)S(1)}, u32[]{:S(2)}, u32[]{:S(2)}) collective-permute-start(f32[8,128]{1,0:T(8,128)S(1)} %add.32), channel_id=1, source_target_pairs={{0,3},{1,2},{2,1},{3,0},{4,7},{5,6},{6,5},{7,4},{8,9},{9,8},{10,11... | collective-permute-start | bytes 12296 | tf_op jit(solution)/shard_map/ppermute | solution.py:31
  65.8 3.6 %collective-permute-start.24 = (f32[8,128]{1,0:T(8,128)S(1)}, f32[8,128]{1,0:T(8,128)S(1)}, u32[]{:S(2)}, u32[]{:S(2)}) collective-permute-start(f32[8,128]{1,0:T(8,128)S(1)} %add.32), channel_id=1, source_target_pairs={{0,1},{1,0},{2,3},{3,2},{4,5},{5,4},{6,7},{7,6},{8,11},{9,10},{10,... | collective-permute-start | bytes 12296 | tf_op jit(solution)/shard_map/ppermute | solution.py:31
  71.0 8.4 %collective-permute-start.30 = (bf16[2,2,2,16,1152]{4,3,2,1,0:T(8,128)(2,1)S(1)}, bf16[2,2,2,16,1152]{4,3,2,1,0:T(8,128)(2,1)S(1)}, u32[]{:S(2)}, u32[]{:S(2)}) collective-permute-start(bf16[2,2,2,16,1152]{4,3,2,1,0:T(8,128)(2,1)S(1)} %get-tuple-element.160), channel_id=1, source_target_pairs={{0,3},{1,2},{2,1},{3,0},{4,7},{5,6},{6,5},{7,4},{8,9},{9,8},{10,11... | collective-permute-start | bytes 884744 | tf_op jit(solution)/shard_map/ppermute | solution.py:31
  71.7 8.6 %collective-permute-start.29 = (bf16[2,2,2,16,1152]{4,3,2,1,0:T(8,128)(2,1)S(1)}, bf16[2,2,2,16,1152]{4,3,2,1,0:T(8,128)(2,1)S(1)}, u32[]{:S(2)}, u32[]{:S(2)}) collective-permute-start(bf16[2,2,2,16,1152]{4,3,2,1,0:T(8,128)(2,1)S(1)} %get-tuple-element.157), channel_id=1, source_target_pairs={{0,48},{1,49},{2,50},{3,51},{4,52},{5,53},{6,54},{7,55},{8,24},{9,... | collective-permute-start | bytes 884744 | tf_op jit(solution)/shard_map/ppermute | solution.py:31
  80.4 7.8 %collective-permute-start.31 = (bf16[2,32,1152]{2,1,0:T(8,128)(2,1)S(1)}, bf16[2,32,1152]{2,1,0:T(8,128)(2,1)S(1)}, u32[]{:S(2)}, u32[]{:S(2)}) collective-permute-start(bf16[2,32,1152]{2,1,0:T(8,128)(2,1)S(1)} %get-tuple-element.169), channel_id=1, source_target_pairs={{0,16},{1,17},{2,18},{3,19},{4,20},{5,21},{6,22},{7,23},{8,56},{9,... | collective-permute-start | bytes 442376 | tf_op jit(solution)/shard_map/ppermute | solution.py:31
  80.5 7.7 %collective-permute-start.32 = (bf16[2,32,1152]{2,1,0:T(8,128)(2,1)S(1)}, bf16[2,32,1152]{2,1,0:T(8,128)(2,1)S(1)}, u32[]{:S(2)}, u32[]{:S(2)}) collective-permute-start(bf16[2,32,1152]{2,1,0:T(8,128)(2,1)S(1)} %get-tuple-element.170), channel_id=1, source_target_pairs={{0,1},{1,0},{2,3},{3,2},{4,5},{5,4},{6,7},{7,6},{8,11},{9,10},{10,... | collective-permute-start | bytes 442376 | tf_op jit(solution)/shard_map/ppermute | solution.py:31
  80.6 7.6 %collective-permute-start.33 = (bf16[2,32,1152]{2,1,0:T(8,128)(2,1)S(1)}, bf16[2,32,1152]{2,1,0:T(8,128)(2,1)S(1)}, u32[]{:S(2)}, u32[]{:S(2)}) collective-permute-start(bf16[2,32,1152]{2,1,0:T(8,128)(2,1)S(1)} %get-tuple-element.171), channel_id=1, source_target_pairs={{0,17},{1,16},{2,19},{3,18},{4,21},{5,20},{6,23},{7,22},{8,59},{9,... | collective-permute-start | bytes 442376 | tf_op jit(solution)/shard_map/ppermute | solution.py:31
  88.4 5.6 %collective-permute-start.34 = (bf16[32,576]{1,0:T(8,128)(2,1)S(1)}, bf16[32,576]{1,0:T(8,128)(2,1)S(1)}, u32[]{:S(2)}, u32[]{:S(2)}) collective-permute-start(bf16[32,576]{1,0:T(8,128)(2,1)S(1)} %get-tuple-element.179), channel_id=1, source_target_pairs={{0,64},{1,65},{2,66},{3,67},{4,68},{5,69},{6,70},{7,71},{8,72},{9,... | collective-permute-start | bytes 110600 | tf_op jit(solution)/shard_map/ppermute | solution.py:31
  90.4 4.0 %collective-permute-start.35 = (bf16[32,576]{1,0:T(8,128)(2,1)S(1)}, bf16[32,576]{1,0:T(8,128)(2,1)S(1)}, u32[]{:S(2)}, u32[]{:S(2)}) collective-permute-start(bf16[32,576]{1,0:T(8,128)(2,1)S(1)} %get-tuple-element.180), channel_id=1, source_target_pairs={{0,4},{1,5},{2,6},{3,7},{4,0},{5,1},{6,2},{7,3},{8,12},{9,13},{10,... | collective-permute-start | bytes 110600 | tf_op jit(solution)/shard_map/ppermute | solution.py:31
  91.6 5.2 %collective-permute-start.36 = (bf16[32,576]{1,0:T(8,128)(2,1)S(1)}, bf16[32,576]{1,0:T(8,128)(2,1)S(1)}, u32[]{:S(2)}, u32[]{:S(2)}) collective-permute-start(bf16[32,576]{1,0:T(8,128)(2,1)S(1)} %get-tuple-element.181), channel_id=1, source_target_pairs={{0,68},{1,69},{2,70},{3,71},{4,64},{5,65},{6,66},{7,67},{8,76},{9,... | collective-permute-start | bytes 110600 | tf_op jit(solution)/shard_map/ppermute | solution.py:31
  (6 other events, 26.9 us)

commit v5 on v4

--- a/solution.py
+++ b/solution.py
@@ -370,8 +370,12 @@
     head_rows(0, 5, low_ref, high_ref, dlog_ref, out_ref, *scratch)
 
 
+def head_gradient_mid(low_ref, high_ref, dlog_ref, started_ref, out_ref, *scratch):
+    head_rows(5, 7, low_ref, high_ref, dlog_ref, out_ref, *scratch)
+
+
 def head_gradient_high(low_ref, high_ref, dlog_ref, started_ref, out_ref, *scratch):
-    head_rows(5, 9, low_ref, high_ref, dlog_ref, out_ref, *scratch)
+    head_rows(7, 9, low_ref, high_ref, dlog_ref, out_ref, *scratch)
 
 
 def run_head_gradient(kernel, low, high, dlog, started=()):
@@ -446,10 +450,12 @@
     p_got, q_got, head_grad = tie(p_got, q_got, head_grad)
     keep, *outs = run_join(p_keep, p_got, q_keep, q_got)
     got = [send(out, partner) for out, partner in zip(outs, (X1, Y1, XY1))]
-    head_grad = run_head_gradient(head_gradient_high, rows0, rows1, dlog, (head_grad,))
+    head_grad = run_head_gradient(head_gradient_mid, rows0, rows1, dlog, (head_grad,))
     *got, head_grad = tie(*got, head_grad)
     keep, *outs = run_split(me, keep, *got)
-    z_got = tie(send(outs[1], Z2), send(outs[0], ZL), send(outs[2], ZH))
+    z_got = send(outs[1], Z2), send(outs[0], ZL), send(outs[2], ZH)
+    head_grad = run_head_gradient(head_gradient_high, rows0, rows1, dlog, (head_grad,))
+    *z_got, head_grad = tie(*z_got, head_grad)
     hidden_grad = run_finish(keep, *z_got)
     return (own[:, 0], head_grad, hidden_grad)
 

time: 98.4 us -> 97.7 us (level)
  waiting for transfers between devices: 22.3 us -> 20.8 us
    ppermute x37, waiting for transfers between devices: 22.3 us -> 20.8 us  [send(): return lax.ppermute(array, AXES, partner)]
    pallas_call x2 -> x3, Pallas kernels: 9.38 us -> 9.72 us  [run_head_gradient(): call(kernel, 'vvv' + 'h' * len(started), [('h', (D, WIDTH), bf16)], scrat...]
  transfers between devices with their start and end apart: 37 -> 37, of which waited for: 19 -> 17; matrix products, arithmetic and copies ran while one was open for 1% -> 1% of each run, Pallas kernels for 32% -> 33%
where the time goes in v5:
time: 97.7 us; the launch traced here: 96.2 us
  starting transfers between devices  40.5 us (41%)
  Pallas kernels  33.3 us (34%)
  waiting for transfers between devices  20.8 us (21%)
    ppermute x37, starting transfers between devices, send(): return lax.ppermute(array, AXES, partner)  40.5 us
    ppermute x37, waiting for transfers between devices, send(): return lax.ppermute(array, AXES, partner)  20.8 us
    pallas_call x3, Pallas kernels, run_head_gradient(): call(kernel, 'vvv' + 'h' * len(started), [('h', (D, WIDTH), bf16)], scrat...  9.72 us
    pallas_call x1, Pallas kernels, run_begin(): call(begin, 'shhh', [BLOCKS] * 4 + [('v', (D, WIDTH), bf16), column, colu...  8.24 us
    pallas_call x2, Pallas kernels, run_forward(): call(kernel, 's' + 'v' * 10, [('v', (256, D), bf16), ('v', (256, WIDTH),...  5.96 us
    pallas_call x2, Pallas kernels, run_back(): return call(back, 'svv', [BLOCKS, BLOCKS], **BACK_COST)(me, rows, head)  5.87 us
  transfers between devices with their start and end apart: 37, of which 17 were waited for; matrix products, arithmetic and copies ran while one was open for 1% of the time, Pallas kernels for 33%

profile of v5, /device:TPU:0, one launch (start us, length us, event | category | flops | bytes accessed | tf_op | source)
XLA Modules:
  0.0 96.2 jit_solution(8917511960306939793)
XLA Ops:
  0.6 1.7 %collective-permute-start.3 = (bf16[32,4608]{1,0:T(8,128)(2,1)}, bf16[32,4608]{1,0:T(8,128)(2,1)S(1)}, u32[]{:S(2)}, u32[]{:S(2)}) collective-permute-start(bf16[32,4608]{1,0:T(8,128)(2,1)} %refs_1_.1), channel_id=1, source_target_pairs={{0,16},{1,17},{2,18},{3,19},{4,20},{5,21},{6,22},{7,23},{8,56},{9,... | collective-permute-start | bytes 884744 | tf_op jit(solution)/shard_map/ppermute | solution.py:31
  2.3 2.1 %collective-permute-start.2 = (bf16[32,4608]{1,0:T(8,128)(2,1)}, bf16[32,4608]{1,0:T(8,128)(2,1)S(1)}, u32[]{:S(2)}, u32[]{:S(2)}) collective-permute-start(bf16[32,4608]{1,0:T(8,128)(2,1)} %refs_1_.1), channel_id=1, source_target_pairs={{0,48},{1,49},{2,50},{3,51},{4,52},{5,53},{6,54},{7,55},{8,24},{9,... | collective-permute-start | bytes 884744 | tf_op jit(solution)/shard_map/ppermute | solution.py:31
  5.0 4.0 %collective-permute-start = (bf16[32,4608]{1,0:T(8,128)(2,1)}, bf16[32,4608]{1,0:T(8,128)(2,1)S(1)}, u32[]{:S(2)}, u32[]{:S(2)}) collective-permute-start(bf16[32,4608]{1,0:T(8,128)(2,1)} %refs_1_.1), channel_id=1, source_target_pairs={{0,68},{1,69},{2,70},{3,71},{4,64},{5,65},{6,66},{7,67},{8,76},{9,... | collective-permute-start | bytes 884744 | tf_op jit(solution)/shard_map/ppermute | solution.py:31
  9.1 8.2 %begin.1 = (bf16[4,4,32,1152]{3,2,1,0:T(8,128)(2,1)S(1)}, bf16[4,4,32,1152]{3,2,1,0:T(8,128)(2,1)S(1)}, bf16[4,4,32,1152]{3,2,1,0:T(8,128)(2,1)S(1)}, bf16[4,4,3...) custom-call(s32[1]{0:T(128)} %bitcast.me_ref.refs_0_, ...), custom_call_target="tpu_custom_call" | custom-call | flops 4831838208 | bytes 9437184 | tf_op jit(solution)/shard_map/begin/pallas_call | solution.py:231
  17.3 1.0 %collective-permute-done.1.refs_4_ = bf16[32,4608]{1,0:T(8,128)(2,1)S(1)} collective-permute-done((bf16[32,4608]{1,0:T(8,128)(2,1)}, bf16[32,4608]{1,0:T(8,128)(2,1)S(1)}, u32[]{:S(2)}, u32[]{:S(2)}) %collective-permute-start.1) | collective-permute-done | bytes 294944 | tf_op jit(solution)/shard_map/ppermute | solution.py:31
  19.8 3.5 %collective-permute-start.9 = (bf16[32,4608]{1,0:T(8,128)(2,1)S(1)}, bf16[32,4608]{1,0:T(8,128)(2,1)S(1)}, u32[]{:S(2)}, u32[]{:S(2)}) collective-permute-start(bf16[32,4608]{1,0:T(8,128)(2,1)S(1)} %collective-permute-done.1.refs_4_), channel_id=1, source_target_pairs={{0,68},{1,69},{2,70},{3,71},{4,64},{5,65},{6,66},{7,67},{8,76},{9,... | collective-permute-start | bytes 884744 | tf_op jit(solution)/shard_map/ppermute | solution.py:31
  23.3 1.2 %collective-permute-start.11 = (bf16[32,4608]{1,0:T(8,128)(2,1)S(1)}, bf16[32,4608]{1,0:T(8,128)(2,1)S(1)}, u32[]{:S(2)}, u32[]{:S(2)}) collective-permute-start(bf16[32,4608]{1,0:T(8,128)(2,1)S(1)} %collective-permute-done.refs_1_), channel_id=1, source_target_pairs={{0,8},{1,9},{2,10},{3,11},{4,12},{5,13},{6,14},{7,15},{8,0},{9,1},... | collective-permute-start | bytes 884744 | tf_op jit(solution)/shard_map/ppermute | solution.py:31
  24.6 1.7 %collective-permute-start.10 = (bf16[32,4608]{1,0:T(8,128)(2,1)S(1)}, bf16[32,4608]{1,0:T(8,128)(2,1)S(1)}, u32[]{:S(2)}, u32[]{:S(2)}) collective-permute-start(bf16[32,4608]{1,0:T(8,128)(2,1)S(1)} %collective-permute-done.refs_1_), channel_id=1, source_target_pairs={{0,48},{1,49},{2,50},{3,51},{4,52},{5,53},{6,54},{7,55},{8,24},{9,... | collective-permute-start | bytes 884744 | tf_op jit(solution)/shard_map/ppermute | solution.py:31
  26.2 3.0 %forward_low.1 = (bf16[256,4608]{1,0:T(8,128)(2,1)S(1)}, f32[256,1024]{1,0:T(8,128)S(1)}, bf16[256,1024]{1,0:T(8,128)(2,1)S(1)}, f32[256,128]{1,0:T(8,128)S(1)}, f32[256,128]{1,0:T(8,128)S(1)}) custom-call(s32[1]{0:T(128)} %bitcast.me_ref.refs_0_, bf16[32,4608]{1,0:T(8,128)(2,1)S(1)} %copy-done, bf16[32,4608]{1,0:T(8,128)(2,1)S(1)} %collective-permute-done.3.refs_2_, ...), custom_call_target="tpu_custom_call" | custom-call | flops 2415919104 | bytes 9437184 | tf_op jit(solution)/shard_map/forward_low/pallas_call | solution.py:116
  29.2 2.9 %back.2 = (bf16[4,4,32,1152]{3,2,1,0:T(8,128)(2,1)S(1)}, bf16[4,4,32,1152]{3,2,1,0:T(8,128)(2,1)S(1)}) custom-call(s32[1]{0:T(128)} %bitcast.me_ref.refs_0_, bf16[256,1024]{1,0:T(8,128)(2,1)S(1)} %get-tuple-element.106.rows_ref, bf16[4608,1024]{1,0:T(8,128)(2,1)S(1)} %get-tuple-element.104.refs_10_.head_ref), custom_call_target="tpu_custom_call" | custom-call | flops 2415919104 | bytes 9437184 | tf_op jit(solution)/shard_map/back/pallas_call | solution.py:196
  33.0 1.1 %collective-permute-done.12.refs_6_ = bf16[32,4608]{1,0:T(8,128)(2,1)S(1)} collective-permute-done((bf16[32,4608]{1,0:T(8,128)(2,1)S(1)}, bf16[32,4608]{1,0:T(8,128)(2,1)S(1)}, u32[]{:S(2)}, u32[]{:S(2)}) %collective-permute-start.12) | collective-permute-done | bytes 294944 | tf_op jit(solution)/shard_map/ppermute | solution.py:31
  35.1 3.0 %forward_high.1 = (bf16[256,4608]{1,0:T(8,128)(2,1)S(1)}, f32[256,1024]{1,0:T(8,128)S(1)}, bf16[256,1024]{1,0:T(8,128)(2,1)S(1)}, f32[256,128]{1,0:T(8,128)S(1)}, f32[256,128]{1,0:T(8,128)S(1)}) custom-call(s32[1]{0:T(128)} %bitcast.me_ref.refs_0_, bf16[32,4608]{1,0:T(8,128)(2,1)S(1)} %collective-permute-done.refs_1_, ...), custom_call_target="tpu_custom_call" | custom-call | flops 2415919104 | bytes 9437184 | tf_op jit(solution)/shard_map/forward_high/pallas_call | solution.py:116
  39.0 2.9 %back.3 = (bf16[4,4,32,1152]{3,2,1,0:T(8,128)(2,1)S(1)}, bf16[4,4,32,1152]{3,2,1,0:T(8,128)(2,1)S(1)}) custom-call(s32[1]{0:T(128)} %bitcast.me_ref.refs_0_, bf16[256,1024]{1,0:T(8,128)(2,1)S(1)} %get-tuple-element.128.rows_ref, bf16[4608,1024]{1,0:T(8,128)(2,1)S(1)} %get-tuple-element.104.refs_10_.head_ref), custom_call_target="tpu_custom_call" | custom-call | flops 2415919104 | bytes 9437184 | tf_op jit(solution)/shard_map/back/pallas_call | solution.py:196
  42.7 1.3 %collective-permute-start.19 = (bf16[4,4,32,1152]{3,2,1,0:T(8,128)(2,1)S(1)}, bf16[4,4,32,1152]{3,2,1,0:T(8,128)(2,1)S(1)}, u32[]{:S(2)}, u32[]{:S(2)}) collective-permute-start(bf16[4,4,32,1152]{3,2,1,0:T(8,128)(2,1)S(1)} %get-tuple-element.134), channel_id=1, source_target_pairs={{0,8},{1,9},{2,10},{3,11},{4,12},{5,13},{6,14},{7,15},{8,0},{9,1},... | collective-permute-start | bytes 3538952 | tf_op jit(solution)/shard_map/ppermute | solution.py:31
  44.0 1.6 %collective-permute-start.20 = (f32[8,128]{1,0:T(8,128)S(1)}, f32[8,128]{1,0:T(8,128)S(1)}, u32[]{:S(2)}, u32[]{:S(2)}) collective-permute-start(f32[8,128]{1,0:T(8,128)S(1)} %add.28), channel_id=1, source_target_pairs={{0,48},{1,49},{2,50},{3,51},{4,52},{5,53},{6,54},{7,55},{8,24},{9,... | collective-permute-start | bytes 12296 | tf_op jit(solution)/shard_map/ppermute | solution.py:31
  45.6 3.2 %collective-permute-done.20 = f32[8,128]{1,0:T(8,128)S(1)} collective-permute-done((f32[8,128]{1,0:T(8,128)S(1)}, f32[8,128]{1,0:T(8,128)S(1)}, u32[]{:S(2)}, u32[]{:S(2)}) %collective-permute-start.20) | collective-permute-done | bytes 4128 | tf_op jit(solution)/shard_map/ppermute | solution.py:31
  50.0 3.0 %collective-permute-start.27 = (bf16[2,2,2,2,32,1152]{5,4,3,2,1,0:T(8,128)(2,1)S(1)}, bf16[2,2,2,2,32,1152]{5,4,3,2,1,0:T(8,128)(2,1)S(1)}, u32[]{:S(2)}, u32[]{:S(2)}) collective-permute-start(bf16[2,2,2,2,32,1152]{5,4,3,2,1,0:T(8,128)(2,1)S(1)} %get-tuple-element.146), channel_id=1, source_target_pairs={{0,3},{1,2},{2,1},{3,0},{4,7},{5,6},{6,5},{7,4},{8,9},{9,8},{10,11... | collective-permute-start | bytes 3538952 | tf_op jit(solution)/shard_map/ppermute | solution.py:31
  53.0 1.6 %collective-permute-start.28 = (bf16[2,2,2,2,32,1152]{5,4,3,2,1,0:T(8,128)(2,1)S(1)}, bf16[2,2,2,2,32,1152]{5,4,3,2,1,0:T(8,128)(2,1)S(1)}, u32[]{:S(2)}, u32[]{:S(2)}) collective-permute-start(bf16[2,2,2,2,32,1152]{5,4,3,2,1,0:T(8,128)(2,1)S(1)} %get-tuple-element.147), channel_id=1, source_target_pairs={{0,48},{1,49},{2,50},{3,51},{4,52},{5,53},{6,54},{7,55},{8,24},{9,... | collective-permute-start | bytes 3538952 | tf_op jit(solution)/shard_map/ppermute | solution.py:31
  54.6 3.6 %collective-permute-done.22 = f32[8,128]{1,0:T(8,128)S(1)} collective-permute-done((f32[8,128]{1,0:T(8,128)S(1)}, f32[8,128]{1,0:T(8,128)S(1)}, u32[]{:S(2)}, u32[]{:S(2)}) %collective-permute-start.22) | collective-permute-done | bytes 4128 | tf_op jit(solution)/shard_map/ppermute | solution.py:31
  58.2 2.2 %collective-permute-start.23 = (f32[8,128]{1,0:T(8,128)S(1)}, f32[8,128]{1,0:T(8,128)S(1)}, u32[]{:S(2)}, u32[]{:S(2)}) collective-permute-start(f32[8,128]{1,0:T(8,128)S(1)} %add.31), channel_id=1, source_target_pairs={{0,68},{1,69},{2,70},{3,71},{4,64},{5,65},{6,66},{7,67},{8,76},{9,... | collective-permute-start | bytes 12296 | tf_op jit(solution)/shard_map/ppermute | solution.py:31
  60.4 2.6 %collective-permute-done.23 = f32[8,128]{1,0:T(8,128)S(1)} collective-permute-done((f32[8,128]{1,0:T(8,128)S(1)}, f32[8,128]{1,0:T(8,128)S(1)}, u32[]{:S(2)}, u32[]{:S(2)}) %collective-permute-start.23) | collective-permute-done | bytes 4128 | tf_op jit(solution)/shard_map/ppermute | solution.py:31
  63.7 2.2 %collective-permute-start.25 = (f32[8,128]{1,0:T(8,128)S(1)}, f32[8,128]{1,0:T(8,128)S(1)}, u32[]{:S(2)}, u32[]{:S(2)}) collective-permute-start(f32[8,128]{1,0:T(8,128)S(1)} %add.32), channel_id=1, source_target_pairs={{0,3},{1,2},{2,1},{3,0},{4,7},{5,6},{6,5},{7,4},{8,9},{9,8},{10,11... | collective-permute-start | bytes 12296 | tf_op jit(solution)/shard_map/ppermute | solution.py:31
  66.5 1.6 %collective-permute-done.26 = f32[8,128]{1,0:T(8,128)S(1)} collective-permute-done((f32[8,128]{1,0:T(8,128)S(1)}, f32[8,128]{1,0:T(8,128)S(1)}, u32[]{:S(2)}, u32[]{:S(2)}) %collective-permute-start.26) | collective-permute-done | bytes 4128 | tf_op jit(solution)/shard_map/ppermute | solution.py:31
  71.7 1.7 %collective-permute-start.29 = (bf16[2,2,2,16,1152]{4,3,2,1,0:T(8,128)(2,1)S(1)}, bf16[2,2,2,16,1152]{4,3,2,1,0:T(8,128)(2,1)S(1)}, u32[]{:S(2)}, u32[]{:S(2)}) collective-permute-start(bf16[2,2,2,16,1152]{4,3,2,1,0:T(8,128)(2,1)S(1)} %get-tuple-element.158), channel_id=1, source_target_pairs={{0,48},{1,49},{2,50},{3,51},{4,52},{5,53},{6,54},{7,55},{8,24},{9,... | collective-permute-start | bytes 884744 | tf_op jit(solution)/shard_map/ppermute | solution.py:31
  74.8 5.2 %head_gradient_low.1.started_ref = bf16[4608,1024]{1,0:T(8,128)(2,1)} custom-call(bf16[256,4608]{1,0:T(8,128)(2,1)S(1)} %get-tuple-element.162.low_ref, bf16[256,4608]{1,0:T(8,128)(2,1)S(1)} %get-tuple-element.163.high_ref, bf16[512,1024]{1,0:T(8,128)(2,1)S(1)} %dlogits.1.dlog_ref), custom_call_target="tpu_custom_call" | custom-call | flops 2415919104 | bytes 4718592 | tf_op jit(solution)/shard_map/head_gradient_low/pallas_call | solution.py:382
  80.5 3.2 %collective-permute-start.33 = (bf16[2,32,1152]{2,1,0:T(8,128)(2,1)S(1)}, bf16[2,32,1152]{2,1,0:T(8,128)(2,1)S(1)}, u32[]{:S(2)}, u32[]{:S(2)}) collective-permute-start(bf16[2,32,1152]{2,1,0:T(8,128)(2,1)S(1)} %get-tuple-element.173), channel_id=1, source_target_pairs={{0,17},{1,16},{2,19},{3,18},{4,21},{5,20},{6,23},{7,22},{8,59},{9,... | collective-permute-start | bytes 442376 | tf_op jit(solution)/shard_map/ppermute | solution.py:31
  83.7 2.3 %head_gradient_mid.1.started_ref = bf16[4608,1024]{1,0:T(8,128)(2,1)} custom-call(bf16[256,4608]{1,0:T(8,128)(2,1)S(1)} %get-tuple-element.162.low_ref, bf16[256,4608]{1,0:T(8,128)(2,1)S(1)} %get-tuple-element.163.high_ref, bf16[512,1024]{1,0:T(8,128)(2,1)S(1)} %dlogits.1.dlog_ref, ...), custom_call_target="tpu_custom_call", output_to_operand_aliasing={{}: (3, {})} | custom-call | flops 2415919104 | bytes 4718592 | tf_op jit(solution)/shard_map/head_gradient_mid/pallas_call | solution.py:382
  86.0 1.0 %collective-permute-done.32.refs_2_ = bf16[2,32,1152]{2,1,0:T(8,128)(2,1)S(1)} collective-permute-done((bf16[2,32,1152]{2,1,0:T(8,128)(2,1)S(1)}, bf16[2,32,1152]{2,1,0:T(8,128)(2,1)S(1)}, u32[]{:S(2)}, u32[]{:S(2)}) %collective-permute-start.32) | collective-permute-done | bytes 147488 | tf_op jit(solution)/shard_map/ppermute | solution.py:31
  87.2 2.0 %collective-permute-start.34 = (bf16[32,576]{1,0:T(8,128)(2,1)S(1)}, bf16[32,576]{1,0:T(8,128)(2,1)S(1)}, u32[]{:S(2)}, u32[]{:S(2)}) collective-permute-start(bf16[32,576]{1,0:T(8,128)(2,1)S(1)} %get-tuple-element.178), channel_id=1, source_target_pairs={{0,64},{1,65},{2,66},{3,67},{4,68},{5,69},{6,70},{7,71},{8,72},{9,... | collective-permute-start | bytes 110600 | tf_op jit(solution)/shard_map/ppermute | solution.py:31
  89.2 1.1 %collective-permute-start.35 = (bf16[32,576]{1,0:T(8,128)(2,1)S(1)}, bf16[32,576]{1,0:T(8,128)(2,1)S(1)}, u32[]{:S(2)}, u32[]{:S(2)}) collective-permute-start(bf16[32,576]{1,0:T(8,128)(2,1)S(1)} %get-tuple-element.179), channel_id=1, source_target_pairs={{0,4},{1,5},{2,6},{3,7},{4,0},{5,1},{6,2},{7,3},{8,12},{9,13},{10,... | collective-permute-start | bytes 110600 | tf_op jit(solution)/shard_map/ppermute | solution.py:31
  91.4 2.3 %head_gradient_high.1 = bf16[4608,1024]{1,0:T(8,128)(2,1)} custom-call(bf16[256,4608]{1,0:T(8,128)(2,1)S(1)} %get-tuple-element.162.low_ref, bf16[256,4608]{1,0:T(8,128)(2,1)S(1)} %get-tuple-element.163.high_ref, bf16[512,1024]{1,0:T(8,128)(2,1)S(1)} %dlogits.1.dlog_ref, bf16[4608,1024]{1,0:T(8,128)(2,1)} %head_gradient_mid.1.started_ref), custom_call_target="tpu_custom_call", output_to_operand_aliasing={{}: (3, {})} | custom-call | flops 2415919104 | bytes 4718592 | tf_op jit(solution)/shard_map/head_gradient_high/pallas_call | solution.py:382
  93.7 1.9 %collective-permute-done.36.refs_3_ = bf16[32,576]{1,0:T(8,128)(2,1)S(1)} collective-permute-done((bf16[32,576]{1,0:T(8,128)(2,1)S(1)}, bf16[32,576]{1,0:T(8,128)(2,1)S(1)}, u32[]{:S(2)}, u32[]{:S(2)}) %collective-permute-start.36) | collective-permute-done | bytes 36896 | tf_op jit(solution)/shard_map/ppermute | solution.py:31
  (68 shorter events, 15.4 us)
Async XLA Ops:
  0.6 16.7 %collective-permute-start.3 = (bf16[32,4608]{1,0:T(8,128)(2,1)}, bf16[32,4608]{1,0:T(8,128)(2,1)S(1)}, u32[]{:S(2)}, u32[]{:S(2)}) collective-permute-start(bf16[32,4608]{1,0:T(8,128)(2,1)} %refs_1_.1), channel_id=1, source_target_pairs={{0,16},{1,17},{2,18},{3,19},{4,20},{5,21},{6,22},{7,23},{8,56},{9,... | collective-permute-start | bytes 884744 | tf_op jit(solution)/shard_map/ppermute | solution.py:31
  2.3 15.0 %collective-permute-start.2 = (bf16[32,4608]{1,0:T(8,128)(2,1)}, bf16[32,4608]{1,0:T(8,128)(2,1)S(1)}, u32[]{:S(2)}, u32[]{:S(2)}) collective-permute-start(bf16[32,4608]{1,0:T(8,128)(2,1)} %refs_1_.1), channel_id=1, source_target_pairs={{0,48},{1,49},{2,50},{3,51},{4,52},{5,53},{6,54},{7,55},{8,24},{9,... | collective-permute-start | bytes 884744 | tf_op jit(solution)/shard_map/ppermute | solution.py:31
  4.4 14.0 %collective-permute-start.1 = (bf16[32,4608]{1,0:T(8,128)(2,1)}, bf16[32,4608]{1,0:T(8,128)(2,1)S(1)}, u32[]{:S(2)}, u32[]{:S(2)}) collective-permute-start(bf16[32,4608]{1,0:T(8,128)(2,1)} %refs_1_.1), channel_id=1, source_target_pairs={{0,32},{1,33},{2,34},{3,35},{4,36},{5,37},{6,38},{7,39},{8,40},{9,... | collective-permute-start | bytes 884744 | tf_op jit(solution)/shard_map/ppermute | solution.py:31
  5.0 13.3 %collective-permute-start = (bf16[32,4608]{1,0:T(8,128)(2,1)}, bf16[32,4608]{1,0:T(8,128)(2,1)S(1)}, u32[]{:S(2)}, u32[]{:S(2)}) collective-permute-start(bf16[32,4608]{1,0:T(8,128)(2,1)} %refs_1_.1), channel_id=1, source_target_pairs={{0,68},{1,69},{2,70},{3,71},{4,64},{5,65},{6,66},{7,67},{8,76},{9,... | collective-permute-start | bytes 884744 | tf_op jit(solution)/shard_map/ppermute | solution.py:31
  9.1 10.8 %collective-permute-start.5 = (bf16[32,4608]{1,0:T(8,128)(2,1)}, bf16[32,4608]{1,0:T(8,128)(2,1)S(1)}, u32[]{:S(2)}, u32[]{:S(2)}) collective-permute-start(bf16[32,4608]{1,0:T(8,128)(2,1)} %refs_1_.1), channel_id=1, source_target_pairs={{0,8},{1,9},{2,10},{3,11},{4,12},{5,13},{6,14},{7,15},{8,0},{9,1},... | collective-permute-start | bytes 884744 | tf_op jit(solution)/shard_map/ppermute | solution.py:31
  18.4 4.9 %collective-permute-start.6 = (bf16[32,4608]{1,0:T(8,128)(2,1)S(1)}, bf16[32,4608]{1,0:T(8,128)(2,1)S(1)}, u32[]{:S(2)}, u32[]{:S(2)}) collective-permute-start(bf16[32,4608]{1,0:T(8,128)(2,1)S(1)} %collective-permute-done.3.refs_2_), channel_id=1, source_target_pairs={{0,8},{1,9},{2,10},{3,11},{4,12},{5,13},{6,14},{7,15},{8,0},{9,1},... | collective-permute-start | bytes 884744 | tf_op jit(solution)/shard_map/ppermute | solution.py:31
  18.4 6.2 %collective-permute-start.7 = (bf16[32,4608]{1,0:T(8,128)(2,1)S(1)}, bf16[32,4608]{1,0:T(8,128)(2,1)S(1)}, u32[]{:S(2)}, u32[]{:S(2)}) collective-permute-start(bf16[32,4608]{1,0:T(8,128)(2,1)S(1)} %collective-permute-done.2.refs_3_), channel_id=1, source_target_pairs={{0,8},{1,9},{2,10},{3,11},{4,12},{5,13},{6,14},{7,15},{8,0},{9,1},... | collective-permute-start | bytes 884744 | tf_op jit(solution)/shard_map/ppermute | solution.py:31
  18.9 7.3 %collective-permute-start.8 = (bf16[32,4608]{1,0:T(8,128)(2,1)S(1)}, bf16[32,4608]{1,0:T(8,128)(2,1)S(1)}, u32[]{:S(2)}, u32[]{:S(2)}) collective-permute-start(bf16[32,4608]{1,0:T(8,128)(2,1)S(1)} %collective-permute-done.1.refs_4_), channel_id=1, source_target_pairs={{0,8},{1,9},{2,10},{3,11},{4,12},{5,13},{6,14},{7,15},{8,0},{9,1},... | collective-permute-start | bytes 884744 | tf_op jit(solution)/shard_map/ppermute | solution.py:31
  18.9 10.4 %collective-permute-start.4 = (bf16[32,4608]{1,0:T(8,128)(2,1)S(1)}, bf16[32,4608]{1,0:T(8,128)(2,1)S(1)}, u32[]{:S(2)}, u32[]{:S(2)}) collective-permute-start(bf16[32,4608]{1,0:T(8,128)(2,1)S(1)} %collective-permute-done.refs_1_), channel_id=1, source_target_pairs={{0,16},{1,17},{2,18},{3,19},{4,20},{5,21},{6,22},{7,23},{8,56},{9,... | collective-permute-start | bytes 884744 | tf_op jit(solution)/shard_map/ppermute | solution.py:31
  19.8 12.4 %collective-permute-start.9 = (bf16[32,4608]{1,0:T(8,128)(2,1)S(1)}, bf16[32,4608]{1,0:T(8,128)(2,1)S(1)}, u32[]{:S(2)}, u32[]{:S(2)}) collective-permute-start(bf16[32,4608]{1,0:T(8,128)(2,1)S(1)} %collective-permute-done.1.refs_4_), channel_id=1, source_target_pairs={{0,68},{1,69},{2,70},{3,71},{4,64},{5,65},{6,66},{7,67},{8,76},{9,... | collective-permute-start | bytes 884744 | tf_op jit(solution)/shard_map/ppermute | solution.py:31
  23.3 9.7 %collective-permute-start.11 = (bf16[32,4608]{1,0:T(8,128)(2,1)S(1)}, bf16[32,4608]{1,0:T(8,128)(2,1)S(1)}, u32[]{:S(2)}, u32[]{:S(2)}) collective-permute-start(bf16[32,4608]{1,0:T(8,128)(2,1)S(1)} %collective-permute-done.refs_1_), channel_id=1, source_target_pairs={{0,8},{1,9},{2,10},{3,11},{4,12},{5,13},{6,14},{7,15},{8,0},{9,1},... | collective-permute-start | bytes 884744 | tf_op jit(solution)/shard_map/ppermute | solution.py:31
  24.6 7.9 %collective-permute-start.10 = (bf16[32,4608]{1,0:T(8,128)(2,1)S(1)}, bf16[32,4608]{1,0:T(8,128)(2,1)S(1)}, u32[]{:S(2)}, u32[]{:S(2)}) collective-permute-start(bf16[32,4608]{1,0:T(8,128)(2,1)S(1)} %collective-permute-done.refs_1_), channel_id=1, source_target_pairs={{0,48},{1,49},{2,50},{3,51},{4,52},{5,53},{6,54},{7,55},{8,24},{9,... | collective-permute-start | bytes 884744 | tf_op jit(solution)/shard_map/ppermute | solution.py:31
  38.0 4.5 %collective-permute-start.17 = (bf16[4,4,32,1152]{3,2,1,0:T(8,128)(2,1)S(1)}, bf16[4,4,32,1152]{3,2,1,0:T(8,128)(2,1)S(1)}, u32[]{:S(2)}, u32[]{:S(2)}) collective-permute-start(bf16[4,4,32,1152]{3,2,1,0:T(8,128)(2,1)S(1)} %get-tuple-element.130), channel_id=1, source_target_pairs={{0,8},{1,9},{2,10},{3,11},{4,12},{5,13},{6,14},{7,15},{8,0},{9,1},... | collective-permute-start | bytes 3538952 | tf_op jit(solution)/shard_map/ppermute | solution.py:31
  38.5 4.2 %collective-permute-start.18 = (bf16[4,4,32,1152]{3,2,1,0:T(8,128)(2,1)S(1)}, bf16[4,4,32,1152]{3,2,1,0:T(8,128)(2,1)S(1)}, u32[]{:S(2)}, u32[]{:S(2)}) collective-permute-start(bf16[4,4,32,1152]{3,2,1,0:T(8,128)(2,1)S(1)} %get-tuple-element.131), channel_id=1, source_target_pairs={{0,8},{1,9},{2,10},{3,11},{4,12},{5,13},{6,14},{7,15},{8,0},{9,1},... | collective-permute-start | bytes 3538952 | tf_op jit(solution)/shard_map/ppermute | solution.py:31
  38.9 3.7 %collective-permute-start.16 = (f32[8,128]{1,0:T(8,128)S(1)}, f32[8,128]{1,0:T(8,128)S(1)}, u32[]{:S(2)}, u32[]{:S(2)}) collective-permute-start(f32[8,128]{1,0:T(8,128)S(1)} %pack.1), channel_id=1, source_target_pairs={{0,16},{1,17},{2,18},{3,19},{4,20},{5,21},{6,22},{7,23},{8,56},{9,... | collective-permute-start | bytes 12296 | tf_op jit(solution)/shard_map/ppermute | solution.py:31
  42.7 6.2 %collective-permute-start.19 = (bf16[4,4,32,1152]{3,2,1,0:T(8,128)(2,1)S(1)}, bf16[4,4,32,1152]{3,2,1,0:T(8,128)(2,1)S(1)}, u32[]{:S(2)}, u32[]{:S(2)}) collective-permute-start(bf16[4,4,32,1152]{3,2,1,0:T(8,128)(2,1)S(1)} %get-tuple-element.134), channel_id=1, source_target_pairs={{0,8},{1,9},{2,10},{3,11},{4,12},{5,13},{6,14},{7,15},{8,0},{9,1},... | collective-permute-start | bytes 3538952 | tf_op jit(solution)/shard_map/ppermute | solution.py:31
  44.0 4.8 %collective-permute-start.20 = (f32[8,128]{1,0:T(8,128)S(1)}, f32[8,128]{1,0:T(8,128)S(1)}, u32[]{:S(2)}, u32[]{:S(2)}) collective-permute-start(f32[8,128]{1,0:T(8,128)S(1)} %add.28), channel_id=1, source_target_pairs={{0,48},{1,49},{2,50},{3,51},{4,52},{5,53},{6,54},{7,55},{8,24},{9,... | collective-permute-start | bytes 12296 | tf_op jit(solution)/shard_map/ppermute | solution.py:31
  50.0 19.5 %collective-permute-start.27 = (bf16[2,2,2,2,32,1152]{5,4,3,2,1,0:T(8,128)(2,1)S(1)}, bf16[2,2,2,2,32,1152]{5,4,3,2,1,0:T(8,128)(2,1)S(1)}, u32[]{:S(2)}, u32[]{:S(2)}) collective-permute-start(bf16[2,2,2,2,32,1152]{5,4,3,2,1,0:T(8,128)(2,1)S(1)} %get-tuple-element.146), channel_id=1, source_target_pairs={{0,3},{1,2},{2,1},{3,0},{4,7},{5,6},{6,5},{7,4},{8,9},{9,8},{10,11... | collective-permute-start | bytes 3538952 | tf_op jit(solution)/shard_map/ppermute | solution.py:31
  53.0 17.4 %collective-permute-start.28 = (bf16[2,2,2,2,32,1152]{5,4,3,2,1,0:T(8,128)(2,1)S(1)}, bf16[2,2,2,2,32,1152]{5,4,3,2,1,0:T(8,128)(2,1)S(1)}, u32[]{:S(2)}, u32[]{:S(2)}) collective-permute-start(bf16[2,2,2,2,32,1152]{5,4,3,2,1,0:T(8,128)(2,1)S(1)} %get-tuple-element.147), channel_id=1, source_target_pairs={{0,48},{1,49},{2,50},{3,51},{4,52},{5,53},{6,54},{7,55},{8,24},{9,... | collective-permute-start | bytes 3538952 | tf_op jit(solution)/shard_map/ppermute | solution.py:31
  54.6 3.6 %collective-permute-start.22 = (f32[8,128]{1,0:T(8,128)S(1)}, f32[8,128]{1,0:T(8,128)S(1)}, u32[]{:S(2)}, u32[]{:S(2)}) collective-permute-start(f32[8,128]{1,0:T(8,128)S(1)} %add.30), channel_id=1, source_target_pairs={{0,4},{1,5},{2,6},{3,7},{4,0},{5,1},{6,2},{7,3},{8,12},{9,13},{10,... | collective-permute-start | bytes 12296 | tf_op jit(solution)/shard_map/ppermute | solution.py:31
  58.2 4.8 %collective-permute-start.23 = (f32[8,128]{1,0:T(8,128)S(1)}, f32[8,128]{1,0:T(8,128)S(1)}, u32[]{:S(2)}, u32[]{:S(2)}) collective-permute-start(f32[8,128]{1,0:T(8,128)S(1)} %add.31), channel_id=1, source_target_pairs={{0,68},{1,69},{2,70},{3,71},{4,64},{5,65},{6,66},{7,67},{8,76},{9,... | collective-permute-start | bytes 12296 | tf_op jit(solution)/shard_map/ppermute | solution.py:31
  63.0 5.1 %collective-permute-start.26 = (f32[8,128]{1,0:T(8,128)S(1)}, f32[8,128]{1,0:T(8,128)S(1)}, u32[]{:S(2)}, u32[]{:S(2)}) collective-permute-start(f32[8,128]{1,0:T(8,128)S(1)} %add.32), channel_id=1, source_target_pairs={{0,2},{1,3},{2,0},{3,1},{4,6},{5,7},{6,4},{7,5},{8,10},{9,11},{10,... | collective-permute-start | bytes 12296 | tf_op jit(solution)/shard_map/ppermute | solution.py:31
  63.7 4.8 %collective-permute-start.25 = (f32[8,128]{1,0:T(8,128)S(1)}, f32[8,128]{1,0:T(8,128)S(1)}, u32[]{:S(2)}, u32[]{:S(2)}) collective-permute-start(f32[8,128]{1,0:T(8,128)S(1)} %add.32), channel_id=1, source_target_pairs={{0,3},{1,2},{2,1},{3,0},{4,7},{5,6},{6,5},{7,4},{8,9},{9,8},{10,11... | collective-permute-start | bytes 12296 | tf_op jit(solution)/shard_map/ppermute | solution.py:31
  65.8 3.6 %collective-permute-start.24 = (f32[8,128]{1,0:T(8,128)S(1)}, f32[8,128]{1,0:T(8,128)S(1)}, u32[]{:S(2)}, u32[]{:S(2)}) collective-permute-start(f32[8,128]{1,0:T(8,128)S(1)} %add.32), channel_id=1, source_target_pairs={{0,1},{1,0},{2,3},{3,2},{4,5},{5,4},{6,7},{7,6},{8,11},{9,10},{10,... | collective-permute-start | bytes 12296 | tf_op jit(solution)/shard_map/ppermute | solution.py:31
  71.3 8.7 %collective-permute-start.30 = (bf16[2,2,2,16,1152]{4,3,2,1,0:T(8,128)(2,1)S(1)}, bf16[2,2,2,16,1152]{4,3,2,1,0:T(8,128)(2,1)S(1)}, u32[]{:S(2)}, u32[]{:S(2)}) collective-permute-start(bf16[2,2,2,16,1152]{4,3,2,1,0:T(8,128)(2,1)S(1)} %get-tuple-element.161), channel_id=1, source_target_pairs={{0,3},{1,2},{2,1},{3,0},{4,7},{5,6},{6,5},{7,4},{8,9},{9,8},{10,11... | collective-permute-start | bytes 884744 | tf_op jit(solution)/shard_map/ppermute | solution.py:31
  71.7 8.3 %collective-permute-start.29 = (bf16[2,2,2,16,1152]{4,3,2,1,0:T(8,128)(2,1)S(1)}, bf16[2,2,2,16,1152]{4,3,2,1,0:T(8,128)(2,1)S(1)}, u32[]{:S(2)}, u32[]{:S(2)}) collective-permute-start(bf16[2,2,2,16,1152]{4,3,2,1,0:T(8,128)(2,1)S(1)} %get-tuple-element.158), channel_id=1, source_target_pairs={{0,48},{1,49},{2,50},{3,51},{4,52},{5,53},{6,54},{7,55},{8,24},{9,... | collective-permute-start | bytes 884744 | tf_op jit(solution)/shard_map/ppermute | solution.py:31
  80.1 5.9 %collective-permute-start.31 = (bf16[2,32,1152]{2,1,0:T(8,128)(2,1)S(1)}, bf16[2,32,1152]{2,1,0:T(8,128)(2,1)S(1)}, u32[]{:S(2)}, u32[]{:S(2)}) collective-permute-start(bf16[2,32,1152]{2,1,0:T(8,128)(2,1)S(1)} %get-tuple-element.171), channel_id=1, source_target_pairs={{0,16},{1,17},{2,18},{3,19},{4,20},{5,21},{6,22},{7,23},{8,56},{9,... | collective-permute-start | bytes 442376 | tf_op jit(solution)/shard_map/ppermute | solution.py:31
  80.2 6.8 %collective-permute-start.32 = (bf16[2,32,1152]{2,1,0:T(8,128)(2,1)S(1)}, bf16[2,32,1152]{2,1,0:T(8,128)(2,1)S(1)}, u32[]{:S(2)}, u32[]{:S(2)}) collective-permute-start(bf16[2,32,1152]{2,1,0:T(8,128)(2,1)S(1)} %get-tuple-element.172), channel_id=1, source_target_pairs={{0,1},{1,0},{2,3},{3,2},{4,5},{5,4},{6,7},{7,6},{8,11},{9,10},{10,... | collective-permute-start | bytes 442376 | tf_op jit(solution)/shard_map/ppermute | solution.py:31
  80.5 6.5 %collective-permute-start.33 = (bf16[2,32,1152]{2,1,0:T(8,128)(2,1)S(1)}, bf16[2,32,1152]{2,1,0:T(8,128)(2,1)S(1)}, u32[]{:S(2)}, u32[]{:S(2)}) collective-permute-start(bf16[2,32,1152]{2,1,0:T(8,128)(2,1)S(1)} %get-tuple-element.173), channel_id=1, source_target_pairs={{0,17},{1,16},{2,19},{3,18},{4,21},{5,20},{6,23},{7,22},{8,59},{9,... | collective-permute-start | bytes 442376 | tf_op jit(solution)/shard_map/ppermute | solution.py:31
  87.2 6.5 %collective-permute-start.34 = (bf16[32,576]{1,0:T(8,128)(2,1)S(1)}, bf16[32,576]{1,0:T(8,128)(2,1)S(1)}, u32[]{:S(2)}, u32[]{:S(2)}) collective-permute-start(bf16[32,576]{1,0:T(8,128)(2,1)S(1)} %get-tuple-element.178), channel_id=1, source_target_pairs={{0,64},{1,65},{2,66},{3,67},{4,68},{5,69},{6,70},{7,71},{8,72},{9,... | collective-permute-start | bytes 110600 | tf_op jit(solution)/shard_map/ppermute | solution.py:31
  89.2 4.5 %collective-permute-start.35 = (bf16[32,576]{1,0:T(8,128)(2,1)S(1)}, bf16[32,576]{1,0:T(8,128)(2,1)S(1)}, u32[]{:S(2)}, u32[]{:S(2)}) collective-permute-start(bf16[32,576]{1,0:T(8,128)(2,1)S(1)} %get-tuple-element.179), channel_id=1, source_target_pairs={{0,4},{1,5},{2,6},{3,7},{4,0},{5,1},{6,2},{7,3},{8,12},{9,13},{10,... | collective-permute-start | bytes 110600 | tf_op jit(solution)/shard_map/ppermute | solution.py:31
  90.4 5.2 %collective-permute-start.36 = (bf16[32,576]{1,0:T(8,128)(2,1)S(1)}, bf16[32,576]{1,0:T(8,128)(2,1)S(1)}, u32[]{:S(2)}, u32[]{:S(2)}) collective-permute-start(bf16[32,576]{1,0:T(8,128)(2,1)S(1)} %get-tuple-element.180), channel_id=1, source_target_pairs={{0,68},{1,69},{2,70},{3,71},{4,64},{5,65},{6,66},{7,67},{8,76},{9,... | collective-permute-start | bytes 110600 | tf_op jit(solution)/shard_map/ppermute | solution.py:31
  (6 other events, 26.9 us)

commit v6 on v5

--- a/solution.py
+++ b/solution.py
@@ -367,11 +367,11 @@
 
 
 def head_gradient_low(low_ref, high_ref, dlog_ref, out_ref, *scratch):
-    head_rows(0, 5, low_ref, high_ref, dlog_ref, out_ref, *scratch)
+    head_rows(0, 4, low_ref, high_ref, dlog_ref, out_ref, *scratch)
 
 
 def head_gradient_mid(low_ref, high_ref, dlog_ref, started_ref, out_ref, *scratch):
-    head_rows(5, 7, low_ref, high_ref, dlog_ref, out_ref, *scratch)
+    head_rows(4, 7, low_ref, high_ref, dlog_ref, out_ref, *scratch)
 
 
 def head_gradient_high(low_ref, high_ref, dlog_ref, started_ref, out_ref, *scratch):

time: 97.7 us -> 98.4 us (level)
  transfers between devices with their start and end apart: 37 -> 37, of which waited for: 17 -> 18; matrix products, arithmetic and copies ran while one was open for 1% -> 1% of each run, Pallas kernels for 33% -> 33%
where the time goes in v6:
time: 98.4 us; the launch traced here: 96.9 us
  starting transfers between devices  40.5 us (41%)
  Pallas kernels  33.5 us (34%)
  waiting for transfers between devices  21.3 us (22%)
    ppermute x37, starting transfers between devices, send(): return lax.ppermute(array, AXES, partner)  40.5 us
    ppermute x37, waiting for transfers between devices, send(): return lax.ppermute(array, AXES, partner)  21.3 us
    pallas_call x3, Pallas kernels, run_head_gradient(): call(kernel, 'vvv' + 'h' * len(started), [('h', (D, WIDTH), bf16)], scrat...  9.92 us
    pallas_call x1, Pallas kernels, run_begin(): call(begin, 'shhh', [BLOCKS] * 4 + [('v', (D, WIDTH), bf16), column, colu...  8.24 us
    pallas_call x2, Pallas kernels, run_forward(): call(kernel, 's' + 'v' * 10, [('v', (256, D), bf16), ('v', (256, WIDTH),...  5.96 us
    pallas_call x2, Pallas kernels, run_back(): return call(back, 'svv', [BLOCKS, BLOCKS], **BACK_COST)(me, rows, head)  5.87 us
  transfers between devices with their start and end apart: 37, of which 18 were waited for; matrix products, arithmetic and copies ran while one was open for 1% of the time, Pallas kernels for 33%

profile of v6, /device:TPU:0, one launch (start us, length us, event | category | flops | bytes accessed | tf_op | source)
XLA Modules:
  0.0 96.9 jit_solution(3403888416594048699)
XLA Ops:
  0.6 1.7 %collective-permute-start.3 = (bf16[32,4608]{1,0:T(8,128)(2,1)}, bf16[32,4608]{1,0:T(8,128)(2,1)S(1)}, u32[]{:S(2)}, u32[]{:S(2)}) collective-permute-start(bf16[32,4608]{1,0:T(8,128)(2,1)} %refs_1_.1), channel_id=1, source_target_pairs={{0,16},{1,17},{2,18},{3,19},{4,20},{5,21},{6,22},{7,23},{8,56},{9,... | collective-permute-start | bytes 884744 | tf_op jit(solution)/shard_map/ppermute | solution.py:31
  2.3 2.1 %collective-permute-start.2 = (bf16[32,4608]{1,0:T(8,128)(2,1)}, bf16[32,4608]{1,0:T(8,128)(2,1)S(1)}, u32[]{:S(2)}, u32[]{:S(2)}) collective-permute-start(bf16[32,4608]{1,0:T(8,128)(2,1)} %refs_1_.1), channel_id=1, source_target_pairs={{0,48},{1,49},{2,50},{3,51},{4,52},{5,53},{6,54},{7,55},{8,24},{9,... | collective-permute-start | bytes 884744 | tf_op jit(solution)/shard_map/ppermute | solution.py:31
  5.0 4.0 %collective-permute-start = (bf16[32,4608]{1,0:T(8,128)(2,1)}, bf16[32,4608]{1,0:T(8,128)(2,1)S(1)}, u32[]{:S(2)}, u32[]{:S(2)}) collective-permute-start(bf16[32,4608]{1,0:T(8,128)(2,1)} %refs_1_.1), channel_id=1, source_target_pairs={{0,68},{1,69},{2,70},{3,71},{4,64},{5,65},{6,66},{7,67},{8,76},{9,... | collective-permute-start | bytes 884744 | tf_op jit(solution)/shard_map/ppermute | solution.py:31
  9.1 8.2 %begin.1 = (bf16[4,4,32,1152]{3,2,1,0:T(8,128)(2,1)S(1)}, bf16[4,4,32,1152]{3,2,1,0:T(8,128)(2,1)S(1)}, bf16[4,4,32,1152]{3,2,1,0:T(8,128)(2,1)S(1)}, bf16[4,4,3...) custom-call(s32[1]{0:T(128)} %bitcast.me_ref.refs_0_, ...), custom_call_target="tpu_custom_call" | custom-call | flops 4831838208 | bytes 9437184 | tf_op jit(solution)/shard_map/begin/pallas_call | solution.py:231
  19.8 3.5 %collective-permute-start.9 = (bf16[32,4608]{1,0:T(8,128)(2,1)S(1)}, bf16[32,4608]{1,0:T(8,128)(2,1)S(1)}, u32[]{:S(2)}, u32[]{:S(2)}) collective-permute-start(bf16[32,4608]{1,0:T(8,128)(2,1)S(1)} %collective-permute-done.1.refs_4_), channel_id=1, source_target_pairs={{0,68},{1,69},{2,70},{3,71},{4,64},{5,65},{6,66},{7,67},{8,76},{9,... | collective-permute-start | bytes 884744 | tf_op jit(solution)/shard_map/ppermute | solution.py:31
  23.3 1.2 %collective-permute-start.11 = (bf16[32,4608]{1,0:T(8,128)(2,1)S(1)}, bf16[32,4608]{1,0:T(8,128)(2,1)S(1)}, u32[]{:S(2)}, u32[]{:S(2)}) collective-permute-start(bf16[32,4608]{1,0:T(8,128)(2,1)S(1)} %collective-permute-done.refs_1_), channel_id=1, source_target_pairs={{0,8},{1,9},{2,10},{3,11},{4,12},{5,13},{6,14},{7,15},{8,0},{9,1},... | collective-permute-start | bytes 884744 | tf_op jit(solution)/shard_map/ppermute | solution.py:31
  24.6 1.7 %collective-permute-start.10 = (bf16[32,4608]{1,0:T(8,128)(2,1)S(1)}, bf16[32,4608]{1,0:T(8,128)(2,1)S(1)}, u32[]{:S(2)}, u32[]{:S(2)}) collective-permute-start(bf16[32,4608]{1,0:T(8,128)(2,1)S(1)} %collective-permute-done.refs_1_), channel_id=1, source_target_pairs={{0,48},{1,49},{2,50},{3,51},{4,52},{5,53},{6,54},{7,55},{8,24},{9,... | collective-permute-start | bytes 884744 | tf_op jit(solution)/shard_map/ppermute | solution.py:31
  26.2 3.0 %forward_low.1 = (bf16[256,4608]{1,0:T(8,128)(2,1)S(1)}, f32[256,1024]{1,0:T(8,128)S(1)}, bf16[256,1024]{1,0:T(8,128)(2,1)S(1)}, f32[256,128]{1,0:T(8,128)S(1)}, f32[256,128]{1,0:T(8,128)S(1)}) custom-call(s32[1]{0:T(128)} %bitcast.me_ref.refs_0_, bf16[32,4608]{1,0:T(8,128)(2,1)S(1)} %copy-done, bf16[32,4608]{1,0:T(8,128)(2,1)S(1)} %collective-permute-done.3.refs_2_, ...), custom_call_target="tpu_custom_call" | custom-call | flops 2415919104 | bytes 9437184 | tf_op jit(solution)/shard_map/forward_low/pallas_call | solution.py:116
  29.2 2.9 %back.2 = (bf16[4,4,32,1152]{3,2,1,0:T(8,128)(2,1)S(1)}, bf16[4,4,32,1152]{3,2,1,0:T(8,128)(2,1)S(1)}) custom-call(s32[1]{0:T(128)} %bitcast.me_ref.refs_0_, bf16[256,1024]{1,0:T(8,128)(2,1)S(1)} %get-tuple-element.106.rows_ref, bf16[4608,1024]{1,0:T(8,128)(2,1)S(1)} %get-tuple-element.104.refs_10_.head_ref), custom_call_target="tpu_custom_call" | custom-call | flops 2415919104 | bytes 9437184 | tf_op jit(solution)/shard_map/back/pallas_call | solution.py:196
  33.0 1.1 %collective-permute-done.12.refs_6_ = bf16[32,4608]{1,0:T(8,128)(2,1)S(1)} collective-permute-done((bf16[32,4608]{1,0:T(8,128)(2,1)S(1)}, bf16[32,4608]{1,0:T(8,128)(2,1)S(1)}, u32[]{:S(2)}, u32[]{:S(2)}) %collective-permute-start.12) | collective-permute-done | bytes 294944 | tf_op jit(solution)/shard_map/ppermute | solution.py:31
  35.1 3.0 %forward_high.1 = (bf16[256,4608]{1,0:T(8,128)(2,1)S(1)}, f32[256,1024]{1,0:T(8,128)S(1)}, bf16[256,1024]{1,0:T(8,128)(2,1)S(1)}, f32[256,128]{1,0:T(8,128)S(1)}, f32[256,128]{1,0:T(8,128)S(1)}) custom-call(s32[1]{0:T(128)} %bitcast.me_ref.refs_0_, bf16[32,4608]{1,0:T(8,128)(2,1)S(1)} %collective-permute-done.refs_1_, ...), custom_call_target="tpu_custom_call" | custom-call | flops 2415919104 | bytes 9437184 | tf_op jit(solution)/shard_map/forward_high/pallas_call | solution.py:116
  39.0 2.9 %back.3 = (bf16[4,4,32,1152]{3,2,1,0:T(8,128)(2,1)S(1)}, bf16[4,4,32,1152]{3,2,1,0:T(8,128)(2,1)S(1)}) custom-call(s32[1]{0:T(128)} %bitcast.me_ref.refs_0_, bf16[256,1024]{1,0:T(8,128)(2,1)S(1)} %get-tuple-element.128.rows_ref, bf16[4608,1024]{1,0:T(8,128)(2,1)S(1)} %get-tuple-element.104.refs_10_.head_ref), custom_call_target="tpu_custom_call" | custom-call | flops 2415919104 | bytes 9437184 | tf_op jit(solution)/shard_map/back/pallas_call | solution.py:196
  42.7 1.3 %collective-permute-start.19 = (bf16[4,4,32,1152]{3,2,1,0:T(8,128)(2,1)S(1)}, bf16[4,4,32,1152]{3,2,1,0:T(8,128)(2,1)S(1)}, u32[]{:S(2)}, u32[]{:S(2)}) collective-permute-start(bf16[4,4,32,1152]{3,2,1,0:T(8,128)(2,1)S(1)} %get-tuple-element.134), channel_id=1, source_target_pairs={{0,8},{1,9},{2,10},{3,11},{4,12},{5,13},{6,14},{7,15},{8,0},{9,1},... | collective-permute-start | bytes 3538952 | tf_op jit(solution)/shard_map/ppermute | solution.py:31
  44.0 1.6 %collective-permute-start.20 = (f32[8,128]{1,0:T(8,128)S(1)}, f32[8,128]{1,0:T(8,128)S(1)}, u32[]{:S(2)}, u32[]{:S(2)}) collective-permute-start(f32[8,128]{1,0:T(8,128)S(1)} %add.28), channel_id=1, source_target_pairs={{0,48},{1,49},{2,50},{3,51},{4,52},{5,53},{6,54},{7,55},{8,24},{9,... | collective-permute-start | bytes 12296 | tf_op jit(solution)/shard_map/ppermute | solution.py:31
  45.6 3.2 %collective-permute-done.20 = f32[8,128]{1,0:T(8,128)S(1)} collective-permute-done((f32[8,128]{1,0:T(8,128)S(1)}, f32[8,128]{1,0:T(8,128)S(1)}, u32[]{:S(2)}, u32[]{:S(2)}) %collective-permute-start.20) | collective-permute-done | bytes 4128 | tf_op jit(solution)/shard_map/ppermute | solution.py:31
  50.0 3.0 %collective-permute-start.27 = (bf16[2,2,2,2,32,1152]{5,4,3,2,1,0:T(8,128)(2,1)S(1)}, bf16[2,2,2,2,32,1152]{5,4,3,2,1,0:T(8,128)(2,1)S(1)}, u32[]{:S(2)}, u32[]{:S(2)}) collective-permute-start(bf16[2,2,2,2,32,1152]{5,4,3,2,1,0:T(8,128)(2,1)S(1)} %get-tuple-element.146), channel_id=1, source_target_pairs={{0,3},{1,2},{2,1},{3,0},{4,7},{5,6},{6,5},{7,4},{8,9},{9,8},{10,11... | collective-permute-start | bytes 3538952 | tf_op jit(solution)/shard_map/ppermute | solution.py:31
  53.0 1.6 %collective-permute-start.28 = (bf16[2,2,2,2,32,1152]{5,4,3,2,1,0:T(8,128)(2,1)S(1)}, bf16[2,2,2,2,32,1152]{5,4,3,2,1,0:T(8,128)(2,1)S(1)}, u32[]{:S(2)}, u32[]{:S(2)}) collective-permute-start(bf16[2,2,2,2,32,1152]{5,4,3,2,1,0:T(8,128)(2,1)S(1)} %get-tuple-element.147), channel_id=1, source_target_pairs={{0,48},{1,49},{2,50},{3,51},{4,52},{5,53},{6,54},{7,55},{8,24},{9,... | collective-permute-start | bytes 3538952 | tf_op jit(solution)/shard_map/ppermute | solution.py:31
  54.6 3.6 %collective-permute-done.22 = f32[8,128]{1,0:T(8,128)S(1)} collective-permute-done((f32[8,128]{1,0:T(8,128)S(1)}, f32[8,128]{1,0:T(8,128)S(1)}, u32[]{:S(2)}, u32[]{:S(2)}) %collective-permute-start.22) | collective-permute-done | bytes 4128 | tf_op jit(solution)/shard_map/ppermute | solution.py:31
  58.2 2.2 %collective-permute-start.23 = (f32[8,128]{1,0:T(8,128)S(1)}, f32[8,128]{1,0:T(8,128)S(1)}, u32[]{:S(2)}, u32[]{:S(2)}) collective-permute-start(f32[8,128]{1,0:T(8,128)S(1)} %add.31), channel_id=1, source_target_pairs={{0,68},{1,69},{2,70},{3,71},{4,64},{5,65},{6,66},{7,67},{8,76},{9,... | collective-permute-start | bytes 12296 | tf_op jit(solution)/shard_map/ppermute | solution.py:31
  60.4 2.6 %collective-permute-done.23 = f32[8,128]{1,0:T(8,128)S(1)} collective-permute-done((f32[8,128]{1,0:T(8,128)S(1)}, f32[8,128]{1,0:T(8,128)S(1)}, u32[]{:S(2)}, u32[]{:S(2)}) %collective-permute-start.23) | collective-permute-done | bytes 4128 | tf_op jit(solution)/shard_map/ppermute | solution.py:31
  63.7 2.2 %collective-permute-start.25 = (f32[8,128]{1,0:T(8,128)S(1)}, f32[8,128]{1,0:T(8,128)S(1)}, u32[]{:S(2)}, u32[]{:S(2)}) collective-permute-start(f32[8,128]{1,0:T(8,128)S(1)} %add.32), channel_id=1, source_target_pairs={{0,3},{1,2},{2,1},{3,0},{4,7},{5,6},{6,5},{7,4},{8,9},{9,8},{10,11... | collective-permute-start | bytes 12296 | tf_op jit(solution)/shard_map/ppermute | solution.py:31
  66.5 1.6 %collective-permute-done.26 = f32[8,128]{1,0:T(8,128)S(1)} collective-permute-done((f32[8,128]{1,0:T(8,128)S(1)}, f32[8,128]{1,0:T(8,128)S(1)}, u32[]{:S(2)}, u32[]{:S(2)}) %collective-permute-start.26) | collective-permute-done | bytes 4128 | tf_op jit(solution)/shard_map/ppermute | solution.py:31
  71.7 1.7 %collective-permute-start.29 = (bf16[2,2,2,16,1152]{4,3,2,1,0:T(8,128)(2,1)S(1)}, bf16[2,2,2,16,1152]{4,3,2,1,0:T(8,128)(2,1)S(1)}, u32[]{:S(2)}, u32[]{:S(2)}) collective-permute-start(bf16[2,2,2,16,1152]{4,3,2,1,0:T(8,128)(2,1)S(1)} %get-tuple-element.158), channel_id=1, source_target_pairs={{0,48},{1,49},{2,50},{3,51},{4,52},{5,53},{6,54},{7,55},{8,24},{9,... | collective-permute-start | bytes 884744 | tf_op jit(solution)/shard_map/ppermute | solution.py:31
  74.8 4.2 %head_gradient_low.1.started_ref = bf16[4608,1024]{1,0:T(8,128)(2,1)} custom-call(bf16[256,4608]{1,0:T(8,128)(2,1)S(1)} %get-tuple-element.162.low_ref, bf16[256,4608]{1,0:T(8,128)(2,1)S(1)} %get-tuple-element.163.high_ref, bf16[512,1024]{1,0:T(8,128)(2,1)S(1)} %dlogits.1.dlog_ref), custom_call_target="tpu_custom_call" | custom-call | flops 2415919104 | bytes 4718592 | tf_op jit(solution)/shard_map/head_gradient_low/pallas_call | solution.py:382
  79.4 1.2 %collective-permute-done.29.p_got = bf16[2,2,2,16,1152]{4,3,2,1,0:T(8,128)(2,1)S(1)} collective-permute-done((bf16[2,2,2,16,1152]{4,3,2,1,0:T(8,128)(2,1)S(1)}, bf16[2,2,2,16,1152]{4,3,2,1,0:T(8,128)(2,1)S(1)}, u32[]{:S(2)}, u32[]{:S(2)}) %collective-permute-start.29) | collective-permute-done | bytes 294944 | tf_op jit(solution)/shard_map/ppermute | solution.py:31
  80.9 3.4 %collective-permute-start.33 = (bf16[2,32,1152]{2,1,0:T(8,128)(2,1)S(1)}, bf16[2,32,1152]{2,1,0:T(8,128)(2,1)S(1)}, u32[]{:S(2)}, u32[]{:S(2)}) collective-permute-start(bf16[2,32,1152]{2,1,0:T(8,128)(2,1)S(1)} %get-tuple-element.173), channel_id=1, source_target_pairs={{0,17},{1,16},{2,19},{3,18},{4,21},{5,20},{6,23},{7,22},{8,59},{9,... | collective-permute-start | bytes 442376 | tf_op jit(solution)/shard_map/ppermute | solution.py:31
  84.2 3.4 %head_gradient_mid.1.started_ref = bf16[4608,1024]{1,0:T(8,128)(2,1)} custom-call(bf16[256,4608]{1,0:T(8,128)(2,1)S(1)} %get-tuple-element.162.low_ref, bf16[256,4608]{1,0:T(8,128)(2,1)S(1)} %get-tuple-element.163.high_ref, bf16[512,1024]{1,0:T(8,128)(2,1)S(1)} %dlogits.1.dlog_ref, ...), custom_call_target="tpu_custom_call", output_to_operand_aliasing={{}: (3, {})} | custom-call | flops 2415919104 | bytes 4718592 | tf_op jit(solution)/shard_map/head_gradient_mid/pallas_call | solution.py:382
  87.9 2.0 %collective-permute-start.34 = (bf16[32,576]{1,0:T(8,128)(2,1)S(1)}, bf16[32,576]{1,0:T(8,128)(2,1)S(1)}, u32[]{:S(2)}, u32[]{:S(2)}) collective-permute-start(bf16[32,576]{1,0:T(8,128)(2,1)S(1)} %get-tuple-element.178), channel_id=1, source_target_pairs={{0,64},{1,65},{2,66},{3,67},{4,68},{5,69},{6,70},{7,71},{8,72},{9,... | collective-permute-start | bytes 110600 | tf_op jit(solution)/shard_map/ppermute | solution.py:31
  89.9 1.1 %collective-permute-start.35 = (bf16[32,576]{1,0:T(8,128)(2,1)S(1)}, bf16[32,576]{1,0:T(8,128)(2,1)S(1)}, u32[]{:S(2)}, u32[]{:S(2)}) collective-permute-start(bf16[32,576]{1,0:T(8,128)(2,1)S(1)} %get-tuple-element.179), channel_id=1, source_target_pairs={{0,4},{1,5},{2,6},{3,7},{4,0},{5,1},{6,2},{7,3},{8,12},{9,13},{10,... | collective-permute-start | bytes 110600 | tf_op jit(solution)/shard_map/ppermute | solution.py:31
  91.1 1.0 %collective-permute-start.36 = (bf16[32,576]{1,0:T(8,128)(2,1)S(1)}, bf16[32,576]{1,0:T(8,128)(2,1)S(1)}, u32[]{:S(2)}, u32[]{:S(2)}) collective-permute-start(bf16[32,576]{1,0:T(8,128)(2,1)S(1)} %get-tuple-element.180), channel_id=1, source_target_pairs={{0,68},{1,69},{2,70},{3,71},{4,64},{5,65},{6,66},{7,67},{8,76},{9,... | collective-permute-start | bytes 110600 | tf_op jit(solution)/shard_map/ppermute | solution.py:31
  92.1 2.3 %head_gradient_high.1 = bf16[4608,1024]{1,0:T(8,128)(2,1)} custom-call(bf16[256,4608]{1,0:T(8,128)(2,1)S(1)} %get-tuple-element.162.low_ref, bf16[256,4608]{1,0:T(8,128)(2,1)S(1)} %get-tuple-element.163.high_ref, bf16[512,1024]{1,0:T(8,128)(2,1)S(1)} %dlogits.1.dlog_ref, bf16[4608,1024]{1,0:T(8,128)(2,1)} %head_gradient_mid.1.started_ref), custom_call_target="tpu_custom_call", output_to_operand_aliasing={{}: (3, {})} | custom-call | flops 2415919104 | bytes 4718592 | tf_op jit(solution)/shard_map/head_gradient_high/pallas_call | solution.py:382
  94.4 1.9 %collective-permute-done.36.refs_3_ = bf16[32,576]{1,0:T(8,128)(2,1)S(1)} collective-permute-done((bf16[32,576]{1,0:T(8,128)(2,1)S(1)}, bf16[32,576]{1,0:T(8,128)(2,1)S(1)}, u32[]{:S(2)}, u32[]{:S(2)}) %collective-permute-start.36) | collective-permute-done | bytes 36896 | tf_op jit(solution)/shard_map/ppermute | solution.py:31
  (68 shorter events, 15.5 us)
Async XLA Ops:
  0.6 16.7 %collective-permute-start.3 = (bf16[32,4608]{1,0:T(8,128)(2,1)}, bf16[32,4608]{1,0:T(8,128)(2,1)S(1)}, u32[]{:S(2)}, u32[]{:S(2)}) collective-permute-start(bf16[32,4608]{1,0:T(8,128)(2,1)} %refs_1_.1), channel_id=1, source_target_pairs={{0,16},{1,17},{2,18},{3,19},{4,20},{5,21},{6,22},{7,23},{8,56},{9,... | collective-permute-start | bytes 884744 | tf_op jit(solution)/shard_map/ppermute | solution.py:31
  2.3 15.0 %collective-permute-start.2 = (bf16[32,4608]{1,0:T(8,128)(2,1)}, bf16[32,4608]{1,0:T(8,128)(2,1)S(1)}, u32[]{:S(2)}, u32[]{:S(2)}) collective-permute-start(bf16[32,4608]{1,0:T(8,128)(2,1)} %refs_1_.1), channel_id=1, source_target_pairs={{0,48},{1,49},{2,50},{3,51},{4,52},{5,53},{6,54},{7,55},{8,24},{9,... | collective-permute-start | bytes 884744 | tf_op jit(solution)/shard_map/ppermute | solution.py:31
  4.4 14.0 %collective-permute-start.1 = (bf16[32,4608]{1,0:T(8,128)(2,1)}, bf16[32,4608]{1,0:T(8,128)(2,1)S(1)}, u32[]{:S(2)}, u32[]{:S(2)}) collective-permute-start(bf16[32,4608]{1,0:T(8,128)(2,1)} %refs_1_.1), channel_id=1, source_target_pairs={{0,32},{1,33},{2,34},{3,35},{4,36},{5,37},{6,38},{7,39},{8,40},{9,... | collective-permute-start | bytes 884744 | tf_op jit(solution)/shard_map/ppermute | solution.py:31
  5.0 13.3 %collective-permute-start = (bf16[32,4608]{1,0:T(8,128)(2,1)}, bf16[32,4608]{1,0:T(8,128)(2,1)S(1)}, u32[]{:S(2)}, u32[]{:S(2)}) collective-permute-start(bf16[32,4608]{1,0:T(8,128)(2,1)} %refs_1_.1), channel_id=1, source_target_pairs={{0,68},{1,69},{2,70},{3,71},{4,64},{5,65},{6,66},{7,67},{8,76},{9,... | collective-permute-start | bytes 884744 | tf_op jit(solution)/shard_map/ppermute | solution.py:31
  9.1 10.8 %collective-permute-start.5 = (bf16[32,4608]{1,0:T(8,128)(2,1)}, bf16[32,4608]{1,0:T(8,128)(2,1)S(1)}, u32[]{:S(2)}, u32[]{:S(2)}) collective-permute-start(bf16[32,4608]{1,0:T(8,128)(2,1)} %refs_1_.1), channel_id=1, source_target_pairs={{0,8},{1,9},{2,10},{3,11},{4,12},{5,13},{6,14},{7,15},{8,0},{9,1},... | collective-permute-start | bytes 884744 | tf_op jit(solution)/shard_map/ppermute | solution.py:31
  18.4 4.9 %collective-permute-start.6 = (bf16[32,4608]{1,0:T(8,128)(2,1)S(1)}, bf16[32,4608]{1,0:T(8,128)(2,1)S(1)}, u32[]{:S(2)}, u32[]{:S(2)}) collective-permute-start(bf16[32,4608]{1,0:T(8,128)(2,1)S(1)} %collective-permute-done.3.refs_2_), channel_id=1, source_target_pairs={{0,8},{1,9},{2,10},{3,11},{4,12},{5,13},{6,14},{7,15},{8,0},{9,1},... | collective-permute-start | bytes 884744 | tf_op jit(solution)/shard_map/ppermute | solution.py:31
  18.4 6.2 %collective-permute-start.7 = (bf16[32,4608]{1,0:T(8,128)(2,1)S(1)}, bf16[32,4608]{1,0:T(8,128)(2,1)S(1)}, u32[]{:S(2)}, u32[]{:S(2)}) collective-permute-start(bf16[32,4608]{1,0:T(8,128)(2,1)S(1)} %collective-permute-done.2.refs_3_), channel_id=1, source_target_pairs={{0,8},{1,9},{2,10},{3,11},{4,12},{5,13},{6,14},{7,15},{8,0},{9,1},... | collective-permute-start | bytes 884744 | tf_op jit(solution)/shard_map/ppermute | solution.py:31
  18.9 7.3 %collective-permute-start.8 = (bf16[32,4608]{1,0:T(8,128)(2,1)S(1)}, bf16[32,4608]{1,0:T(8,128)(2,1)S(1)}, u32[]{:S(2)}, u32[]{:S(2)}) collective-permute-start(bf16[32,4608]{1,0:T(8,128)(2,1)S(1)} %collective-permute-done.1.refs_4_), channel_id=1, source_target_pairs={{0,8},{1,9},{2,10},{3,11},{4,12},{5,13},{6,14},{7,15},{8,0},{9,1},... | collective-permute-start | bytes 884744 | tf_op jit(solution)/shard_map/ppermute | solution.py:31
  18.9 10.4 %collective-permute-start.4 = (bf16[32,4608]{1,0:T(8,128)(2,1)S(1)}, bf16[32,4608]{1,0:T(8,128)(2,1)S(1)}, u32[]{:S(2)}, u32[]{:S(2)}) collective-permute-start(bf16[32,4608]{1,0:T(8,128)(2,1)S(1)} %collective-permute-done.refs_1_), channel_id=1, source_target_pairs={{0,16},{1,17},{2,18},{3,19},{4,20},{5,21},{6,22},{7,23},{8,56},{9,... | collective-permute-start | bytes 884744 | tf_op jit(solution)/shard_map/ppermute | solution.py:31
  19.8 12.4 %collective-permute-start.9 = (bf16[32,4608]{1,0:T(8,128)(2,1)S(1)}, bf16[32,4608]{1,0:T(8,128)(2,1)S(1)}, u32[]{:S(2)}, u32[]{:S(2)}) collective-permute-start(bf16[32,4608]{1,0:T(8,128)(2,1)S(1)} %collective-permute-done.1.refs_4_), channel_id=1, source_target_pairs={{0,68},{1,69},{2,70},{3,71},{4,64},{5,65},{6,66},{7,67},{8,76},{9,... | collective-permute-start | bytes 884744 | tf_op jit(solution)/shard_map/ppermute | solution.py:31
  23.3 9.7 %collective-permute-start.11 = (bf16[32,4608]{1,0:T(8,128)(2,1)S(1)}, bf16[32,4608]{1,0:T(8,128)(2,1)S(1)}, u32[]{:S(2)}, u32[]{:S(2)}) collective-permute-start(bf16[32,4608]{1,0:T(8,128)(2,1)S(1)} %collective-permute-done.refs_1_), channel_id=1, source_target_pairs={{0,8},{1,9},{2,10},{3,11},{4,12},{5,13},{6,14},{7,15},{8,0},{9,1},... | collective-permute-start | bytes 884744 | tf_op jit(solution)/shard_map/ppermute | solution.py:31
  24.6 7.9 %collective-permute-start.10 = (bf16[32,4608]{1,0:T(8,128)(2,1)S(1)}, bf16[32,4608]{1,0:T(8,128)(2,1)S(1)}, u32[]{:S(2)}, u32[]{:S(2)}) collective-permute-start(bf16[32,4608]{1,0:T(8,128)(2,1)S(1)} %collective-permute-done.refs_1_), channel_id=1, source_target_pairs={{0,48},{1,49},{2,50},{3,51},{4,52},{5,53},{6,54},{7,55},{8,24},{9,... | collective-permute-start | bytes 884744 | tf_op jit(solution)/shard_map/ppermute | solution.py:31
  38.0 4.5 %collective-permute-start.17 = (bf16[4,4,32,1152]{3,2,1,0:T(8,128)(2,1)S(1)}, bf16[4,4,32,1152]{3,2,1,0:T(8,128)(2,1)S(1)}, u32[]{:S(2)}, u32[]{:S(2)}) collective-permute-start(bf16[4,4,32,1152]{3,2,1,0:T(8,128)(2,1)S(1)} %get-tuple-element.130), channel_id=1, source_target_pairs={{0,8},{1,9},{2,10},{3,11},{4,12},{5,13},{6,14},{7,15},{8,0},{9,1},... | collective-permute-start | bytes 3538952 | tf_op jit(solution)/shard_map/ppermute | solution.py:31
  38.5 4.2 %collective-permute-start.18 = (bf16[4,4,32,1152]{3,2,1,0:T(8,128)(2,1)S(1)}, bf16[4,4,32,1152]{3,2,1,0:T(8,128)(2,1)S(1)}, u32[]{:S(2)}, u32[]{:S(2)}) collective-permute-start(bf16[4,4,32,1152]{3,2,1,0:T(8,128)(2,1)S(1)} %get-tuple-element.131), channel_id=1, source_target_pairs={{0,8},{1,9},{2,10},{3,11},{4,12},{5,13},{6,14},{7,15},{8,0},{9,1},... | collective-permute-start | bytes 3538952 | tf_op jit(solution)/shard_map/ppermute | solution.py:31
  38.9 3.7 %collective-permute-start.16 = (f32[8,128]{1,0:T(8,128)S(1)}, f32[8,128]{1,0:T(8,128)S(1)}, u32[]{:S(2)}, u32[]{:S(2)}) collective-permute-start(f32[8,128]{1,0:T(8,128)S(1)} %pack.1), channel_id=1, source_target_pairs={{0,16},{1,17},{2,18},{3,19},{4,20},{5,21},{6,22},{7,23},{8,56},{9,... | collective-permute-start | bytes 12296 | tf_op jit(solution)/shard_map/ppermute | solution.py:31
  42.7 6.2 %collective-permute-start.19 = (bf16[4,4,32,1152]{3,2,1,0:T(8,128)(2,1)S(1)}, bf16[4,4,32,1152]{3,2,1,0:T(8,128)(2,1)S(1)}, u32[]{:S(2)}, u32[]{:S(2)}) collective-permute-start(bf16[4,4,32,1152]{3,2,1,0:T(8,128)(2,1)S(1)} %get-tuple-element.134), channel_id=1, source_target_pairs={{0,8},{1,9},{2,10},{3,11},{4,12},{5,13},{6,14},{7,15},{8,0},{9,1},... | collective-permute-start | bytes 3538952 | tf_op jit(solution)/shard_map/ppermute | solution.py:31
  44.0 4.8 %collective-permute-start.20 = (f32[8,128]{1,0:T(8,128)S(1)}, f32[8,128]{1,0:T(8,128)S(1)}, u32[]{:S(2)}, u32[]{:S(2)}) collective-permute-start(f32[8,128]{1,0:T(8,128)S(1)} %add.28), channel_id=1, source_target_pairs={{0,48},{1,49},{2,50},{3,51},{4,52},{5,53},{6,54},{7,55},{8,24},{9,... | collective-permute-start | bytes 12296 | tf_op jit(solution)/shard_map/ppermute | solution.py:31
  50.0 19.5 %collective-permute-start.27 = (bf16[2,2,2,2,32,1152]{5,4,3,2,1,0:T(8,128)(2,1)S(1)}, bf16[2,2,2,2,32,1152]{5,4,3,2,1,0:T(8,128)(2,1)S(1)}, u32[]{:S(2)}, u32[]{:S(2)}) collective-permute-start(bf16[2,2,2,2,32,1152]{5,4,3,2,1,0:T(8,128)(2,1)S(1)} %get-tuple-element.146), channel_id=1, source_target_pairs={{0,3},{1,2},{2,1},{3,0},{4,7},{5,6},{6,5},{7,4},{8,9},{9,8},{10,11... | collective-permute-start | bytes 3538952 | tf_op jit(solution)/shard_map/ppermute | solution.py:31
  53.0 17.4 %collective-permute-start.28 = (bf16[2,2,2,2,32,1152]{5,4,3,2,1,0:T(8,128)(2,1)S(1)}, bf16[2,2,2,2,32,1152]{5,4,3,2,1,0:T(8,128)(2,1)S(1)}, u32[]{:S(2)}, u32[]{:S(2)}) collective-permute-start(bf16[2,2,2,2,32,1152]{5,4,3,2,1,0:T(8,128)(2,1)S(1)} %get-tuple-element.147), channel_id=1, source_target_pairs={{0,48},{1,49},{2,50},{3,51},{4,52},{5,53},{6,54},{7,55},{8,24},{9,... | collective-permute-start | bytes 3538952 | tf_op jit(solution)/shard_map/ppermute | solution.py:31
  54.6 3.6 %collective-permute-start.22 = (f32[8,128]{1,0:T(8,128)S(1)}, f32[8,128]{1,0:T(8,128)S(1)}, u32[]{:S(2)}, u32[]{:S(2)}) collective-permute-start(f32[8,128]{1,0:T(8,128)S(1)} %add.30), channel_id=1, source_target_pairs={{0,4},{1,5},{2,6},{3,7},{4,0},{5,1},{6,2},{7,3},{8,12},{9,13},{10,... | collective-permute-start | bytes 12296 | tf_op jit(solution)/shard_map/ppermute | solution.py:31
  58.2 4.8 %collective-permute-start.23 = (f32[8,128]{1,0:T(8,128)S(1)}, f32[8,128]{1,0:T(8,128)S(1)}, u32[]{:S(2)}, u32[]{:S(2)}) collective-permute-start(f32[8,128]{1,0:T(8,128)S(1)} %add.31), channel_id=1, source_target_pairs={{0,68},{1,69},{2,70},{3,71},{4,64},{5,65},{6,66},{7,67},{8,76},{9,... | collective-permute-start | bytes 12296 | tf_op jit(solution)/shard_map/ppermute | solution.py:31
  63.0 5.1 %collective-permute-start.26 = (f32[8,128]{1,0:T(8,128)S(1)}, f32[8,128]{1,0:T(8,128)S(1)}, u32[]{:S(2)}, u32[]{:S(2)}) collective-permute-start(f32[8,128]{1,0:T(8,128)S(1)} %add.32), channel_id=1, source_target_pairs={{0,2},{1,3},{2,0},{3,1},{4,6},{5,7},{6,4},{7,5},{8,10},{9,11},{10,... | collective-permute-start | bytes 12296 | tf_op jit(solution)/shard_map/ppermute | solution.py:31
  63.7 4.8 %collective-permute-start.25 = (f32[8,128]{1,0:T(8,128)S(1)}, f32[8,128]{1,0:T(8,128)S(1)}, u32[]{:S(2)}, u32[]{:S(2)}) collective-permute-start(f32[8,128]{1,0:T(8,128)S(1)} %add.32), channel_id=1, source_target_pairs={{0,3},{1,2},{2,1},{3,0},{4,7},{5,6},{6,5},{7,4},{8,9},{9,8},{10,11... | collective-permute-start | bytes 12296 | tf_op jit(solution)/shard_map/ppermute | solution.py:31
  65.8 3.6 %collective-permute-start.24 = (f32[8,128]{1,0:T(8,128)S(1)}, f32[8,128]{1,0:T(8,128)S(1)}, u32[]{:S(2)}, u32[]{:S(2)}) collective-permute-start(f32[8,128]{1,0:T(8,128)S(1)} %add.32), channel_id=1, source_target_pairs={{0,1},{1,0},{2,3},{3,2},{4,5},{5,4},{6,7},{7,6},{8,11},{9,10},{10,... | collective-permute-start | bytes 12296 | tf_op jit(solution)/shard_map/ppermute | solution.py:31
  71.3 8.0 %collective-permute-start.30 = (bf16[2,2,2,16,1152]{4,3,2,1,0:T(8,128)(2,1)S(1)}, bf16[2,2,2,16,1152]{4,3,2,1,0:T(8,128)(2,1)S(1)}, u32[]{:S(2)}, u32[]{:S(2)}) collective-permute-start(bf16[2,2,2,16,1152]{4,3,2,1,0:T(8,128)(2,1)S(1)} %get-tuple-element.161), channel_id=1, source_target_pairs={{0,3},{1,2},{2,1},{3,0},{4,7},{5,6},{6,5},{7,4},{8,9},{9,8},{10,11... | collective-permute-start | bytes 884744 | tf_op jit(solution)/shard_map/ppermute | solution.py:31
  71.7 8.9 %collective-permute-start.29 = (bf16[2,2,2,16,1152]{4,3,2,1,0:T(8,128)(2,1)S(1)}, bf16[2,2,2,16,1152]{4,3,2,1,0:T(8,128)(2,1)S(1)}, u32[]{:S(2)}, u32[]{:S(2)}) collective-permute-start(bf16[2,2,2,16,1152]{4,3,2,1,0:T(8,128)(2,1)S(1)} %get-tuple-element.158), channel_id=1, source_target_pairs={{0,48},{1,49},{2,50},{3,51},{4,52},{5,53},{6,54},{7,55},{8,24},{9,... | collective-permute-start | bytes 884744 | tf_op jit(solution)/shard_map/ppermute | solution.py:31
  80.7 7.0 %collective-permute-start.31 = (bf16[2,32,1152]{2,1,0:T(8,128)(2,1)S(1)}, bf16[2,32,1152]{2,1,0:T(8,128)(2,1)S(1)}, u32[]{:S(2)}, u32[]{:S(2)}) collective-permute-start(bf16[2,32,1152]{2,1,0:T(8,128)(2,1)S(1)} %get-tuple-element.171), channel_id=1, source_target_pairs={{0,16},{1,17},{2,18},{3,19},{4,20},{5,21},{6,22},{7,23},{8,56},{9,... | collective-permute-start | bytes 442376 | tf_op jit(solution)/shard_map/ppermute | solution.py:31
  80.8 6.9 %collective-permute-start.32 = (bf16[2,32,1152]{2,1,0:T(8,128)(2,1)S(1)}, bf16[2,32,1152]{2,1,0:T(8,128)(2,1)S(1)}, u32[]{:S(2)}, u32[]{:S(2)}) collective-permute-start(bf16[2,32,1152]{2,1,0:T(8,128)(2,1)S(1)} %get-tuple-element.172), channel_id=1, source_target_pairs={{0,1},{1,0},{2,3},{3,2},{4,5},{5,4},{6,7},{7,6},{8,11},{9,10},{10,... | collective-permute-start | bytes 442376 | tf_op jit(solution)/shard_map/ppermute | solution.py:31
  80.9 6.9 %collective-permute-start.33 = (bf16[2,32,1152]{2,1,0:T(8,128)(2,1)S(1)}, bf16[2,32,1152]{2,1,0:T(8,128)(2,1)S(1)}, u32[]{:S(2)}, u32[]{:S(2)}) collective-permute-start(bf16[2,32,1152]{2,1,0:T(8,128)(2,1)S(1)} %get-tuple-element.173), channel_id=1, source_target_pairs={{0,17},{1,16},{2,19},{3,18},{4,21},{5,20},{6,23},{7,22},{8,59},{9,... | collective-permute-start | bytes 442376 | tf_op jit(solution)/shard_map/ppermute | solution.py:31
  87.9 6.5 %collective-permute-start.34 = (bf16[32,576]{1,0:T(8,128)(2,1)S(1)}, bf16[32,576]{1,0:T(8,128)(2,1)S(1)}, u32[]{:S(2)}, u32[]{:S(2)}) collective-permute-start(bf16[32,576]{1,0:T(8,128)(2,1)S(1)} %get-tuple-element.178), channel_id=1, source_target_pairs={{0,64},{1,65},{2,66},{3,67},{4,68},{5,69},{6,70},{7,71},{8,72},{9,... | collective-permute-start | bytes 110600 | tf_op jit(solution)/shard_map/ppermute | solution.py:31
  89.9 4.5 %collective-permute-start.35 = (bf16[32,576]{1,0:T(8,128)(2,1)S(1)}, bf16[32,576]{1,0:T(8,128)(2,1)S(1)}, u32[]{:S(2)}, u32[]{:S(2)}) collective-permute-start(bf16[32,576]{1,0:T(8,128)(2,1)S(1)} %get-tuple-element.179), channel_id=1, source_target_pairs={{0,4},{1,5},{2,6},{3,7},{4,0},{5,1},{6,2},{7,3},{8,12},{9,13},{10,... | collective-permute-start | bytes 110600 | tf_op jit(solution)/shard_map/ppermute | solution.py:31
  91.1 5.2 %collective-permute-start.36 = (bf16[32,576]{1,0:T(8,128)(2,1)S(1)}, bf16[32,576]{1,0:T(8,128)(2,1)S(1)}, u32[]{:S(2)}, u32[]{:S(2)}) collective-permute-start(bf16[32,576]{1,0:T(8,128)(2,1)S(1)} %get-tuple-element.180), channel_id=1, source_target_pairs={{0,68},{1,69},{2,70},{3,71},{4,64},{5,65},{6,66},{7,67},{8,76},{9,... | collective-permute-start | bytes 110600 | tf_op jit(solution)/shard_map/ppermute | solution.py:31
  (6 other events, 26.9 us)
